TPU v7x, 512 devices: a whole 4x8x8 slice. The times are simulated.
512 devices in a mesh: dp: 32 (over z, y_lo), fsdp: 16 (over y_hi, x, core).
Axes of the slice: x: 4, y: 8 (y_hi: 2, y_lo: 4; y = y_hi * 4 + y_lo), z: 8, core: 2. Of those that a mesh axis runs over, the one named last changes fastest.
Arguments:
- images: bfloat16 [65536, 1152], P(('dp', 'fsdp')), may hold values from -0.017944336 to 0.017944336
- pooled: bfloat16 [65536, 1152], P(('dp', 'fsdp')), may hold values from -0.0625 to 0.0625
- head_weight: bfloat16 [1152, 1152], P('fsdp'), may hold values from -0.1875 to 0.1875
- head_bias: float32 [1152], replicated, may hold values from -0.018 to 0.018
- log_scale: float32 [1], replicated, may hold values from 4.3 to 4.7
- bias: float32 [1], replicated, may hold values from -3 to -1
Outputs:
- row_loss: float32 [65536], P(('dp', 'fsdp'))
- image_grad: bfloat16 [65536, 1152], P(('dp', 'fsdp'))
- pooled_grad: bfloat16 [65536, 1152], P(('dp', 'fsdp'))
- head_grad: float32 [36864, 1152], P(('dp', 'fsdp'))
All inputs are finite; a program needn't handle non-finite values.
Results may differ from a plain program's by a relative error of at most 0.025.
Values may be sent and summed in bfloat16 or wider, within the bound.
A program may use at most 64 MiB of HBM per device.

v0:
```python
import jax
import jax.numpy as jnp
from jax import lax
from jax.sharding import PartitionSpec as P

STEPS = 4


def shifted(value, axis, steps):
    count = lax.axis_size(axis)
    pairs = [(source, (source + steps) % count) for source in range(count)]
    return lax.ppermute(value, axis, pairs)


def normalize(v):
    total = jnp.sum(v * v, axis=-1, keepdims=True)
    scale_r = lax.rsqrt(total + 1e-06)
    return (v * scale_r, scale_r)


def per_device(images, pooled, head_weight, head_bias, log_scale, bias):
    rows = images.shape[0]
    width = images.shape[1]
    temper = jnp.exp(log_scale[0])
    offset = bias[0]
    image_features, xr = normalize(images.astype(jnp.float32))
    normalized_image = image_features.astype(jnp.bfloat16)
    u_pre = jnp.dot(
        pooled,
        lax.all_gather(head_weight, "fsdp", axis=0, tiled=True),
        preferred_element_type=jnp.float32,
    )
    u_pre = u_pre + head_bias
    ztxt, zr = normalize(u_pre)
    zhat = ztxt.astype(jnp.bfloat16)
    eye_mask = jnp.eye(rows, dtype=bool)
    contract_over_rows = (((1,), (1,)), ((), ()))
    contract_leading_axis = (((0,), (0,)), ((), ()))
    current_text_block = zhat
    loss_sum = jnp.zeros((rows,), jnp.float32)
    dx_sum = jnp.zeros((rows, width), jnp.float32)
    carried = jnp.zeros((rows, width), jnp.float32)
    for step in range(STEPS):
        if step > 0:
            current_text_block = shifted(current_text_block, "dp", 1)
        logits = (
            temper
            * lax.dot_general(
                normalized_image,
                current_text_block,
                contract_over_rows,
                preferred_element_type=jnp.float32,
            )
            + offset
        )
        if step == 0:
            label = jnp.where(eye_mask, 1.0, -1.0).astype(jnp.float32)
        else:
            label = -jnp.ones((rows, rows), jnp.float32)
        loss_sum = loss_sum + jnp.sum(jax.nn.softplus(-label * logits), axis=-1) / rows
        bias_gradient = (-label * jax.nn.sigmoid(-label * logits) * temper / rows).astype(
            jnp.bfloat16
        )
        dx_sum = dx_sum + jnp.dot(
            bias_gradient, current_text_block, preferred_element_type=jnp.float32
        )
        text_gradient_step = lax.dot_general(
            bias_gradient,
            normalized_image,
            contract_leading_axis,
            preferred_element_type=jnp.float32,
        )
        if step == 0:
            carried = text_gradient_step
        else:
            carried = (
                shifted(carried.astype(jnp.bfloat16), "dp", 1).astype(carried.dtype)
                + text_gradient_step
            )
    home_sum = shifted(carried.astype(jnp.bfloat16), "dp", -(STEPS - 1)).astype(carried.dtype)
    image_grad = (
        xr * (dx_sum - image_features * jnp.sum(image_features * dx_sum, axis=-1, keepdims=True))
    ).astype(jnp.bfloat16)
    dzb = (zr * (home_sum - ztxt * jnp.sum(ztxt * home_sum, axis=-1, keepdims=True))).astype(
        jnp.bfloat16
    )
    pooled_grad = lax.dot_general(
        dzb,
        lax.all_gather(head_weight, "fsdp", axis=0, tiled=True),
        contract_over_rows,
        preferred_element_type=jnp.float32,
    )
    pooled_grad = pooled_grad.astype(jnp.bfloat16)
    head_term = lax.dot_general(
        pooled, dzb, contract_leading_axis, preferred_element_type=jnp.float32
    )
    head_grad = lax.psum_scatter(
        head_term.astype(jnp.bfloat16), "fsdp", scatter_dimension=0, tiled=True
    ).astype(jnp.float32)
    return (loss_sum, image_grad, pooled_grad, head_grad)


def solution(mesh):
    in_specs = (P(("dp", "fsdp"), None), P(("dp", "fsdp"), None), P("fsdp", None), P(), P(), P())
    out_specs = (
        P(("dp", "fsdp")),
        P(("dp", "fsdp"), None),
        P(("dp", "fsdp"), None),
        P(("dp", "fsdp"), None),
    )
    return jax.shard_map(
        per_device, mesh=mesh, in_specs=in_specs, out_specs=out_specs, check_vma=False
    )
```

profile of v0, /device:TPU:56, one launch (start us, length us, event | category | flops | bytes accessed | tf_op | source)
XLA Modules:
  0.0 346.8 jit_solution(10388322568068421442)
XLA Ops:
  7.2 0.0 copy-start
  7.2 0.0 copy-start.2
  7.2 0.0 all-gather.2.cloned.1.call-start
  7.2 0.7 all-gather.2.cloned.1.call-update
  7.9 0.0 all-reduce.3.cloned.1.call-start
  9.3 1.1 fusion.13
  10.4 71.9 %all-gather.2.cloned.1.call-done = bf16[1152,1152]{1,0:T(8,128)(2,1)} async-done(((bf16[72,1152]{1,0:T(8,128)(2,1)}), bf16[1152,1152]{1,0:T(8,128)(2,1)}) %all-gather.2.cloned.1.call-update) | async-done | bytes 2654224 | tf_op jit(solution)/shard_map/all_gather | solution.py:30
  82.3 0.0 copy-done
  82.3 2.4 multiply_reduce_fusion
  84.8 0.1 multiply_convert_fusion
  84.9 3.2 collective-permute-start
  88.1 0.0 copy-done.2
  88.1 0.4 fusion.17
  88.5 0.3 convolution_convert_fusion.2
  88.8 6.6 %collective-permute-start.3 = (bf16[128,1152]{1,0:T(8,128)(2,1)S(1)}, bf16[128,1152]{1,0:T(8,128)(2,1)S(1)}, u32[]{:S(2)}, u32[]{:S(2)}) collective-permute-start(bf16[128,1152]{1,0:T(8,128)(2,1)S(1)} %convolution_convert_fusion.2), channel_id=1, source_target_pairs={{0,16},{16,32},{32,48},{48,64},{64,80},{80,96},{96,112},{112,128},... | collective-permute-start | bytes 884744 | tf_op jit(solution)/shard_map/ppermute | solution.py:12
  95.4 2.7 collective-permute-done
  98.1 3.9 %collective-permute-start.1 = (bf16[128,1152]{1,0:T(8,128)(2,1)S(1)}, bf16[128,1152]{1,0:T(8,128)(2,1)S(1)}, u32[]{:S(2)}, u32[]{:S(2)}) collective-permute-start(bf16[128,1152]{1,0:T(8,128)(2,1)S(1)} %collective-permute-done), channel_id=1, source_target_pairs={{0,16},{16,32},{32,48},{48,64},{64,80},{80,96},{96,112},{112,128},... | collective-permute-start | bytes 884744 | tf_op jit(solution)/shard_map/ppermute | solution.py:12
  102.0 0.4 fusion.18
  102.4 2.0 collective-permute-done.3
  104.4 0.3 add_convert_fusion.2
  104.7 4.9 %collective-permute-start.4 = (bf16[128,1152]{1,0:T(8,128)(2,1)S(1)}, bf16[128,1152]{1,0:T(8,128)(2,1)S(1)}, u32[]{:S(2)}, u32[]{:S(2)}) collective-permute-start(bf16[128,1152]{1,0:T(8,128)(2,1)S(1)} %add_convert_fusion.2), channel_id=1, source_target_pairs={{0,16},{16,32},{32,48},{48,64},{64,80},{80,96},{96,112},{112,128},... | collective-permute-start | bytes 884744 | tf_op jit(solution)/shard_map/ppermute | solution.py:12
  109.6 1.1 collective-permute-done.1
  110.7 4.5 %collective-permute-start.2 = (bf16[128,1152]{1,0:T(8,128)(2,1)S(1)}, bf16[128,1152]{1,0:T(8,128)(2,1)S(1)}, u32[]{:S(2)}, u32[]{:S(2)}) collective-permute-start(bf16[128,1152]{1,0:T(8,128)(2,1)S(1)} %collective-permute-done.1), channel_id=1, source_target_pairs={{0,16},{16,32},{32,48},{48,64},{64,80},{80,96},{96,112},{112,128},... | collective-permute-start | bytes 884744 | tf_op jit(solution)/shard_map/ppermute | solution.py:12
  115.2 0.4 fusion.19
  115.6 0.3 fusion.22
  115.9 1.1 collective-permute-done.4
  117.1 0.1 add_convert_fusion.1
  117.1 5.4 %collective-permute-start.5 = (bf16[128,1152]{1,0:T(8,128)(2,1)S(1)}, bf16[128,1152]{1,0:T(8,128)(2,1)S(1)}, u32[]{:S(2)}, u32[]{:S(2)}) collective-permute-start(bf16[128,1152]{1,0:T(8,128)(2,1)S(1)} %add_convert_fusion.1), channel_id=1, source_target_pairs={{0,16},{16,32},{32,48},{48,64},{64,80},{80,96},{96,112},{112,128},... | collective-permute-start | bytes 884744 | tf_op jit(solution)/shard_map/ppermute | solution.py:12
  122.5 0.9 collective-permute-done.2
  123.4 0.4 fusion.20
  123.8 0.3 fusion.23
  124.1 5.3 %collective-permute-done.5 = bf16[128,1152]{1,0:T(8,128)(2,1)S(1)} collective-permute-done((bf16[128,1152]{1,0:T(8,128)(2,1)S(1)}, bf16[128,1152]{1,0:T(8,128)(2,1)S(1)}, u32[]{:S(2)}, u32[]{:S(2)}) %collective-permute-start.5) | collective-permute-done | bytes 294944 | tf_op jit(solution)/shard_map/ppermute | solution.py:12
  129.3 0.1 add_convert_fusion
  129.4 8.8 %collective-permute-start.6 = (bf16[128,1152]{1,0:T(8,128)(2,1)S(1)}, bf16[128,1152]{1,0:T(8,128)(2,1)S(1)}, u32[]{:S(2)}, u32[]{:S(2)}) collective-permute-start(bf16[128,1152]{1,0:T(8,128)(2,1)S(1)} %add_convert_fusion), channel_id=1, source_target_pairs={{0,464},{16,480},{32,496},{48,0},{64,16},{80,32},{96,48},{112,64},... | collective-permute-start | bytes 884744 | tf_op jit(solution)/shard_map/ppermute | solution.py:12
  138.2 4.4 %collective-permute-done.6 = bf16[128,1152]{1,0:T(8,128)(2,1)S(1)} collective-permute-done((bf16[128,1152]{1,0:T(8,128)(2,1)S(1)}, bf16[128,1152]{1,0:T(8,128)(2,1)S(1)}, u32[]{:S(2)}, u32[]{:S(2)}) %collective-permute-start.6) | collective-permute-done | bytes 294944 | tf_op jit(solution)/shard_map/ppermute | solution.py:12
  142.6 0.2 fusion.14
  142.8 0.2 fusion.16
  143.0 2.4 fusion
  145.4 0.0 all-reduce.3.cloned.1.call-update
  145.4 1.3 dynamic-slice
  147.3 0.3 fusion.24
  147.6 0.3 convolution_add_fusion.2
  147.9 0.0 copy-start.1
  147.9 0.3 convolution_add_fusion.1
  148.2 0.5 add_multiply_fusion
  148.7 0.4 fusion.9
  149.1 0.9 fusion.12
  150.1 0.0 copy-done.1
  150.1 1.6 convolution_convert_fusion.1
  151.7 186.1 %all-reduce.3.cloned.1.call-done = bf16[1152,1152]{0,1:T(8,128)(2,1)} async-done(((bf16[1152,1152]{0,1:T(8,128)(2,1)}), bf16[1152,1152]{0,1:T(8,128)(2,1)}) %all-reduce.3.cloned.1.call-update) | async-done | bytes 2654224
  337.8 1.2 dynamic-slice_convert_fusion
  339.0 0.9 copy.11
  (2 shorter events, 0.0 us)
Async XLA Ops:
  7.2 75.1 %copy-start = (bf16[128,1152]{1,0:T(8,128)(2,1)S(1)}, bf16[128,1152]{1,0:T(8,128)(2,1)}, u32[]{:S(2)}) copy-start(bf16[128,1152]{1,0:T(8,128)(2,1)} %param.7) | copy-start | bytes 884740
  7.2 80.9 %copy-start.2 = (bf16[128,1152]{1,0:T(8,128)(2,1)S(1)}, bf16[128,1152]{1,0:T(8,128)(2,1)}, u32[]{:S(2)}) copy-start(bf16[128,1152]{1,0:T(8,128)(2,1)} %param.6) | copy-start | bytes 884740
  7.2 75.1 %all-gather.2.cloned.1.call-start = ((), (), s32[]{:S(2)}) async-start(), calls=%async_computation | async-start | bytes 2820096 | tf_op jit(solution)/shard_map/all_gather | solution.py:30
  7.9 329.9 %all-reduce.3.cloned.1.call-start = ((), (), s32[]{:S(2)}) async-start(), calls=%async_computation.1 | async-start | bytes 5308416
  84.9 13.2 %collective-permute-start = (bf16[128,1152]{1,0:T(8,128)(2,1)S(1)}, bf16[128,1152]{1,0:T(8,128)(2,1)S(1)}, u32[]{:S(2)}, u32[]{:S(2)}) collective-permute-start(bf16[128,1152]{1,0:T(8,128)(2,1)S(1)} %multiply_convert_fusion), channel_id=1, source_target_pairs={{0,16},{16,32},{32,48},{48,64},{64,80},{80,96},{96,112},{112,128},... | collective-permute-start | bytes 884744 | tf_op jit(solution)/shard_map/ppermute | solution.py:12
  88.8 15.6 %collective-permute-start.3 = (bf16[128,1152]{1,0:T(8,128)(2,1)S(1)}, bf16[128,1152]{1,0:T(8,128)(2,1)S(1)}, u32[]{:S(2)}, u32[]{:S(2)}) collective-permute-start(bf16[128,1152]{1,0:T(8,128)(2,1)S(1)} %convolution_convert_fusion.2), channel_id=1, source_target_pairs={{0,16},{16,32},{32,48},{48,64},{64,80},{80,96},{96,112},{112,128},... | collective-permute-start | bytes 884744 | tf_op jit(solution)/shard_map/ppermute | solution.py:12
  98.1 12.6 %collective-permute-start.1 = (bf16[128,1152]{1,0:T(8,128)(2,1)S(1)}, bf16[128,1152]{1,0:T(8,128)(2,1)S(1)}, u32[]{:S(2)}, u32[]{:S(2)}) collective-permute-start(bf16[128,1152]{1,0:T(8,128)(2,1)S(1)} %collective-permute-done), channel_id=1, source_target_pairs={{0,16},{16,32},{32,48},{48,64},{64,80},{80,96},{96,112},{112,128},... | collective-permute-start | bytes 884744 | tf_op jit(solution)/shard_map/ppermute | solution.py:12
  104.7 12.3 %collective-permute-start.4 = (bf16[128,1152]{1,0:T(8,128)(2,1)S(1)}, bf16[128,1152]{1,0:T(8,128)(2,1)S(1)}, u32[]{:S(2)}, u32[]{:S(2)}) collective-permute-start(bf16[128,1152]{1,0:T(8,128)(2,1)S(1)} %add_convert_fusion.2), channel_id=1, source_target_pairs={{0,16},{16,32},{32,48},{48,64},{64,80},{80,96},{96,112},{112,128},... | collective-permute-start | bytes 884744 | tf_op jit(solution)/shard_map/ppermute | solution.py:12
  110.7 12.6 %collective-permute-start.2 = (bf16[128,1152]{1,0:T(8,128)(2,1)S(1)}, bf16[128,1152]{1,0:T(8,128)(2,1)S(1)}, u32[]{:S(2)}, u32[]{:S(2)}) collective-permute-start(bf16[128,1152]{1,0:T(8,128)(2,1)S(1)} %collective-permute-done.1), channel_id=1, source_target_pairs={{0,16},{16,32},{32,48},{48,64},{64,80},{80,96},{96,112},{112,128},... | collective-permute-start | bytes 884744 | tf_op jit(solution)/shard_map/ppermute | solution.py:12
  117.1 12.2 %collective-permute-start.5 = (bf16[128,1152]{1,0:T(8,128)(2,1)S(1)}, bf16[128,1152]{1,0:T(8,128)(2,1)S(1)}, u32[]{:S(2)}, u32[]{:S(2)}) collective-permute-start(bf16[128,1152]{1,0:T(8,128)(2,1)S(1)} %add_convert_fusion.1), channel_id=1, source_target_pairs={{0,16},{16,32},{32,48},{48,64},{64,80},{80,96},{96,112},{112,128},... | collective-permute-start | bytes 884744 | tf_op jit(solution)/shard_map/ppermute | solution.py:12
  129.4 13.2 %collective-permute-start.6 = (bf16[128,1152]{1,0:T(8,128)(2,1)S(1)}, bf16[128,1152]{1,0:T(8,128)(2,1)S(1)}, u32[]{:S(2)}, u32[]{:S(2)}) collective-permute-start(bf16[128,1152]{1,0:T(8,128)(2,1)S(1)} %add_convert_fusion), channel_id=1, source_target_pairs={{0,464},{16,480},{32,496},{48,0},{64,16},{80,32},{96,48},{112,64},... | collective-permute-start | bytes 884744 | tf_op jit(solution)/shard_map/ppermute | solution.py:12
  147.9 2.2 copy-start.1
Sparse Core Ops, SparseCore 0:
  11.4 70.8 all-gather.1
  145.5 192.2 all-reduce.2
where the time goes:
time: 348 us; the launch traced here: 347 us
  waiting for transfers between devices  276 us (79%)
  starting transfers between devices  37.3 us (11%)
  between operations  16.2 us (5%)
  matrix products  10.5 us (3%)
  other arithmetic  4.42 us (1%)
    unnamed x3, waiting for transfers between devices  187 us
    all_gather x1, waiting for transfers between devices, per_device(): lax.all_gather(head_weight, 'fsdp', axis=0, tiled=True)  71.9 us
    ppermute x7, starting transfers between devices, shifted(): return lax.ppermute(value, axis, pairs)  37.2 us
    ppermute x7, waiting for transfers between devices, shifted(): return lax.ppermute(value, axis, pairs)  17.4 us
  transfers between devices with their start and end apart: 9, of which 9 were waited for; matrix products, arithmetic and copies ran while one was open for 3% of the time, Pallas kernels for 0%

commit v1 on v0

v1 whole, which is shorter than its diff:
```python
import jax
import jax.numpy as jnp
from jax import lax
from jax.experimental import pallas as pl
from jax.experimental.pallas import tpu as pltpu
from jax.sharding import PartitionSpec as P

MESH = pl.DeviceIdType.MESH
F32 = jnp.float32
BF16 = jnp.bfloat16
NT = (((1,), (1,)), ((), ()))

ROWS = 128
WIDTH = 1152
SHARD = 72
CHIP = 144
UNIT = 80
PART = 64
AHEAD = 48
TILE = 384
ORDER = ((0, 2), (1, 2), (0, 1), (1, 1), (0, 3), (1, 3), (0, 0), (1, 0))


def normalize(v):
    r = lax.rsqrt(jnp.sum(v * v, axis=-1, keepdims=True) + 1e-06)
    return v * r, r


def kernel(
    img, pool, wsh, hb, log_scale, bias,
    loss_out, img_out, pool_out, head_out,
    wtmp, wf, xbuf, pbuf, xhat, ximg, zhat, ztxt, dz, dx, dzb, pt, ssum,
    tbuf, rbuf, stage, far, near, yout, yin,
    w_s, w_r, x_s, x_r, p_s, p_r, t_s, t_r, g_s, g_r,
):
    dp = lax.axis_index("dp")
    f = lax.axis_index("fsdp")
    j = lax.rem(dp, 4)
    yh = lax.div(f, 8)
    x = lax.rem(lax.div(f, 2), 4)
    c = lax.rem(f, 2)
    base = yh * 8 + c

    sib = (dp, f + 1 - 2 * c)
    xp = (dp, base + 2 * lax.rem(x + 1, 4))
    xm = (dp, base + 2 * lax.rem(x + 3, 4))
    zp = (lax.rem(dp + 4, 32), f)
    zm = (lax.rem(dp + 28, 32), f)
    wrap_up = lax.div(j + 1, 4)
    up = (dp + 1 - 4 * wrap_up, lax.rem(f + 8 * wrap_up, 16))
    wrap_dn = lax.div(3 - j, 3)
    dn = (dp - 1 + 4 * wrap_dn, lax.rem(f + 8 * wrap_dn, 16))
    opp = (dp, lax.rem(f + 8, 16))

    barrier = pltpu.get_barrier_semaphore()
    for who in (sib, xp, xm, zp, zm, up, dn, opp):
        pl.semaphore_signal(barrier, inc=1, device_id=who, device_id_type=MESH)
    pl.semaphore_wait(barrier, 8)

    def copy(src, dst, send, recv, who):
        return pltpu.make_async_remote_copy(
            src_ref=src, dst_ref=dst, send_sem=send, recv_sem=recv, device_id=who, device_id_type=MESH
        )

    def send_x(k, src):
        @pl.when(jnp.logical_and(k <= 3 - j, j >= 1))
        def _():
            copy(src, xbuf.at[k + 1], x_s.at[k], x_r.at[k + 1], dn).start()

        @pl.when(jnp.logical_and(k > 3 - j, j <= 2))
        def _():
            copy(src, xbuf.at[k - 1], x_s.at[k], x_r.at[k - 1], up).start()

    def send_p(k, src):
        @pl.when(jnp.logical_and(k <= j, j <= 2))
        def _():
            copy(src, pbuf.at[k + 1], p_s.at[k], p_r.at[k + 1], up).start()

        @pl.when(jnp.logical_and(k > j, j >= 1))
        def _():
            copy(src, pbuf.at[k - 1], p_s.at[k], p_r.at[k - 1], dn).start()

    def wait_x(k):
        copy(xbuf.at[k], xbuf.at[k], x_s.at[k], x_r.at[k], up).wait_recv()

    def wait_p(k):
        copy(pbuf.at[k], pbuf.at[k], p_s.at[k], p_r.at[k], up).wait_recv()

    def x_done(k, src):
        @pl.when(jnp.logical_or(jnp.logical_and(k <= 3 - j, j >= 1), jnp.logical_and(k > 3 - j, j <= 2)))
        def _():
            copy(src, xbuf.at[1], x_s.at[k], x_r.at[1], up).wait_send()

    def p_done(k, src):
        @pl.when(jnp.logical_or(jnp.logical_and(k <= j, j <= 2), jnp.logical_and(k > j, j >= 1)))
        def _():
            copy(src, pbuf.at[1], p_s.at[k], p_r.at[1], up).wait_send()

    xk0 = 1 + 2 * lax.div(j, 3)
    xk1 = 2 + lax.div(j, 2) - lax.div(j, 3)
    xk2 = 6 - xk0 - xk1
    pk0 = 1 + 2 * lax.div(3 - j, 3)
    pk1 = 2 + lax.rem(lax.div(j + 1, 2), 2)
    pk2 = 6 - pk0 - pk1

    w_swap = copy(wsh, wtmp, w_s.at[0], w_r.at[0], sib)
    w_swap.start()
    x_hop = copy(img, xbuf.at[4], x_s.at[5], x_r.at[4], zm)
    p_hop = copy(pool, pbuf.at[4], p_s.at[5], p_r.at[4], zp)

    @pl.when(j <= 2)
    def _():
        x_hop.start()

    send_x(0, img)

    @pl.when(j >= 1)
    def _():
        p_hop.start()

    send_p(0, pool)

    v, xr = normalize(img[...].astype(F32))
    ximg[...] = v
    xhat[...] = v.astype(BF16)

    def chip(h, off):
        return h * 4 + lax.rem(x + off, 4)

    def rows_of(m, start, size):
        return wf.at[pl.ds(pl.multiple_of(m * CHIP + start, 16), size), :]

    def unit(m):
        return rows_of(m, 64 * c, UNIT)

    def w_copy(src, dst, ident, who, send=None):
        return copy(src, dst, w_s.at[ident if send is None else send], w_r.at[ident], who)

    w_sent = []

    def w_go(src, ident, who):
        d = w_copy(src, src, ident, who)
        d.start()
        w_sent.append(d)

    mine = chip(yh, 0)
    theirs = chip(1 - yh, 0)
    w_swap.wait_recv()
    own_rows = wsh[...].astype(F32)
    sib_rows = wtmp[...].astype(F32)
    first = c == 0
    wf[pl.ds(pl.multiple_of(mine * CHIP, 16), CHIP), :] = jnp.concatenate(
        [jnp.where(first, own_rows, sib_rows), jnp.where(first, sib_rows, own_rows)], axis=0
    ).astype(BF16)

    w_edge_up = w_copy(unit(mine), unit(mine), 9, up)
    w_edge_dn = w_copy(unit(mine), unit(mine), 9, dn)
    w_pass_up = w_copy(unit(theirs), unit(theirs), 9, up, 10)
    w_pass_dn = w_copy(unit(theirs), unit(theirs), 9, dn, 10)

    @pl.when(j == 3)
    def _():
        w_edge_up.start()

    @pl.when(j == 0)
    def _():
        w_edge_dn.start()

    w_go(unit(mine), 1, xp)
    w_go(unit(mine), 2, xm)

    pt[...] = pool[...].astype(F32).T.astype(BF16)

    def to_sibling(m, ident):
        w_go(rows_of(m, 80 * c, PART), ident, sib)

    def near_units(r, h):
        for d, (off, onward) in enumerate(((3, xp), (1, xm))):
            m = chip(h, off)
            w_copy(unit(m), unit(m), 1 + 2 * r + d, xp).wait_recv()
            if d == 0:
                w_go(rows_of(m, 64 * c, AHEAD), 5 + 2 * r, onward)
            else:
                w_go(rows_of(m, 64 * c + AHEAD, UNIT - AHEAD), 6 + 2 * r, onward)
            to_sibling(m, 11 + 4 * r + d)

    def far_units(r, h):
        m = chip(h, 2)
        part = rows_of(m, 64 * c, AHEAD)
        w_copy(part, part, 5 + 2 * r, xp).wait_recv()
        part = rows_of(m, 64 * c + AHEAD, UNIT - AHEAD)
        w_copy(part, part, 6 + 2 * r, xp).wait_recv()
        to_sibling(m, 13 + 4 * r)

    other = w_copy(unit(theirs), unit(theirs), 9, xp)
    near_units(0, yh)

    outer = jnp.logical_or(j == 0, j == 3)
    inner = jnp.logical_and(j >= 1, j <= 2)

    @pl.when(outer)
    def _():
        other.wait_recv()

    @pl.when(j == 0)
    def _():
        w_pass_up.start()

    @pl.when(j == 3)
    def _():
        w_pass_dn.start()

    @pl.when(j <= 2)
    def _():
        wait_x(1)
        send_x(1, xbuf.at[1])
        wait_x(4)
        send_x(4, xbuf.at[4])

    far_units(0, yh)

    @pl.when(inner)
    def _():
        other.wait_recv()

    w_go(unit(theirs), 3, xp)
    w_go(unit(theirs), 4, xm)
    to_sibling(theirs, 14)

    @pl.when(j <= 2)
    def _():
        wait_x(xk1)
        send_x(xk1, xbuf.at[xk1])

    @pl.when(j >= 1)
    def _():
        wait_p(4)
        send_p(4, pbuf.at[4])

    near_units(1, 1 - yh)
    far_units(1, 1 - yh)

    @pl.when(inner)
    def _():
        wait_x(xk2)
        send_x(xk2, xbuf.at[xk2])

    @pl.when(j >= 1)
    def _():
        wait_p(1)
        send_p(1, pbuf.at[1])

    for ident, m in (
        (11, chip(yh, 3)), (12, chip(yh, 1)), (13, chip(yh, 2)), (14, theirs),
        (15, chip(1 - yh, 3)), (16, chip(1 - yh, 1)), (17, chip(1 - yh, 2)),
    ):
        got = rows_of(m, 80 - 80 * c, PART)
        w_copy(got, got, ident, sib).wait_recv()

    temper = jnp.exp(jnp.full((1, 128), log_scale[0], F32))
    offset = jnp.full((1, 128), bias[0], F32)
    gain = temper * (1.0 / ROWS)
    eye = lax.broadcasted_iota(jnp.int32, (ROWS, ROWS), 0) == lax.broadcasted_iota(jnp.int32, (ROWS, ROWS), 1)

    def project(block, out):
        @pl.loop(0, WIDTH // TILE)
        def _(n):
            cols = pl.ds(pl.multiple_of(n * TILE, TILE), TILE)
            out[:, cols] = jnp.dot(block[...], wf[:, cols], preferred_element_type=F32) + hb[:, cols]

    def weights(a, b, own):
        l = temper * lax.dot_general(a, b, NT, preferred_element_type=F32) + offset
        m = jnp.where(eye, -l, l) if own else l
        g = gain / (1.0 + jnp.exp(-m))
        if own:
            g = jnp.where(eye, -g, g)
        return m, g.astype(BF16)

    def softplus(m):
        return jnp.maximum(m, 0.0) + jnp.log1p(jnp.exp(-jnp.abs(m)))

    project(pool, ztxt)
    v, zr = normalize(ztxt[...])
    ztxt[...] = v
    zhat[...] = v.astype(BF16)

    _, g = weights(zhat[...], xhat[...], True)
    dz[...] = jnp.dot(g, xhat[...], preferred_element_type=F32)
    for i, k in enumerate((xk0, xk1, xk2)):
        @pl.when(outer if i == 2 else j == 3)
        def _():
            wait_x(k)

        xh = normalize(xbuf[k].astype(F32))[0].astype(BF16)
        _, g = weights(zhat[...], xh, False)
        dz[...] += jnp.dot(g, xh, preferred_element_type=F32)

    v = ztxt[...]
    d = dz[...]
    dzb[...] = (zr * (d - v * jnp.sum(v * d, axis=-1, keepdims=True))).astype(BF16)

    for i, (h, off) in enumerate(ORDER):
        m = chip(h, off)
        t = jnp.dot(
            pt[pl.ds(pl.multiple_of(m * CHIP, 16), CHIP), :], dzb[...], preferred_element_type=F32
        ).astype(BF16).astype(F32)
        tbuf[0, i] = t[:SHARD].astype(BF16)
        tbuf[1, i] = t[SHARD:].astype(BF16)
        copy(tbuf.at[1 - c, i], rbuf.at[i], t_s.at[i], t_r.at[i], sib).start()

    @pl.when(inner)
    def _():
        wait_p(pk1)
        send_p(pk1, pbuf.at[pk1])

    def pair_sum(i):
        copy(rbuf.at[i], rbuf.at[i], t_s.at[i], t_r.at[i], sib).wait_recv()
        return tbuf[c, i].astype(F32) + rbuf[i].astype(F32)

    g_sent = []

    def g_go(value, ident, dst, who):
        stage[ident] = value.astype(BF16)
        d = copy(stage.at[ident], dst, g_s.at[ident], g_r.at[ident], who)
        d.start()
        g_sent.append(d)

    def g_wait(ref, ident):
        copy(ref, ref, g_s.at[ident], g_r.at[ident], xp).wait_recv()
        return ref[...].astype(F32)

    g_go(pair_sum(0), 0, far.at[0], xp)
    g_go(pair_sum(1), 1, far.at[1], xm)
    g_go(pair_sum(3), 2, near.at[0, 1], xp)
    g_go(pair_sum(4), 3, near.at[1, 0], xm)
    g_go(pair_sum(2) + g_wait(far.at[0], 0), 4, near.at[0, 0], xp)
    g_go(pair_sum(5) + g_wait(far.at[1], 1), 5, near.at[1, 1], xm)

    @pl.when(inner)
    def _():
        wait_p(pk2)
        send_p(pk2, pbuf.at[pk2])

    m, g = weights(xhat[...], zhat[...], True)
    ssum[...] = softplus(m)
    dx[...] = jnp.dot(g, zhat[...], preferred_element_type=F32)

    def text(k, u):
        project(pbuf.at[k], u)
        zh = normalize(u[...])[0].astype(BF16)
        m, g = weights(xhat[...], zh, False)
        ssum[...] += softplus(m)
        dx[...] += jnp.dot(g, zh, preferred_element_type=F32)

    @pl.when(j == 0)
    def _():
        wait_p(pk0)

    text(pk0, dz)

    @pl.loop(0, WIDTH // TILE)
    def _(n):
        cols = pl.ds(pl.multiple_of(n * TILE, TILE), TILE)
        pool_out[:, cols] = lax.dot_general(
            dzb[...], wf[cols, :], NT, preferred_element_type=F32
        ).astype(BF16)

    total = []
    for h in range(2):
        total.append(pair_sum(6 + h) + g_wait(near.at[0, h], 4 - 2 * h) + g_wait(near.at[1, h], 3 + 2 * h))
    low = yh == 0
    yout[...] = jnp.where(low, total[1], total[0]).astype(BF16)
    head_out[...] = jnp.where(low, total[0], total[1])
    y_copy = copy(yout, yin, g_s.at[6], g_r.at[6], opp)
    y_copy.start()

    for k in (pk1, pk2):
        @pl.when(outer)
        def _():
            wait_p(k)

        text(k, dz)

    loss_out[...] = jnp.sum(ssum[...].T, axis=0, keepdims=True) * (1.0 / ROWS)
    v = ximg[...]
    d = dx[...]
    img_out[...] = (xr * (d - v * jnp.sum(v * d, axis=-1, keepdims=True))).astype(BF16)

    y_copy.wait_recv()
    head_out[...] += yin[...].astype(F32)

    w_swap.wait_send()
    for d in w_sent:
        d.wait_send()

    @pl.when(j == 3)
    def _():
        w_edge_up.wait_send()
        w_pass_dn.wait_send()

    @pl.when(j == 0)
    def _():
        w_edge_dn.wait_send()
        w_pass_up.wait_send()

    @pl.when(j <= 2)
    def _():
        x_hop.wait_send()

    @pl.when(j >= 1)
    def _():
        p_hop.wait_send()

    x_done(0, img)
    p_done(0, pool)
    for k in range(1, 4):
        x_done(k, xbuf.at[k])
        p_done(k, pbuf.at[k])
    x_done(4, xbuf.at[4])
    p_done(4, pbuf.at[4])
    for i in range(8):
        copy(tbuf.at[1 - c, i], rbuf.at[i], t_s.at[i], t_r.at[i], sib).wait_send()
    for d in g_sent:
        d.wait_send()
    y_copy.wait_send()


def per_device(images, pooled, head_weight, head_bias, log_scale, bias):
    vmem = pl.BlockSpec(memory_space=pltpu.VMEM)
    smem = pl.BlockSpec(memory_space=pltpu.SMEM)
    block = (ROWS, WIDTH)
    slab = (SHARD, WIDTH)
    dma = pltpu.SemaphoreType.DMA
    loss, image_grad, pooled_grad, head_grad = pl.pallas_call(
        kernel,
        out_shape=(
            jax.ShapeDtypeStruct((1, ROWS), F32),
            jax.ShapeDtypeStruct(block, BF16),
            jax.ShapeDtypeStruct(block, BF16),
            jax.ShapeDtypeStruct(slab, F32),
        ),
        in_specs=[vmem, vmem, vmem, vmem, smem, smem],
        out_specs=(vmem, vmem, vmem, vmem),
        scratch_shapes=[
            pltpu.VMEM(slab, BF16),
            pltpu.VMEM((WIDTH, WIDTH), BF16),
            pltpu.VMEM((5,) + block, BF16),
            pltpu.VMEM((5,) + block, BF16),
            pltpu.VMEM(block, BF16),
            pltpu.VMEM(block, F32),
            pltpu.VMEM(block, BF16),
            pltpu.VMEM(block, F32),
            pltpu.VMEM(block, F32),
            pltpu.VMEM(block, F32),
            pltpu.VMEM(block, BF16),
            pltpu.VMEM((WIDTH, ROWS), BF16),
            pltpu.VMEM((ROWS, ROWS), F32),
            pltpu.VMEM((2, 8) + slab, BF16),
            pltpu.VMEM((8,) + slab, BF16),
            pltpu.VMEM((6,) + slab, BF16),
            pltpu.VMEM((2,) + slab, BF16),
            pltpu.VMEM((2, 2) + slab, BF16),
            pltpu.VMEM(slab, BF16),
            pltpu.VMEM(slab, BF16),
            dma((18,)), dma((18,)),
            dma((6,)), dma((6,)),
            dma((6,)), dma((6,)),
            dma((8,)), dma((8,)),
            dma((7,)), dma((7,)),
        ],
        compiler_params=pltpu.CompilerParams(
            collective_id=0, has_side_effects=True, vmem_limit_bytes=40 * 1024 * 1024
        ),
        cost_estimate=pl.CostEstimate(flops=4_000_000_000, bytes_accessed=6_000_000, transcendentals=300_000),
    )(images, pooled, head_weight, head_bias.reshape(1, WIDTH), log_scale, bias)
    return loss.reshape(ROWS), image_grad, pooled_grad, head_grad


def solution(mesh):
    in_specs = (P(("dp", "fsdp"), None), P(("dp", "fsdp"), None), P("fsdp", None), P(), P(), P())
    out_specs = (
        P(("dp", "fsdp")),
        P(("dp", "fsdp"), None),
        P(("dp", "fsdp"), None),
        P(("dp", "fsdp"), None),
    )
    return jax.shard_map(
        per_device, mesh=mesh, in_specs=in_specs, out_specs=out_specs, check_vma=False
    )
```

time: 348 us -> 81.7 us (0.23)
  the two profiles are of different devices: /device:TPU:56 before, /device:TPU:24 now
where the time goes in v1:
time: 81.7 us; the launch traced here: 81.4 us
  Pallas kernels  73.3 us (90%)
  local copies, waits for them, and re-layouts  6.2 us (8%)
  between operations  1.94 us (2%)
    pallas_call x1, Pallas kernels, per_device(): pl.pallas_call(kernel, out_shape=(jax.ShapeDtypeStruct((1, ROWS), F32), j...  73.3 us
    unnamed x10, local copies, waits for them, and re-layouts  5.5 us

profile of v1, /device:TPU:24, one launch (start us, length us, event | category | flops | bytes accessed | tf_op | source)
XLA Modules:
  0.0 81.4 jit_solution(2898608505911839317)
XLA Ops:
  1.9 0.7 reshape.14.hb
  2.6 0.0 copy-start
  2.6 1.0 %copy-done = bf16[128,1152]{1,0:T(8,128)(2,1)S(1)} copy-done((bf16[128,1152]{1,0:T(8,128)(2,1)S(1)}, bf16[128,1152]{1,0:T(8,128)(2,1)}, u32[]{:S(2)}) %copy-start) | copy-done | bytes 294936
  3.6 0.0 copy-start.1
  3.6 1.0 %copy-done.1 = bf16[128,1152]{1,0:T(8,128)(2,1)S(1)} copy-done((bf16[128,1152]{1,0:T(8,128)(2,1)S(1)}, bf16[128,1152]{1,0:T(8,128)(2,1)}, u32[]{:S(2)}) %copy-start.1) | copy-done | bytes 294936
  4.5 0.0 copy-start.2
  4.6 0.9 %copy-done.2 = bf16[72,1152]{1,0:T(8,128)(2,1)S(1)} copy-done((bf16[72,1152]{1,0:T(8,128)(2,1)S(1)}, bf16[72,1152]{1,0:T(8,128)(2,1)}, u32[]{:S(2)}) %copy-start.2) | copy-done | bytes 165912
  5.5 73.3 %shard_map.93 = (f32[1,128]{1,0:T(1,128)S(1)}, bf16[128,1152]{1,0:T(8,128)(2,1)S(1)}, bf16[128,1152]{1,0:T(8,128)(2,1)S(1)}, f32[72,1152]{1,0:T(8,128)S(1)}) custom-call(bf16[128,1152]{1,0:T(8,128)(2,1)S(1)} %copy-done, bf16[128,1152]{1,0:T(8,128)(2,1)S(1)} %copy-done.1, bf16[72,1152]{1,0:T(8,128)(2,1)S(1)} %copy-done.2, f32[1,1152]{1,0:T(1,128)S(1)} %reshape.14.hb, ...), custom_call_target="tpu_custom_call" | custom-call | flops 4000000000 | bytes 6000000 | tf_op jit(solution)/shard_map/pallas_call | solution.py:434
  78.8 0.5 copy.16
  79.3 0.7 copy.17
  80.0 0.7 copy.18
  80.7 0.7 copy.19
Async XLA Ops:
  2.6 1.0 %copy-start = (bf16[128,1152]{1,0:T(8,128)(2,1)S(1)}, bf16[128,1152]{1,0:T(8,128)(2,1)}, u32[]{:S(2)}) copy-start(bf16[128,1152]{1,0:T(8,128)(2,1)} %img.1) | copy-start | bytes 884740
  3.6 1.0 %copy-start.1 = (bf16[128,1152]{1,0:T(8,128)(2,1)S(1)}, bf16[128,1152]{1,0:T(8,128)(2,1)}, u32[]{:S(2)}) copy-start(bf16[128,1152]{1,0:T(8,128)(2,1)} %pool.1) | copy-start | bytes 884740
  4.5 0.9 %copy-start.2 = (bf16[72,1152]{1,0:T(8,128)(2,1)S(1)}, bf16[72,1152]{1,0:T(8,128)(2,1)}, u32[]{:S(2)}) copy-start(bf16[72,1152]{1,0:T(8,128)(2,1)} %wsh.1) | copy-start | bytes 497668

commit v2 on v1

v2 whole, which is shorter than its diff:
```python
import jax
import jax.numpy as jnp
from jax import lax
from jax.experimental import pallas as pl
from jax.experimental.pallas import tpu as pltpu
from jax.sharding import PartitionSpec as P

MESH = pl.DeviceIdType.MESH
F32 = jnp.float32
BF16 = jnp.bfloat16
NT = (((1,), (1,)), ((), ()))

ROWS = 128
WIDTH = 1152
SHARD = 72
CHIP = 144
UNIT = 80
PART = 64
AHEAD = 48
TILE = 384
VMEM_GRANT = 60 * 1024 * 1024
HALF = 64
SPLIT = 640
ORDER = (2, 1, 3, 0)


def normalize(v):
    r = lax.rsqrt(jnp.sum(v * v, axis=-1, keepdims=True) + 1e-06)
    return v * r, r


def kernel(
    img_hbm, pool_hbm, wsh_hbm, hb_hbm, log_scale, bias,
    loss_hbm, img_grad_hbm, pool_grad_hbm, head_grad_hbm,
    img, pool, wsh, hb, loss_out, img_out, pool_out, head_out,
    wtmp, wf, xbuf, pbuf, xhat, ximg, zhat, ztxt, dz, dx, dzb, pt, ssum,
    t_a, t_b, r_a, r_b, st_a, st_b, far_a, far_b, near_a, near_b,
    y_a, y_b, pass_a, pass_b, in_a, in_b,
    xg, gdx, gsum, gdx_out, gsum_out, gdx_in, gsum_in,
    l_s, o_s, w_s, w_r, x_s, x_r, p_s, p_r, t_s, t_r, g_s, g_r, h_s, h_r,
):
    loads = [
        pltpu.make_async_copy(src, dst, l_s.at[i])
        for i, (src, dst) in enumerate(
            ((wsh_hbm, wsh), (img_hbm, img), (pool_hbm, pool), (hb_hbm, hb.at[0]))
        )
    ]
    for d in loads:
        d.start()
    stores = [
        pltpu.make_async_copy(src, dst, o_s.at[i])
        for i, (src, dst) in enumerate(
            ((loss_out, loss_hbm), (img_out, img_grad_hbm), (pool_out, pool_grad_hbm), (head_out, head_grad_hbm))
        )
    ]

    dp = lax.axis_index("dp")
    f = lax.axis_index("fsdp")
    j = lax.rem(dp, 4)
    yh = lax.div(f, 8)
    x = lax.rem(lax.div(f, 2), 4)
    c = lax.rem(f, 2)
    base = yh * 8 + c

    sib = (dp, f + 1 - 2 * c)
    xp = (dp, base + 2 * lax.rem(x + 1, 4))
    xm = (dp, base + 2 * lax.rem(x + 3, 4))
    zp = (lax.rem(dp + 4, 32), f)
    zm = (lax.rem(dp + 28, 32), f)
    wrap_up = lax.div(j + 1, 4)
    up = (dp + 1 - 4 * wrap_up, lax.rem(f + 8 * wrap_up, 16))
    wrap_dn = lax.div(3 - j, 3)
    dn = (dp - 1 + 4 * wrap_dn, lax.rem(f + 8 * wrap_dn, 16))
    wrap = lax.div(j + 2, 4)
    up2 = (dp + 2 - 4 * wrap, lax.rem(f + 8 * wrap, 16))
    wrap = lax.div(3 - j, 2)
    dn2 = (dp - 2 + 4 * wrap, lax.rem(f + 8 * wrap, 16))

    barrier = pltpu.get_barrier_semaphore()
    for who in (sib, xp, xm, zp, zm, up, dn, up2, dn2):
        pl.semaphore_signal(barrier, inc=1, device_id=who, device_id_type=MESH)
    pl.semaphore_wait(barrier, 9)
    for d in loads:
        d.wait()

    def copy(src, dst, send, recv, who):
        return pltpu.make_async_remote_copy(
            src_ref=src, dst_ref=dst, send_sem=send, recv_sem=recv, device_id=who, device_id_type=MESH
        )

    def part(ref, h):
        return ref.at[pl.ds(HALF * h, HALF), :]

    def send_x(k, src, h):
        @pl.when(jnp.logical_and(k <= 3 - j, j >= 1))
        def _():
            copy(part(src, h), part(xbuf.at[k + 1], h), x_s.at[k, h], x_r.at[k + 1, h], dn).start()

        @pl.when(jnp.logical_and(k > 3 - j, j <= 2))
        def _():
            copy(part(src, h), part(xbuf.at[k - 1], h), x_s.at[k, h], x_r.at[k - 1, h], up).start()

    def send_p(k, src, h):
        @pl.when(jnp.logical_and(k <= j, j <= 1))
        def _():
            copy(part(src, h), part(pbuf.at[k + 1], h), p_s.at[k, h], p_r.at[k + 1, h], up).start()

        @pl.when(jnp.logical_and(k > j, j >= 2))
        def _():
            copy(part(src, h), part(pbuf.at[k - 1], h), p_s.at[k, h], p_r.at[k - 1, h], dn).start()

    def wait_x(k, h, whole=False):
        dst = xbuf.at[k] if whole else part(xbuf.at[k], h)
        copy(dst, dst, x_s.at[k, h], x_r.at[k, h], up).wait_recv()

    def wait_p(k, h):
        dst = part(pbuf.at[k], h)
        copy(dst, dst, p_s.at[k, h], p_r.at[k, h], up).wait_recv()

    def pass_x(k, h):
        wait_x(k, h)
        send_x(k, xbuf.at[k], h)

    def pass_p(k):
        for h in range(2):
            wait_p(k, h)
            send_p(k, pbuf.at[k], h)

    def x_done(k, src):
        @pl.when(jnp.logical_or(jnp.logical_and(k <= 3 - j, j >= 1), jnp.logical_and(k > 3 - j, j <= 2)))
        def _():
            for h in range(2):
                copy(part(src, h), part(xbuf.at[1], h), x_s.at[k, h], x_r.at[1, h], up).wait_send()

    def p_done(k, src):
        @pl.when(jnp.logical_or(jnp.logical_and(k <= j, j <= 1), jnp.logical_and(k > j, j >= 2)))
        def _():
            for h in range(2):
                copy(part(src, h), part(pbuf.at[1], h), p_s.at[k, h], p_r.at[1, h], up).wait_send()

    middle = lax.rem(lax.div(j + 1, 2), 2)
    outer = middle == 0
    inner = middle == 1
    xk0 = 1 + 2 * lax.div(j, 3)
    xk1 = 2 + middle
    xk2 = 6 - xk0 - xk1
    guest = copy(img, xbuf.at[5], x_s.at[6, 0], x_r.at[5, 0], up)

    w_swap = copy(wsh, wtmp, w_s.at[0], w_r.at[0], sib)
    w_swap.start()
    x_hop = [copy(part(img, h), part(xbuf.at[4], h), x_s.at[5, h], x_r.at[4, h], zm) for h in range(2)]
    p_hop = [copy(part(pool, h), part(pbuf.at[4], h), p_s.at[5, h], p_r.at[4, h], zp) for h in range(2)]

    @pl.when(j <= 2)
    def _():
        for d in x_hop:
            d.start()

    send_x(0, img, 0)
    send_x(0, img, 1)
    send_p(0, pool, 0)

    @pl.when(j >= 1)
    def _():
        for d in p_hop:
            d.start()

    v, xr = normalize(img[...].astype(F32))
    ximg[...] = v
    xhat[...] = v.astype(BF16)

    def chip(h, off):
        return h * 4 + lax.rem(x + off, 4)

    def rows_of(m, start, size):
        return wf.at[pl.ds(pl.multiple_of(m * CHIP + start, 16), size), :]

    def unit(m):
        return rows_of(m, 64 * c, UNIT)

    def w_copy(src, dst, ident, who, send=None):
        return copy(src, dst, w_s.at[ident if send is None else send], w_r.at[ident], who)

    w_sent = []

    def w_go(src, ident, who):
        d = w_copy(src, src, ident, who)
        d.start()
        w_sent.append(d)

    mine = chip(yh, 0)
    theirs = chip(1 - yh, 0)
    w_swap.wait_recv()
    own_rows = wsh[...].astype(F32)
    sib_rows = wtmp[...].astype(F32)
    first = c == 0
    wf[pl.ds(pl.multiple_of(mine * CHIP, 16), CHIP), :] = jnp.concatenate(
        [jnp.where(first, own_rows, sib_rows), jnp.where(first, sib_rows, own_rows)], axis=0
    ).astype(BF16)

    w_edge_up = w_copy(unit(mine), unit(mine), 9, up)
    w_edge_dn = w_copy(unit(mine), unit(mine), 9, dn)
    w_pass_up = w_copy(unit(theirs), unit(theirs), 9, up, 10)
    w_pass_dn = w_copy(unit(theirs), unit(theirs), 9, dn, 10)

    @pl.when(j == 3)
    def _():
        w_edge_up.start()

    @pl.when(j == 0)
    def _():
        w_edge_dn.start()

    w_go(unit(mine), 1, xp)
    w_go(unit(mine), 2, xm)

    pt[...] = pool[...].astype(F32).T.astype(BF16)

    def to_sibling(m, ident):
        w_go(rows_of(m, 80 * c, PART), ident, sib)

    def near_units(r, h):
        for d, (off, onward) in enumerate(((3, xp), (1, xm))):
            m = chip(h, off)
            w_copy(unit(m), unit(m), 1 + 2 * r + d, xp).wait_recv()
            if d == 0:
                w_go(rows_of(m, 64 * c, AHEAD), 5 + 2 * r, onward)
            else:
                w_go(rows_of(m, 64 * c + AHEAD, UNIT - AHEAD), 6 + 2 * r, onward)
            to_sibling(m, 11 + 4 * r + d)

    def far_units(r, h):
        m = chip(h, 2)
        part = rows_of(m, 64 * c, AHEAD)
        w_copy(part, part, 5 + 2 * r, xp).wait_recv()
        part = rows_of(m, 64 * c + AHEAD, UNIT - AHEAD)
        w_copy(part, part, 6 + 2 * r, xp).wait_recv()
        to_sibling(m, 13 + 4 * r)

    other = w_copy(unit(theirs), unit(theirs), 9, xp)
    theirs_xp = w_copy(unit(theirs), unit(theirs), 3, xp)
    theirs_xm = w_copy(unit(theirs), unit(theirs), 4, xm)
    theirs_part = rows_of(theirs, 80 * c, PART)
    theirs_sib = w_copy(theirs_part, theirs_part, 14, sib)
    w_sent.extend((theirs_xp, theirs_xm, theirs_sib))

    def send_theirs():
        theirs_xp.start()
        theirs_xm.start()
        theirs_sib.start()

    for h in range(2):
        @pl.when(j <= 2)
        def _():
            pass_x(4, h)

        @pl.when(inner)
        def _():
            pass_x(1, h)

    near_units(0, yh)

    @pl.when(outer)
    def _():
        other.wait_recv()

    @pl.when(j == 0)
    def _():
        w_pass_up.start()

    @pl.when(j == 3)
    def _():
        w_pass_dn.start()

    @pl.when(outer)
    def _():
        send_theirs()

    @pl.when(inner)
    def _():
        pass_x(3, 0)

    @pl.when(j == 0)
    def _():
        send_p(0, pool, 1)
        guest.start()

    @pl.when(j == 3)
    def _():
        pass_p(4)

    far_units(0, yh)

    @pl.when(inner)
    def _():
        pass_x(3, 1)
        other.wait_recv()
        send_theirs()
        pass_x(2, 0)

    near_units(1, 1 - yh)

    @pl.when(inner)
    def _():
        pass_x(2, 1)

    @pl.when(j == 1)
    def _():
        send_p(0, pool, 1)
        pass_p(1)

    @pl.when(j == 2)
    def _():
        pass_p(4)

    far_units(1, 1 - yh)

    @pl.when(j == 2)
    def _():
        pass_p(3)

    for ident, m in (
        (11, chip(yh, 3)), (12, chip(yh, 1)), (13, chip(yh, 2)), (14, theirs),
        (15, chip(1 - yh, 3)), (16, chip(1 - yh, 1)), (17, chip(1 - yh, 2)),
    ):
        got = rows_of(m, 80 - 80 * c, PART)
        w_copy(got, got, ident, sib).wait_recv()

    temper = jnp.exp(jnp.full((1, 128), log_scale[0], F32))
    offset = jnp.full((1, 128), bias[0], F32)
    gain = temper * (1.0 / ROWS)
    eye = lax.broadcasted_iota(jnp.int32, (ROWS, ROWS), 0) == lax.broadcasted_iota(jnp.int32, (ROWS, ROWS), 1)

    def project(block, out):
        @pl.loop(0, WIDTH // TILE)
        def _(n):
            cols = pl.ds(pl.multiple_of(n * TILE, TILE), TILE)
            out[:, cols] = jnp.dot(block[...], wf[:, cols], preferred_element_type=F32) + hb[:, cols]

    def weights(a, b, own):
        l = temper * lax.dot_general(a, b, NT, preferred_element_type=F32) + offset
        m = jnp.where(eye, -l, l) if own else l
        g = gain / (1.0 + jnp.exp(-m))
        if own:
            g = jnp.where(eye, -g, g)
        return m, g.astype(BF16)

    def softplus(m):
        return jnp.maximum(m, 0.0) + jnp.log1p(jnp.exp(-jnp.abs(m)))

    project(pool, ztxt)
    v, zr = normalize(ztxt[...])
    ztxt[...] = v
    zhat[...] = v.astype(BF16)

    _, g = weights(zhat[...], xhat[...], True)
    dz[...] = jnp.dot(g, xhat[...], preferred_element_type=F32)
    for i, k in enumerate((xk0, xk1, xk2)):
        @pl.when(outer)
        def _():
            wait_x(k, 0)
            wait_x(k, 1)

        xh = normalize(xbuf[k].astype(F32))[0].astype(BF16)
        _, g = weights(zhat[...], xh, False)
        dz[...] += jnp.dot(g, xh, preferred_element_type=F32)

    v = ztxt[...]
    d = dz[...]
    dzb[...] = (zr * (d - v * jnp.sum(v * d, axis=-1, keepdims=True))).astype(BF16)

    def term(n):
        m = chip(1 - yh if n < 4 else yh, ORDER[n % 4])
        t = jnp.dot(
            pt[pl.ds(pl.multiple_of(m * CHIP, 16), CHIP), :], dzb[...], preferred_element_type=F32
        )
        for o, u in enumerate((t[:SHARD].astype(BF16), t[SHARD:].astype(BF16))):
            t_a[o, n] = u[:, :SPLIT]
            t_b[o, n] = u[:, SPLIT:]
        copy(t_a.at[1 - c, n], r_a.at[n], t_s.at[0, n], t_r.at[0, n], sib).start()
        copy(t_b.at[1 - c, n], r_b.at[n], t_s.at[1, n], t_r.at[1, n], sib).start()

    def pair_a(n):
        copy(r_a.at[n], r_a.at[n], t_s.at[0, n], t_r.at[0, n], sib).wait_recv()
        return t_a[c, n].astype(F32) + r_a[n].astype(F32)

    def pair_b(n):
        copy(r_b.at[n], r_b.at[n], t_s.at[1, n], t_r.at[1, n], sib).wait_recv()
        return t_b[c, n].astype(F32) + r_b[n].astype(F32)

    g_sent = []

    def g_go(src, value, ident, dst, who):
        src[...] = value.astype(BF16)
        d = copy(src, dst, g_s.at[ident], g_r.at[ident], who)
        d.start()
        g_sent.append(d)

    def g_wait(ref, ident):
        copy(ref, ref, g_s.at[ident], g_r.at[ident], xp).wait_recv()
        return ref[...].astype(F32)

    def first_sends(g):
        n = 4 * g
        g_go(st_a.at[g, 0], pair_a(n), 6 * g, far_a.at[g], xp)
        g_go(st_b.at[g, 0], pair_b(n), 6 * g + 1, far_b.at[g], xm)
        g_go(st_b.at[g, 1], pair_b(n + 1), 6 * g + 2, near_b.at[g, 0], xp)
        g_go(st_a.at[g, 1], pair_a(n + 2), 6 * g + 3, near_a.at[g, 1], xm)

    def second_sends(g):
        n = 4 * g
        g_go(st_a.at[g, 2], pair_a(n + 1) + g_wait(far_a.at[g], 6 * g), 6 * g + 4, near_a.at[g, 0], xp)
        g_go(st_b.at[g, 2], pair_b(n + 2) + g_wait(far_b.at[g], 6 * g + 1), 6 * g + 5, near_b.at[g, 1], xm)

    def sums(g):
        n = 4 * g + 3
        a = pair_a(n) + g_wait(near_a.at[g, 0], 6 * g + 4) + g_wait(near_a.at[g, 1], 6 * g + 3)
        b = pair_b(n) + g_wait(near_b.at[g, 0], 6 * g + 2) + g_wait(near_b.at[g, 1], 6 * g + 5)
        return a, b

    def host(zh, add):
        m, g = weights(xg[...], zh, False)
        if add:
            gsum[...] += softplus(m)
            gdx[...] += jnp.dot(g, zh, preferred_element_type=F32)
        else:
            gsum[...] = softplus(m)
            gdx[...] = jnp.dot(g, zh, preferred_element_type=F32)

    def text(k):
        project(pbuf.at[k], dz)
        return normalize(dz[...])[0].astype(BF16)

    def own_text(zh):
        m, g = weights(xhat[...], zh, False)
        ssum[...] += softplus(m)
        dx[...] += jnp.dot(g, zh, preferred_element_type=F32)

    def back():
        @pl.loop(0, WIDTH // TILE)
        def _(n):
            cols = pl.ds(pl.multiple_of(n * TILE, TILE), TILE)
            pool_out[:, cols] = lax.dot_general(
                dzb[...], wf[cols, :], NT, preferred_element_type=F32
            ).astype(BF16)

        stores[2].start()

    gdx_up = copy(gdx_out, gdx_in, h_s.at[0], h_r.at[0], up)
    gdx_dn = copy(gdx_out, gdx_in, h_s.at[0], h_r.at[0], dn)
    gsum_up = copy(gsum_out, gsum_in, h_s.at[1], h_r.at[1], up)
    gsum_dn = copy(gsum_out, gsum_in, h_s.at[1], h_r.at[1], dn)

    for n in range(3):
        term(n)
    first_sends(0)
    for n in range(3, 7):
        term(n)

    m, g = weights(xhat[...], zhat[...], True)
    ssum[...] = softplus(m)
    dx[...] = jnp.dot(g, zhat[...], preferred_element_type=F32)

    @pl.when(j == 1)
    def _():
        wait_p(4, 0)
        wait_p(4, 1)
        wait_x(5, 0, whole=True)

    @pl.when(inner)
    def _():
        xg[...] = normalize(xbuf[9 - 4 * j].astype(F32))[0].astype(BF16)

    @pl.when(j == 1)
    def _():
        host(text(4), False)

    @pl.when(j == 2)
    def _():
        host(zhat[...], False)

    second_sends(0)
    first_sends(1)
    term(7)

    @pl.when(j == 2)
    def _():
        wait_p(1, 0)
        wait_p(1, 1)

    @pl.when(inner)
    def _():
        zh = text(1)
        own_text(zh)

        @pl.when(j == 2)
        def _():
            host(zh, True)

    second_sends(1)

    @pl.when(j == 1)
    def _():
        wait_p(3, 0)
        wait_p(3, 1)

    @pl.when(inner)
    def _():
        zh = text(3)
        own_text(zh)

        @pl.when(j == 1)
        def _():
            host(zh, True)

    a, b = sums(0)
    g_go(y_a, a, 12, pass_a, up2)
    g_go(y_b, b, 13, pass_b, dn2)

    @pl.when(inner)
    def _():
        wait_p(2, 0)
        wait_p(2, 1)
        zh = text(2)
        host(zh, True)
        gdx_out[...] = gdx[...].astype(BF16)
        gsum_out[...] = jnp.sum(gsum[...].T, axis=0, keepdims=True)

        @pl.when(j == 1)
        def _():
            gdx_dn.start()
            gsum_dn.start()

        @pl.when(j == 2)
        def _():
            gdx_up.start()
            gsum_up.start()

        own_text(zh)

    @pl.when(outer)
    def _():
        back()

    a, b = sums(1)
    head_out[:, :SPLIT] = a
    head_out[:, SPLIT:] = b

    onward = []
    for ref, ident, dst, who in ((pass_a, 12, in_a, up2), (pass_b, 13, in_b, dn2)):
        copy(ref, ref, g_s.at[ident], g_r.at[ident], xp).wait_recv()
        d = copy(ref, dst, g_s.at[ident + 2], g_r.at[ident + 2], who)
        d.start()
        onward.append(d)

    @pl.when(inner)
    def _():
        back()

    @pl.when(outer)
    def _():
        gdx_up.wait_recv()
        gsum_up.wait_recv()
        dx[...] += gdx_in[...].astype(F32)
        loss_out[...] = (jnp.sum(ssum[...].T, axis=0, keepdims=True) + gsum_in[...]) * (1.0 / ROWS)

    @pl.when(inner)
    def _():
        loss_out[...] = jnp.sum(ssum[...].T, axis=0, keepdims=True) * (1.0 / ROWS)

    stores[0].start()
    v = ximg[...]
    d = dx[...]
    img_out[...] = (xr * (d - v * jnp.sum(v * d, axis=-1, keepdims=True))).astype(BF16)
    stores[1].start()

    head_out[:, :SPLIT] += g_wait(in_a, 14)
    head_out[:, SPLIT:] += g_wait(in_b, 15)
    stores[3].start()

    w_swap.wait_send()
    for d in w_sent:
        d.wait_send()

    @pl.when(j == 3)
    def _():
        w_edge_up.wait_send()
        w_pass_dn.wait_send()

    @pl.when(j == 0)
    def _():
        w_edge_dn.wait_send()
        w_pass_up.wait_send()

    @pl.when(j <= 2)
    def _():
        for d in x_hop:
            d.wait_send()

    @pl.when(j >= 1)
    def _():
        for d in p_hop:
            d.wait_send()

    @pl.when(j == 0)
    def _():
        guest.wait_send()

    @pl.when(inner)
    def _():
        gdx_up.wait_send()
        gsum_up.wait_send()

    x_done(0, img)
    p_done(0, pool)
    for k in range(1, 4):
        x_done(k, xbuf.at[k])
        p_done(k, pbuf.at[k])
    x_done(4, xbuf.at[4])
    p_done(4, pbuf.at[4])
    for n in range(8):
        copy(t_a.at[1 - c, n], r_a.at[n], t_s.at[0, n], t_r.at[0, n], sib).wait_send()
        copy(t_b.at[1 - c, n], r_b.at[n], t_s.at[1, n], t_r.at[1, n], sib).wait_send()
    for d in g_sent + onward:
        d.wait_send()
    for d in stores:
        d.wait()


def finish(*refs):
    into, out = refs[12], refs[13]
    loads = [pltpu.make_async_copy(refs[i], refs[8 + i], into.at[i]) for i in range(4)]
    stores = [pltpu.make_async_copy(refs[8 + i], refs[4 + i], out.at[i]) for i in range(4)]
    for d in loads:
        d.start()
    for d, e in zip(loads, stores):
        d.wait()
        e.start()
    for e in stores:
        e.wait()


def per_device(images, pooled, head_weight, head_bias, log_scale, bias):
    smem = pl.BlockSpec(memory_space=pltpu.SMEM)
    hbm = pl.BlockSpec(memory_space=pltpu.HBM)
    block = (ROWS, WIDTH)
    slab = (SHARD, WIDTH)
    slab_a = (SHARD, SPLIT)
    slab_b = (SHARD, WIDTH - SPLIT)
    dma = pltpu.SemaphoreType.DMA
    results = (
        jax.ShapeDtypeStruct((1, ROWS), F32),
        jax.ShapeDtypeStruct(block, BF16),
        jax.ShapeDtypeStruct(block, BF16),
        jax.ShapeDtypeStruct(slab, F32),
    )
    made = pl.pallas_call(
        kernel,
        out_shape=results,
        in_specs=[hbm, hbm, hbm, hbm, smem, smem],
        out_specs=(hbm, hbm, hbm, hbm),
        scratch_shapes=[
            pltpu.VMEM(block, BF16),
            pltpu.VMEM(block, BF16),
            pltpu.VMEM(slab, BF16),
            pltpu.VMEM((1, WIDTH), F32),
            pltpu.VMEM((1, ROWS), F32),
            pltpu.VMEM(block, BF16),
            pltpu.VMEM(block, BF16),
            pltpu.VMEM(slab, F32),
            pltpu.VMEM(slab, BF16),
            pltpu.VMEM((WIDTH, WIDTH), BF16),
            pltpu.VMEM((6,) + block, BF16),
            pltpu.VMEM((5,) + block, BF16),
            pltpu.VMEM(block, BF16),
            pltpu.VMEM(block, F32),
            pltpu.VMEM(block, BF16),
            pltpu.VMEM(block, F32),
            pltpu.VMEM(block, F32),
            pltpu.VMEM(block, F32),
            pltpu.VMEM(block, BF16),
            pltpu.VMEM((WIDTH, ROWS), BF16),
            pltpu.VMEM((ROWS, ROWS), F32),
            pltpu.VMEM((2, 8) + slab_a, BF16),
            pltpu.VMEM((2, 8) + slab_b, BF16),
            pltpu.VMEM((8,) + slab_a, BF16),
            pltpu.VMEM((8,) + slab_b, BF16),
            pltpu.VMEM((2, 3) + slab_a, BF16),
            pltpu.VMEM((2, 3) + slab_b, BF16),
            pltpu.VMEM((2,) + slab_a, BF16),
            pltpu.VMEM((2,) + slab_b, BF16),
            pltpu.VMEM((2, 2) + slab_a, BF16),
            pltpu.VMEM((2, 2) + slab_b, BF16),
            pltpu.VMEM(slab_a, BF16),
            pltpu.VMEM(slab_b, BF16),
            pltpu.VMEM(slab_a, BF16),
            pltpu.VMEM(slab_b, BF16),
            pltpu.VMEM(slab_a, BF16),
            pltpu.VMEM(slab_b, BF16),
            pltpu.VMEM(block, BF16),
            pltpu.VMEM(block, F32),
            pltpu.VMEM((ROWS, ROWS), F32),
            pltpu.VMEM(block, BF16),
            pltpu.VMEM((1, ROWS), F32),
            pltpu.VMEM(block, BF16),
            pltpu.VMEM((1, ROWS), F32),
            dma((4,)), dma((4,)),
            dma((18,)), dma((18,)),
            dma((7, 2)), dma((6, 2)),
            dma((6, 2)), dma((5, 2)),
            dma((2, 8)), dma((2, 8)),
            dma((16,)), dma((16,)),
            dma((2,)), dma((2,)),
        ],
        compiler_params=pltpu.CompilerParams(
            collective_id=0, has_side_effects=True, vmem_limit_bytes=VMEM_GRANT
        ),
        cost_estimate=pl.CostEstimate(flops=4_000_000_000, bytes_accessed=6_000_000, transcendentals=300_000),
    )(images, pooled, head_weight, head_bias, log_scale, bias)
    loss, image_grad, pooled_grad, head_grad = pl.pallas_call(
        finish,
        out_shape=results,
        in_specs=[hbm] * 4,
        out_specs=(hbm,) * 4,
        scratch_shapes=[pltpu.VMEM(r.shape, r.dtype) for r in results] + [dma((4,)), dma((4,))],
        compiler_params=pltpu.CompilerParams(vmem_limit_bytes=VMEM_GRANT),
    )(*made)
    return loss.reshape(ROWS), image_grad, pooled_grad, head_grad


def solution(mesh):
    in_specs = (P(("dp", "fsdp"), None), P(("dp", "fsdp"), None), P("fsdp", None), P(), P(), P())
    out_specs = (
        P(("dp", "fsdp")),
        P(("dp", "fsdp"), None),
        P(("dp", "fsdp"), None),
        P(("dp", "fsdp"), None),
    )
    return jax.shard_map(
        per_device, mesh=mesh, in_specs=in_specs, out_specs=out_specs, check_vma=False
    )
```

time: 81.7 us -> 75.2 us (0.920)
  local copies, waits for them, and re-layouts: 6.2 us -> 0 us
    unnamed x10 -> x0, local copies, waits for them, and re-layouts: 5.5 us -> none
    pallas_call x1 -> x2, Pallas kernels: 73.3 us -> 73.1 us  [the longest x1 71.1 us: per_device(): pl.pallas_call(kernel, out_shape=results, in_specs=[hbm, hbm, hbm, hbm, s...]
where the time goes in v2:
time: 75.2 us; the launch traced here: 75 us
  Pallas kernels  73.1 us (97%)
  between operations  1.93 us (3%)
    pallas_call x1, Pallas kernels, per_device(): pl.pallas_call(kernel, out_shape=results, in_specs=[hbm, hbm, hbm, hbm, s...  71.1 us
    pallas_call x1, Pallas kernels, per_device(): pl.pallas_call(finish, out_shape=results, in_specs=[hbm] * 4, out_specs=(...  1.96 us

profile of v2, /device:TPU:24, one launch (start us, length us, event | category | flops | bytes accessed | tf_op | source)
XLA Modules:
  0.0 75.0 jit_solution(8547173783500506436)
XLA Ops:
  1.9 71.1 %shard_map.93 = (f32[1,128]{1,0:T(1,128)}, bf16[128,1152]{1,0:T(8,128)(2,1)}, bf16[128,1152]{1,0:T(8,128)(2,1)}, f32[72,1152]{1,0:T(8,128)}) custom-call(bf16[128,1152]{1,0:T(8,128)(2,1)} %img_hbm.1, bf16[128,1152]{1,0:T(8,128)(2,1)} %pool_hbm.1, bf16[72,1152]{1,0:T(8,128)(2,1)} %wsh_hbm.1, f32[1152]{0:T(1024)} %hb_hbm.1, f32[1]{0:T(128)S(6)} %copy.10.log_scale, ...), custom_call_target="tpu_custom_call" | custom-call | flops 4000000000 | bytes 6000000 | tf_op jit(solution)/shard_map/pallas_call | solution.py:657
  73.1 2.0 %shard_map.94 = (f32[1,128]{1,0:T(1,128)}, bf16[128,1152]{1,0:T(8,128)(2,1)}, bf16[128,1152]{1,0:T(8,128)(2,1)}, f32[72,1152]{1,0:T(8,128)}) custom-call(f32[1,128]{1,0:T(1,128)} %get-tuple-element.12.refs_0_, bf16[128,1152]{1,0:T(8,128)(2,1)} %get-tuple-element.13.refs_1_, bf16[128,1152]{1,0:T(8,128)(2,1)} %get-tuple-element.14.refs_2_, ...), custom_call_target="tpu_custom_call" | custom-call | tf_op jit(solution)/shard_map/pallas_call | solution.py:720

commit v3 on v2

--- a/solution.py
+++ b/solution.py
@@ -33,10 +33,10 @@
     img_hbm, pool_hbm, wsh_hbm, hb_hbm, log_scale, bias,
     loss_hbm, img_grad_hbm, pool_grad_hbm, head_grad_hbm,
     img, pool, wsh, hb, loss_out, img_out, pool_out, head_out,
-    wtmp, wf, xbuf, pbuf, xhat, ximg, zhat, ztxt, dz, dx, dzb, pt, ssum,
+    wtmp, wf, xbuf, pbuf, xb, zb, ximg, ztxt, u, dzb, pt,
     t_a, t_b, r_a, r_b, st_a, st_b, far_a, far_b, near_a, near_b,
     y_a, y_b, pass_a, pass_b, in_a, in_b,
-    xg, gdx, gsum, gdx_out, gsum_out, gdx_in, gsum_in,
+    gdx_out, gsum_out, gdx_in, gsum_in,
     l_s, o_s, w_s, w_r, x_s, x_r, p_s, p_r, t_s, t_r, g_s, g_r, h_s, h_r,
 ):
     loads = [
@@ -113,6 +113,12 @@
         dst = xbuf.at[k] if whole else part(xbuf.at[k], h)
         copy(dst, dst, x_s.at[k, h], x_r.at[k, h], up).wait_recv()
 
+    def quarter(k, q):
+        return xbuf.at[k, pl.ds(HALF // 2 * q, HALF // 2), :]
+
+    hop_in = [copy(quarter(4, q), quarter(4, q), x_s.at[5, q], x_r.at[4, q], zm) for q in range(4)]
+    hop_up = [copy(quarter(4, q), quarter(3, q), x_s.at[4, q], x_r.at[3, q // 2], up) for q in range(4)]
+
     def wait_p(k, h):
         dst = part(pbuf.at[k], h)
         copy(dst, dst, p_s.at[k, h], p_r.at[k, h], up).wait_recv()
@@ -148,7 +154,10 @@
 
     w_swap = copy(wsh, wtmp, w_s.at[0], w_r.at[0], sib)
     w_swap.start()
-    x_hop = [copy(part(img, h), part(xbuf.at[4], h), x_s.at[5, h], x_r.at[4, h], zm) for h in range(2)]
+    x_hop = [
+        copy(img.at[pl.ds(HALF // 2 * q, HALF // 2), :], quarter(4, q), x_s.at[5, q], x_r.at[4, q], zm)
+        for q in range(4)
+    ]
     p_hop = [copy(part(pool, h), part(pbuf.at[4], h), p_s.at[5, h], p_r.at[4, h], zp) for h in range(2)]
 
     @pl.when(j <= 2)
@@ -167,7 +176,7 @@
 
     v, xr = normalize(img[...].astype(F32))
     ximg[...] = v
-    xhat[...] = v.astype(BF16)
+    xb[0] = v.astype(BF16)
 
     def chip(h, off):
         return h * 4 + lax.rem(x + off, 4)
@@ -252,7 +261,9 @@
     for h in range(2):
         @pl.when(j <= 2)
         def _():
-            pass_x(4, h)
+            for q in (2 * h, 2 * h + 1):
+                hop_in[q].wait_recv()
+                hop_up[q].start()
 
         @pl.when(inner)
         def _():
@@ -318,6 +329,14 @@
     @pl.when(j == 2)
     def _():
         pass_p(3)
+
+    def ready(k):
+        xb[k] = normalize(xbuf[k].astype(F32))[0].astype(BF16)
+
+    @pl.when(inner)
+    def _():
+        for k in range(1, 4):
+            ready(k)
 
     for ident, m in (
         (11, chip(yh, 3)), (12, chip(yh, 1)), (13, chip(yh, 2)), (14, theirs),
@@ -326,47 +345,55 @@
         got = rows_of(m, 80 - 80 * c, PART)
         w_copy(got, got, ident, sib).wait_recv()
 
-    temper = jnp.exp(jnp.full((1, 128), log_scale[0], F32))
-    offset = jnp.full((1, 128), bias[0], F32)
+    temper = jnp.exp(jnp.full((1, 1), log_scale[0], F32))
+    offset = jnp.full((1, 1), bias[0], F32)
     gain = temper * (1.0 / ROWS)
-    eye = lax.broadcasted_iota(jnp.int32, (ROWS, ROWS), 0) == lax.broadcasted_iota(jnp.int32, (ROWS, ROWS), 1)
 
     def project(block, out):
-        @pl.loop(0, WIDTH // TILE)
-        def _(n):
-            cols = pl.ds(pl.multiple_of(n * TILE, TILE), TILE)
-            out[:, cols] = jnp.dot(block[...], wf[:, cols], preferred_element_type=F32) + hb[:, cols]
+        for start in range(0, WIDTH, 512):
+            cols = pl.ds(start, min(512, WIDTH - start))
+            out[:, cols] = jnp.dot(block, wf[:, cols], preferred_element_type=F32) + hb[:, cols]
 
     def weights(a, b, own):
         l = temper * lax.dot_general(a, b, NT, preferred_element_type=F32) + offset
-        m = jnp.where(eye, -l, l) if own else l
-        g = gain / (1.0 + jnp.exp(-m))
+        if own:
+            eye = lax.broadcasted_iota(jnp.int32, l.shape, 0) == lax.broadcasted_iota(jnp.int32, l.shape, 1)
+            l = jnp.where(eye, -l, l)
+        g = gain / (1.0 + jnp.exp(-l))
         if own:
             g = jnp.where(eye, -g, g)
-        return m, g.astype(BF16)
-
-    def softplus(m):
-        return jnp.maximum(m, 0.0) + jnp.log1p(jnp.exp(-jnp.abs(m)))
-
-    project(pool, ztxt)
+        return l, g.astype(BF16)
+
+    def losses(m):
+        e = jnp.maximum(m, 0.0) + jnp.log1p(jnp.exp(-jnp.abs(m)))
+        total = e[:, :ROWS]
+        for start in range(ROWS, m.shape[1], ROWS):
+            total = total + e[:, start:start + ROWS]
+        return jnp.sum(total.T, axis=0, keepdims=True)
+
+    def image_side(d, row):
+        loss_out[...] = row * (1.0 / ROWS)
+        stores[0].start()
+        v = ximg[...]
+        img_out[...] = (xr * (d - v * jnp.sum(v * d, axis=-1, keepdims=True))).astype(BF16)
+        stores[1].start()
+
+    project(pool[...], ztxt)
     v, zr = normalize(ztxt[...])
     ztxt[...] = v
-    zhat[...] = v.astype(BF16)
-
-    _, g = weights(zhat[...], xhat[...], True)
-    dz[...] = jnp.dot(g, xhat[...], preferred_element_type=F32)
-    for i, k in enumerate((xk0, xk1, xk2)):
-        @pl.when(outer)
-        def _():
+    zb[0] = v.astype(BF16)
+
+    @pl.when(outer)
+    def _():
+        for k in (xk0, xk1, xk2):
             wait_x(k, 0)
             wait_x(k, 1)
-
-        xh = normalize(xbuf[k].astype(F32))[0].astype(BF16)
-        _, g = weights(zhat[...], xh, False)
-        dz[...] += jnp.dot(g, xh, preferred_element_type=F32)
-
+            ready(k)
+
+    seen = xb[0:4].reshape(4 * ROWS, WIDTH)
+    _, g = weights(zb[0], seen, True)
+    d = jnp.dot(g, seen, preferred_element_type=F32)
     v = ztxt[...]
-    d = dz[...]
     dzb[...] = (zr * (d - v * jnp.sum(v * d, axis=-1, keepdims=True))).astype(BF16)
 
     def term(n):
@@ -418,24 +445,6 @@
         b = pair_b(n) + g_wait(near_b.at[g, 0], 6 * g + 2) + g_wait(near_b.at[g, 1], 6 * g + 5)
         return a, b
 
-    def host(zh, add):
-        m, g = weights(xg[...], zh, False)
-        if add:
-            gsum[...] += softplus(m)
-            gdx[...] += jnp.dot(g, zh, preferred_element_type=F32)
-        else:
-            gsum[...] = softplus(m)
-            gdx[...] = jnp.dot(g, zh, preferred_element_type=F32)
-
-    def text(k):
-        project(pbuf.at[k], dz)
-        return normalize(dz[...])[0].astype(BF16)
-
-    def own_text(zh):
-        m, g = weights(xhat[...], zh, False)
-        ssum[...] += softplus(m)
-        dx[...] += jnp.dot(g, zh, preferred_element_type=F32)
-
     def back():
         @pl.loop(0, WIDTH // TILE)
         def _(n):
@@ -454,93 +463,66 @@
     for n in range(3):
         term(n)
     first_sends(0)
-    for n in range(3, 7):
+    for n in range(3, 8):
         term(n)
-
-    m, g = weights(xhat[...], zhat[...], True)
-    ssum[...] = softplus(m)
-    dx[...] = jnp.dot(g, zhat[...], preferred_element_type=F32)
+    first_sends(1)
 
     @pl.when(j == 1)
     def _():
-        wait_p(4, 0)
-        wait_p(4, 1)
+        for h in range(2):
+            wait_p(4, h)
+            wait_p(3, h)
         wait_x(5, 0, whole=True)
-
-    @pl.when(inner)
-    def _():
-        xg[...] = normalize(xbuf[9 - 4 * j].astype(F32))[0].astype(BF16)
-
-    @pl.when(j == 1)
-    def _():
-        host(text(4), False)
+        ready(5)
 
     @pl.when(j == 2)
     def _():
-        host(zhat[...], False)
+        for h in range(2):
+            wait_p(1, h)
+
+    @pl.when(inner)
+    def _():
+        for h in range(2):
+            wait_p(2, h)
+        project(pbuf[1:5].reshape(4 * ROWS, WIDTH), u)
 
     second_sends(0)
-    first_sends(1)
-    term(7)
-
-    @pl.when(j == 2)
-    def _():
-        wait_p(1, 0)
-        wait_p(1, 1)
-
-    @pl.when(inner)
-    def _():
-        zh = text(1)
-        own_text(zh)
+
+    @pl.when(inner)
+    def _():
+        @pl.loop(1, 5)
+        def _(k):
+            zb[k] = normalize(u[pl.ds(pl.multiple_of((k - 1) * ROWS, ROWS), ROWS), :])[0].astype(BF16)
+
+        hosted = zb[pl.ds(4 - 2 * j, 3)].reshape(3 * ROWS, WIDTH)
+        m, g = weights(xb[9 - 4 * j], hosted, False)
+        gdx_out[...] = jnp.dot(g, hosted, preferred_element_type=F32).astype(BF16)
+        gsum_out[...] = losses(m)
+
+        @pl.when(j == 1)
+        def _():
+            gdx_dn.start()
+            gsum_dn.start()
 
         @pl.when(j == 2)
         def _():
-            host(zh, True)
-
-    second_sends(1)
-
-    @pl.when(j == 1)
-    def _():
-        wait_p(3, 0)
-        wait_p(3, 1)
-
-    @pl.when(inner)
-    def _():
-        zh = text(3)
-        own_text(zh)
-
-        @pl.when(j == 1)
-        def _():
-            host(zh, True)
+            gdx_up.start()
+            gsum_up.start()
+
+    @pl.when(outer)
+    def _():
+        back()
 
     a, b = sums(0)
     g_go(y_a, a, 12, pass_a, up2)
     g_go(y_b, b, 13, pass_b, dn2)
-
-    @pl.when(inner)
-    def _():
-        wait_p(2, 0)
-        wait_p(2, 1)
-        zh = text(2)
-        host(zh, True)
-        gdx_out[...] = gdx[...].astype(BF16)
-        gsum_out[...] = jnp.sum(gsum[...].T, axis=0, keepdims=True)
-
-        @pl.when(j == 1)
-        def _():
-            gdx_dn.start()
-            gsum_dn.start()
-
-        @pl.when(j == 2)
-        def _():
-            gdx_up.start()
-            gsum_up.start()
-
-        own_text(zh)
-
-    @pl.when(outer)
-    def _():
-        back()
+    second_sends(1)
+
+    @pl.when(inner)
+    def _():
+        texts = zb[0:4].reshape(4 * ROWS, WIDTH)
+        m, g = weights(xb[0], texts, True)
+        image_side(jnp.dot(g, texts, preferred_element_type=F32), losses(m))
 
     a, b = sums(1)
     head_out[:, :SPLIT] = a
@@ -559,20 +541,12 @@
 
     @pl.when(outer)
     def _():
+        m, g = weights(xb[0], zb[0], True)
+        row = losses(m)
+        d = jnp.dot(g, zb[0], preferred_element_type=F32)
+        gsum_up.wait_recv()
         gdx_up.wait_recv()
-        gsum_up.wait_recv()
-        dx[...] += gdx_in[...].astype(F32)
-        loss_out[...] = (jnp.sum(ssum[...].T, axis=0, keepdims=True) + gsum_in[...]) * (1.0 / ROWS)
-
-    @pl.when(inner)
-    def _():
-        loss_out[...] = jnp.sum(ssum[...].T, axis=0, keepdims=True) * (1.0 / ROWS)
-
-    stores[0].start()
-    v = ximg[...]
-    d = dx[...]
-    img_out[...] = (xr * (d - v * jnp.sum(v * d, axis=-1, keepdims=True))).astype(BF16)
-    stores[1].start()
+        image_side(d + gdx_in[...].astype(F32), row + gsum_in[...])
 
     head_out[:, :SPLIT] += g_wait(in_a, 14)
     head_out[:, SPLIT:] += g_wait(in_b, 15)
@@ -594,7 +568,7 @@
 
     @pl.when(j <= 2)
     def _():
-        for d in x_hop:
+        for d in x_hop + hop_up:
             d.wait_send()
 
     @pl.when(j >= 1)
@@ -616,7 +590,6 @@
     for k in range(1, 4):
         x_done(k, xbuf.at[k])
         p_done(k, pbuf.at[k])
-    x_done(4, xbuf.at[4])
     p_done(4, pbuf.at[4])
     for n in range(8):
         copy(t_a.at[1 - c, n], r_a.at[n], t_s.at[0, n], t_r.at[0, n], sib).wait_send()
@@ -672,15 +645,13 @@
             pltpu.VMEM((WIDTH, WIDTH), BF16),
             pltpu.VMEM((6,) + block, BF16),
             pltpu.VMEM((5,) + block, BF16),
-            pltpu.VMEM(block, BF16),
-            pltpu.VMEM(block, F32),
-            pltpu.VMEM(block, BF16),
+            pltpu.VMEM((6,) + block, BF16),
+            pltpu.VMEM((5,) + block, BF16),
             pltpu.VMEM(block, F32),
             pltpu.VMEM(block, F32),
-            pltpu.VMEM(block, F32),
+            pltpu.VMEM((4 * ROWS, WIDTH), F32),
             pltpu.VMEM(block, BF16),
             pltpu.VMEM((WIDTH, ROWS), BF16),
-            pltpu.VMEM((ROWS, ROWS), F32),
             pltpu.VMEM((2, 8) + slab_a, BF16),
             pltpu.VMEM((2, 8) + slab_b, BF16),
             pltpu.VMEM((8,) + slab_a, BF16),
@@ -698,15 +669,12 @@
             pltpu.VMEM(slab_a, BF16),
             pltpu.VMEM(slab_b, BF16),
             pltpu.VMEM(block, BF16),
-            pltpu.VMEM(block, F32),
-            pltpu.VMEM((ROWS, ROWS), F32),
-            pltpu.VMEM(block, BF16),
             pltpu.VMEM((1, ROWS), F32),
             pltpu.VMEM(block, BF16),
             pltpu.VMEM((1, ROWS), F32),
             dma((4,)), dma((4,)),
             dma((18,)), dma((18,)),
-            dma((7, 2)), dma((6, 2)),
+            dma((7, 4)), dma((6, 4)),
             dma((6, 2)), dma((5, 2)),
             dma((2, 8)), dma((2, 8)),
             dma((16,)), dma((16,)),

time: 75.2 us -> 74.5 us (level)
  the two profiles are of different devices: /device:TPU:24 before, /device:TPU:8 now
where the time goes in v3:
time: 74.5 us; the launch traced here: 74.3 us
  Pallas kernels  72.4 us (97%)
  between operations  1.93 us (3%)
    pallas_call x1, Pallas kernels, per_device(): pl.pallas_call(kernel, out_shape=results, in_specs=[hbm, hbm, hbm, hbm, s...  70.4 us
    pallas_call x1, Pallas kernels, per_device(): pl.pallas_call(finish, out_shape=results, in_specs=[hbm] * 4, out_specs=(...  1.96 us

profile of v3, /device:TPU:8, one launch (start us, length us, event | category | flops | bytes accessed | tf_op | source)
XLA Modules:
  0.0 74.3 jit_solution(7455721902983754089)
XLA Ops:
  1.9 70.4 %shard_map.93 = (f32[1,128]{1,0:T(1,128)}, bf16[128,1152]{1,0:T(8,128)(2,1)}, bf16[128,1152]{1,0:T(8,128)(2,1)}, f32[72,1152]{1,0:T(8,128)}) custom-call(bf16[128,1152]{1,0:T(8,128)(2,1)} %img_hbm.1, bf16[128,1152]{1,0:T(8,128)(2,1)} %pool_hbm.1, bf16[72,1152]{1,0:T(8,128)(2,1)} %wsh_hbm.1, f32[1152]{0:T(1024)} %hb_hbm.1, f32[1]{0:T(128)S(6)} %copy.10.log_scale, ...), custom_call_target="tpu_custom_call" | custom-call | flops 4000000000 | bytes 6000000 | tf_op jit(solution)/shard_map/pallas_call | solution.py:630
  72.4 2.0 %shard_map.94 = (f32[1,128]{1,0:T(1,128)}, bf16[128,1152]{1,0:T(8,128)(2,1)}, bf16[128,1152]{1,0:T(8,128)(2,1)}, f32[72,1152]{1,0:T(8,128)}) custom-call(f32[1,128]{1,0:T(1,128)} %get-tuple-element.12.refs_0_, bf16[128,1152]{1,0:T(8,128)(2,1)} %get-tuple-element.13.refs_1_, bf16[128,1152]{1,0:T(8,128)(2,1)} %get-tuple-element.14.refs_2_, ...), custom_call_target="tpu_custom_call" | custom-call | tf_op jit(solution)/shard_map/pallas_call | solution.py:688

commit v4 on v3

--- a/solution.py
+++ b/solution.py
@@ -167,7 +167,10 @@
 
     send_x(0, img, 0)
     send_x(0, img, 1)
-    send_p(0, pool, 0)
+
+    @pl.when(j == 1)
+    def _():
+        send_p(0, pool, 0)
 
     @pl.when(j >= 1)
     def _():
@@ -184,8 +187,8 @@
     def rows_of(m, start, size):
         return wf.at[pl.ds(pl.multiple_of(m * CHIP + start, 16), size), :]
 
-    def unit(m):
-        return rows_of(m, 64 * c, UNIT)
+    def piece(m, p):
+        return rows_of(m, 64 * c, AHEAD) if p == 0 else rows_of(m, 64 * c + AHEAD, UNIT - AHEAD)
 
     def w_copy(src, dst, ident, who, send=None):
         return copy(src, dst, w_s.at[ident if send is None else send], w_r.at[ident], who)
@@ -207,58 +210,93 @@
         [jnp.where(first, own_rows, sib_rows), jnp.where(first, sib_rows, own_rows)], axis=0
     ).astype(BF16)
 
-    w_edge_up = w_copy(unit(mine), unit(mine), 9, up)
-    w_edge_dn = w_copy(unit(mine), unit(mine), 9, dn)
-    w_pass_up = w_copy(unit(theirs), unit(theirs), 9, up, 10)
-    w_pass_dn = w_copy(unit(theirs), unit(theirs), 9, dn, 10)
+    edge_up = [w_copy(piece(mine, p), piece(mine, p), 13 + p, up) for p in range(2)]
+    edge_dn = [w_copy(piece(mine, p), piece(mine, p), 13 + p, dn) for p in range(2)]
+    pass_up = [w_copy(piece(theirs, p), piece(theirs, p), 13 + p, up, 15 + p) for p in range(2)]
+    pass_dn = [w_copy(piece(theirs, p), piece(theirs, p), 13 + p, dn, 15 + p) for p in range(2)]
 
     @pl.when(j == 3)
     def _():
-        w_edge_up.start()
+        for d in edge_up:
+            d.start()
 
     @pl.when(j == 0)
     def _():
-        w_edge_dn.start()
-
-    w_go(unit(mine), 1, xp)
-    w_go(unit(mine), 2, xm)
+        for d in edge_dn:
+            d.start()
+
+    def along_x(r, m):
+        return {
+            (d, p): w_copy(piece(m, p), piece(m, p), 1 + 4 * r + 2 * d + p, xp if d == 0 else xm)
+            for d in range(2)
+            for p in range(2)
+        }
+
+    mine_x = along_x(0, mine)
+    theirs_x = along_x(1, theirs)
+    for key in ((0, 0), (1, 1), (0, 1), (1, 0)):
+        mine_x[key].start()
+    w_sent.extend(mine_x.values())
+    w_sent.extend(theirs_x.values())
 
     pt[...] = pool[...].astype(F32).T.astype(BF16)
 
     def to_sibling(m, ident):
         w_go(rows_of(m, 80 * c, PART), ident, sib)
 
-    def near_units(r, h):
+    def near_first(r, h):
         for d, (off, onward) in enumerate(((3, xp), (1, xm))):
+            got = piece(chip(h, off), d)
+            w_copy(got, got, 1 + 4 * r + 3 * d, xp).wait_recv()
+            w_go(got, 9 + 2 * r + d, onward)
+
+    def near_rest(r, h):
+        for d, off in enumerate((3, 1)):
             m = chip(h, off)
-            w_copy(unit(m), unit(m), 1 + 2 * r + d, xp).wait_recv()
-            if d == 0:
-                w_go(rows_of(m, 64 * c, AHEAD), 5 + 2 * r, onward)
-            else:
-                w_go(rows_of(m, 64 * c + AHEAD, UNIT - AHEAD), 6 + 2 * r, onward)
-            to_sibling(m, 11 + 4 * r + d)
+            got = piece(m, 1 - d)
+            w_copy(got, got, 2 + 4 * r + d, xp).wait_recv()
+            to_sibling(m, 17 + 4 * r + d)
 
     def far_units(r, h):
         m = chip(h, 2)
-        part = rows_of(m, 64 * c, AHEAD)
-        w_copy(part, part, 5 + 2 * r, xp).wait_recv()
-        part = rows_of(m, 64 * c + AHEAD, UNIT - AHEAD)
-        w_copy(part, part, 6 + 2 * r, xp).wait_recv()
-        to_sibling(m, 13 + 4 * r)
-
-    other = w_copy(unit(theirs), unit(theirs), 9, xp)
-    theirs_xp = w_copy(unit(theirs), unit(theirs), 3, xp)
-    theirs_xm = w_copy(unit(theirs), unit(theirs), 4, xm)
+        for p in range(2):
+            w_copy(piece(m, p), piece(m, p), 9 + 2 * r + p, xp).wait_recv()
+        to_sibling(m, 19 + 4 * r)
+
+    edge_in = [w_copy(piece(theirs, p), piece(theirs, p), 13 + p, xp) for p in range(2)]
     theirs_part = rows_of(theirs, 80 * c, PART)
-    theirs_sib = w_copy(theirs_part, theirs_part, 14, sib)
-    w_sent.extend((theirs_xp, theirs_xm, theirs_sib))
-
-    def send_theirs():
-        theirs_xp.start()
-        theirs_xm.start()
+    theirs_sib = w_copy(theirs_part, theirs_part, 20, sib)
+    w_sent.append(theirs_sib)
+
+    def theirs_first():
+        edge_in[0].wait_recv()
+
+        @pl.when(j == 0)
+        def _():
+            pass_up[0].start()
+
+        @pl.when(j == 3)
+        def _():
+            pass_dn[0].start()
+
+        theirs_x[0, 0].start()
+
+    def theirs_rest():
+        edge_in[1].wait_recv()
+
+        @pl.when(j == 0)
+        def _():
+            pass_up[1].start()
+
+        @pl.when(j == 3)
+        def _():
+            pass_dn[1].start()
+
+        for key in ((1, 1), (0, 1), (1, 0)):
+            theirs_x[key].start()
         theirs_sib.start()
 
-    for h in range(2):
+    def hop_on(h):
         @pl.when(j <= 2)
         def _():
             for q in (2 * h, 2 * h + 1):
@@ -269,30 +307,24 @@
         def _():
             pass_x(1, h)
 
-    near_units(0, yh)
+    hop_on(0)
 
     @pl.when(outer)
     def _():
-        other.wait_recv()
+        theirs_first()
+
+    near_first(0, yh)
+
+    @pl.when(outer)
+    def _():
+        theirs_rest()
+
+    hop_on(1)
+    near_rest(0, yh)
 
     @pl.when(j == 0)
     def _():
-        w_pass_up.start()
-
-    @pl.when(j == 3)
-    def _():
-        w_pass_dn.start()
-
-    @pl.when(outer)
-    def _():
-        send_theirs()
-
-    @pl.when(inner)
-    def _():
-        pass_x(3, 0)
-
-    @pl.when(j == 0)
-    def _():
+        send_p(0, pool, 0)
         send_p(0, pool, 1)
         guest.start()
 
@@ -300,20 +332,26 @@
     def _():
         pass_p(4)
 
+    @pl.when(inner)
+    def _():
+        pass_x(3, 0)
+        theirs_first()
+
     far_units(0, yh)
 
     @pl.when(inner)
     def _():
         pass_x(3, 1)
-        other.wait_recv()
-        send_theirs()
+        theirs_rest()
         pass_x(2, 0)
 
-    near_units(1, 1 - yh)
+    near_first(1, 1 - yh)
 
     @pl.when(inner)
     def _():
         pass_x(2, 1)
+
+    near_rest(1, 1 - yh)
 
     @pl.when(j == 1)
     def _():
@@ -339,8 +377,8 @@
             ready(k)
 
     for ident, m in (
-        (11, chip(yh, 3)), (12, chip(yh, 1)), (13, chip(yh, 2)), (14, theirs),
-        (15, chip(1 - yh, 3)), (16, chip(1 - yh, 1)), (17, chip(1 - yh, 2)),
+        (17, chip(yh, 3)), (18, chip(yh, 1)), (19, chip(yh, 2)), (20, theirs),
+        (21, chip(1 - yh, 3)), (22, chip(1 - yh, 1)), (23, chip(1 - yh, 2)),
     ):
         got = rows_of(m, 80 - 80 * c, PART)
         w_copy(got, got, ident, sib).wait_recv()
@@ -558,13 +596,13 @@
 
     @pl.when(j == 3)
     def _():
-        w_edge_up.wait_send()
-        w_pass_dn.wait_send()
+        for d in edge_up + pass_dn:
+            d.wait_send()
 
     @pl.when(j == 0)
     def _():
-        w_edge_dn.wait_send()
-        w_pass_up.wait_send()
+        for d in edge_dn + pass_up:
+            d.wait_send()
 
     @pl.when(j <= 2)
     def _():
@@ -673,7 +711,7 @@
             pltpu.VMEM(block, BF16),
             pltpu.VMEM((1, ROWS), F32),
             dma((4,)), dma((4,)),
-            dma((18,)), dma((18,)),
+            dma((24,)), dma((24,)),
             dma((7, 4)), dma((6, 4)),
             dma((6, 2)), dma((5, 2)),
             dma((2, 8)), dma((2, 8)),

time: 74.5 us -> 73 us (0.980)
  Pallas kernels: 72.4 us -> 70.9 us
    pallas_call x1, Pallas kernels: 70.4 us -> 69 us  [per_device(): pl.pallas_call(kernel, out_shape=results, in_specs=[hbm, hbm, hbm, hbm, s...]
where the time goes in v4:
time: 73 us; the launch traced here: 72.8 us
  Pallas kernels  70.9 us (97%)
  between operations  1.93 us (3%)
    pallas_call x1, Pallas kernels, per_device(): pl.pallas_call(kernel, out_shape=results, in_specs=[hbm, hbm, hbm, hbm, s...  69 us
    pallas_call x1, Pallas kernels, per_device(): pl.pallas_call(finish, out_shape=results, in_specs=[hbm] * 4, out_specs=(...  1.96 us

profile of v4, /device:TPU:8, one launch (start us, length us, event | category | flops | bytes accessed | tf_op | source)
XLA Modules:
  0.0 72.8 jit_solution(16905241719219847131)
XLA Ops:
  1.9 69.0 %shard_map.93 = (f32[1,128]{1,0:T(1,128)}, bf16[128,1152]{1,0:T(8,128)(2,1)}, bf16[128,1152]{1,0:T(8,128)(2,1)}, f32[72,1152]{1,0:T(8,128)}) custom-call(bf16[128,1152]{1,0:T(8,128)(2,1)} %img_hbm.1, bf16[128,1152]{1,0:T(8,128)(2,1)} %pool_hbm.1, bf16[72,1152]{1,0:T(8,128)(2,1)} %wsh_hbm.1, f32[1152]{0:T(1024)} %hb_hbm.1, f32[1]{0:T(128)S(6)} %copy.10.log_scale, ...), custom_call_target="tpu_custom_call" | custom-call | flops 4000000000 | bytes 6000000 | tf_op jit(solution)/shard_map/pallas_call | solution.py:668
  70.9 2.0 %shard_map.94 = (f32[1,128]{1,0:T(1,128)}, bf16[128,1152]{1,0:T(8,128)(2,1)}, bf16[128,1152]{1,0:T(8,128)(2,1)}, f32[72,1152]{1,0:T(8,128)}) custom-call(f32[1,128]{1,0:T(1,128)} %get-tuple-element.12.refs_0_, bf16[128,1152]{1,0:T(8,128)(2,1)} %get-tuple-element.13.refs_1_, bf16[128,1152]{1,0:T(8,128)(2,1)} %get-tuple-element.14.refs_2_, ...), custom_call_target="tpu_custom_call" | custom-call | tf_op jit(solution)/shard_map/pallas_call | solution.py:726

commit v5 on v4

--- a/solution.py
+++ b/solution.py
@@ -33,11 +33,11 @@
     img_hbm, pool_hbm, wsh_hbm, hb_hbm, log_scale, bias,
     loss_hbm, img_grad_hbm, pool_grad_hbm, head_grad_hbm,
     img, pool, wsh, hb, loss_out, img_out, pool_out, head_out,
-    wtmp, wf, xbuf, pbuf, xb, zb, ximg, ztxt, u, dzb, pt,
-    t_a, t_b, r_a, r_b, st_a, st_b, far_a, far_b, near_a, near_b,
+    wtmp, wf, xbuf, pbuf, xb, zb, ximg, ztxt, u, dzb, psib, ptf, pt, terms,
+    st_a, st_b, far_a, far_b, near_a, near_b,
     y_a, y_b, pass_a, pass_b, in_a, in_b,
     gdx_out, gsum_out, gdx_in, gsum_in,
-    l_s, o_s, w_s, w_r, x_s, x_r, p_s, p_r, t_s, t_r, g_s, g_r, h_s, h_r,
+    l_s, o_s, w_s, w_r, x_s, x_r, p_s, p_r, g_s, g_r, h_s, h_r,
 ):
     loads = [
         pltpu.make_async_copy(src, dst, l_s.at[i])
@@ -154,6 +154,7 @@
 
     w_swap = copy(wsh, wtmp, w_s.at[0], w_r.at[0], sib)
     w_swap.start()
+    pool_swap = copy(pool, psib, h_s.at[2], h_r.at[2], sib)
     x_hop = [
         copy(img.at[pl.ds(HALF // 2 * q, HALF // 2), :], quarter(4, q), x_s.at[5, q], x_r.at[4, q], zm)
         for q in range(4)
@@ -238,8 +239,18 @@
         mine_x[key].start()
     w_sent.extend(mine_x.values())
     w_sent.extend(theirs_x.values())
-
-    pt[...] = pool[...].astype(F32).T.astype(BF16)
+    pool_swap.start()
+
+    def slab_rows(n):
+        m = chip(1 - yh if n < 4 else yh, ORDER[n % 4])
+        return ptf[pl.ds(pl.multiple_of(m * CHIP + SHARD * c, 8), SHARD), :]
+
+    def transpose_into(ref, start):
+        ptf[...] = ref[...].astype(F32).T
+        for n in range(0, 8, 2):
+            pt[SHARD * n:SHARD * (n + 2), start:start + ROWS] = jnp.concatenate(
+                [slab_rows(n), slab_rows(n + 1)], axis=0
+            ).astype(BF16)
 
     def to_sibling(m, ident):
         w_go(rows_of(m, 80 * c, PART), ident, sib)
@@ -308,6 +319,7 @@
             pass_x(1, h)
 
     hop_on(0)
+    transpose_into(pool, 0)
 
     @pl.when(outer)
     def _():
@@ -321,6 +333,8 @@
 
     hop_on(1)
     near_rest(0, yh)
+    pool_swap.wait_recv()
+    transpose_into(psib, ROWS)
 
     @pl.when(j == 0)
     def _():
@@ -421,37 +435,43 @@
     ztxt[...] = v
     zb[0] = v.astype(BF16)
 
+    def text_grad(a, own):
+        _, g = weights(zb[0], a, own)
+        return jnp.dot(g, a, preferred_element_type=F32)
+
+    def text_side(d):
+        v = ztxt[...]
+        dzb[:ROWS] = (zr * (d - v * jnp.sum(v * d, axis=-1, keepdims=True))).astype(BF16)
+
+    @pl.when(inner)
+    def _():
+        text_side(text_grad(xb[0:4].reshape(4 * ROWS, WIDTH), True))
+
     @pl.when(outer)
     def _():
-        for k in (xk0, xk1, xk2):
+        for k in (xk0, xk1):
             wait_x(k, 0)
             wait_x(k, 1)
             ready(k)
-
-    seen = xb[0:4].reshape(4 * ROWS, WIDTH)
-    _, g = weights(zb[0], seen, True)
-    d = jnp.dot(g, seen, preferred_element_type=F32)
-    v = ztxt[...]
-    dzb[...] = (zr * (d - v * jnp.sum(v * d, axis=-1, keepdims=True))).astype(BF16)
-
-    def term(n):
-        m = chip(1 - yh if n < 4 else yh, ORDER[n % 4])
-        t = jnp.dot(
-            pt[pl.ds(pl.multiple_of(m * CHIP, 16), CHIP), :], dzb[...], preferred_element_type=F32
-        )
-        for o, u in enumerate((t[:SHARD].astype(BF16), t[SHARD:].astype(BF16))):
-            t_a[o, n] = u[:, :SPLIT]
-            t_b[o, n] = u[:, SPLIT:]
-        copy(t_a.at[1 - c, n], r_a.at[n], t_s.at[0, n], t_r.at[0, n], sib).start()
-        copy(t_b.at[1 - c, n], r_b.at[n], t_s.at[1, n], t_r.at[1, n], sib).start()
+        u[:ROWS] = text_grad(xb[0], True) + text_grad(xb[xk0], False) + text_grad(xb[xk1], False)
+        wait_x(xk2, 0)
+        wait_x(xk2, 1)
+        ready(xk2)
+        text_side(u[:ROWS] + text_grad(xb[xk2], False))
+
+    pair = copy(dzb.at[:ROWS], dzb.at[ROWS:], h_s.at[3], h_r.at[3], sib)
+    pair.start()
+
+    def make(n):
+        t = jnp.dot(pt[SHARD * n:SHARD * (n + 2), :], dzb[...], preferred_element_type=F32)
+        terms[n] = t[:SHARD]
+        terms[n + 1] = t[SHARD:]
 
     def pair_a(n):
-        copy(r_a.at[n], r_a.at[n], t_s.at[0, n], t_r.at[0, n], sib).wait_recv()
-        return t_a[c, n].astype(F32) + r_a[n].astype(F32)
+        return terms[n, :, :SPLIT]
 
     def pair_b(n):
-        copy(r_b.at[n], r_b.at[n], t_s.at[1, n], t_r.at[1, n], sib).wait_recv()
-        return t_b[c, n].astype(F32) + r_b[n].astype(F32)
+        return terms[n, :, SPLIT:]
 
     g_sent = []
 
@@ -488,7 +508,7 @@
         def _(n):
             cols = pl.ds(pl.multiple_of(n * TILE, TILE), TILE)
             pool_out[:, cols] = lax.dot_general(
-                dzb[...], wf[cols, :], NT, preferred_element_type=F32
+                dzb[:ROWS], wf[cols, :], NT, preferred_element_type=F32
             ).astype(BF16)
 
         stores[2].start()
@@ -498,11 +518,24 @@
     gsum_up = copy(gsum_out, gsum_in, h_s.at[1], h_r.at[1], up)
     gsum_dn = copy(gsum_out, gsum_in, h_s.at[1], h_r.at[1], dn)
 
-    for n in range(3):
-        term(n)
+    @pl.when(outer)
+    def _():
+        m, g = weights(xb[0], zb[0], True)
+        u[ROWS:2 * ROWS] = jnp.dot(g, zb[0], preferred_element_type=F32)
+        loss_out[...] = losses(m)
+
+    pair.wait_recv()
+    make(0)
+    make(2)
     first_sends(0)
-    for n in range(3, 8):
-        term(n)
+    make(4)
+    make(6)
+
+    @pl.when(outer)
+    def _():
+        back()
+
+    second_sends(0)
     first_sends(1)
 
     @pl.when(j == 1)
@@ -524,7 +557,25 @@
             wait_p(2, h)
         project(pbuf[1:5].reshape(4 * ROWS, WIDTH), u)
 
-    second_sends(0)
+    a, b = sums(0)
+    g_go(y_a, a, 12, pass_a, up2)
+    g_go(y_b, b, 13, pass_b, dn2)
+
+    onward = [
+        copy(pass_a, in_a, g_s.at[14], g_r.at[14], up2),
+        copy(pass_b, in_b, g_s.at[15], g_r.at[15], dn2),
+    ]
+
+    def relay():
+        for ref, ident, d in ((pass_a, 12, onward[0]), (pass_b, 13, onward[1])):
+            copy(ref, ref, g_s.at[ident], g_r.at[ident], xp).wait_recv()
+            d.start()
+
+    @pl.when(outer)
+    def _():
+        relay()
+
+    second_sends(1)
 
     @pl.when(inner)
     def _():
@@ -547,44 +598,24 @@
             gdx_up.start()
             gsum_up.start()
 
-    @pl.when(outer)
-    def _():
-        back()
-
-    a, b = sums(0)
-    g_go(y_a, a, 12, pass_a, up2)
-    g_go(y_b, b, 13, pass_b, dn2)
-    second_sends(1)
-
-    @pl.when(inner)
-    def _():
         texts = zb[0:4].reshape(4 * ROWS, WIDTH)
         m, g = weights(xb[0], texts, True)
         image_side(jnp.dot(g, texts, preferred_element_type=F32), losses(m))
+        back()
 
     a, b = sums(1)
     head_out[:, :SPLIT] = a
     head_out[:, SPLIT:] = b
 
-    onward = []
-    for ref, ident, dst, who in ((pass_a, 12, in_a, up2), (pass_b, 13, in_b, dn2)):
-        copy(ref, ref, g_s.at[ident], g_r.at[ident], xp).wait_recv()
-        d = copy(ref, dst, g_s.at[ident + 2], g_r.at[ident + 2], who)
-        d.start()
-        onward.append(d)
-
-    @pl.when(inner)
-    def _():
-        back()
+    @pl.when(inner)
+    def _():
+        relay()
 
     @pl.when(outer)
     def _():
-        m, g = weights(xb[0], zb[0], True)
-        row = losses(m)
-        d = jnp.dot(g, zb[0], preferred_element_type=F32)
         gsum_up.wait_recv()
         gdx_up.wait_recv()
-        image_side(d + gdx_in[...].astype(F32), row + gsum_in[...])
+        image_side(u[ROWS:2 * ROWS] + gdx_in[...].astype(F32), loss_out[...] + gsum_in[...])
 
     head_out[:, :SPLIT] += g_wait(in_a, 14)
     head_out[:, SPLIT:] += g_wait(in_b, 15)
@@ -629,9 +660,8 @@
         x_done(k, xbuf.at[k])
         p_done(k, pbuf.at[k])
     p_done(4, pbuf.at[4])
-    for n in range(8):
-        copy(t_a.at[1 - c, n], r_a.at[n], t_s.at[0, n], t_r.at[0, n], sib).wait_send()
-        copy(t_b.at[1 - c, n], r_b.at[n], t_s.at[1, n], t_r.at[1, n], sib).wait_send()
+    pool_swap.wait_send()
+    pair.wait_send()
     for d in g_sent + onward:
         d.wait_send()
     for d in stores:
@@ -688,12 +718,11 @@
             pltpu.VMEM(block, F32),
             pltpu.VMEM(block, F32),
             pltpu.VMEM((4 * ROWS, WIDTH), F32),
+            pltpu.VMEM((2 * ROWS, WIDTH), BF16),
             pltpu.VMEM(block, BF16),
-            pltpu.VMEM((WIDTH, ROWS), BF16),
-            pltpu.VMEM((2, 8) + slab_a, BF16),
-            pltpu.VMEM((2, 8) + slab_b, BF16),
-            pltpu.VMEM((8,) + slab_a, BF16),
-            pltpu.VMEM((8,) + slab_b, BF16),
+            pltpu.VMEM((WIDTH, ROWS), F32),
+            pltpu.VMEM((8 * SHARD, 2 * ROWS), BF16),
+            pltpu.VMEM((8,) + slab, F32),
             pltpu.VMEM((2, 3) + slab_a, BF16),
             pltpu.VMEM((2, 3) + slab_b, BF16),
             pltpu.VMEM((2,) + slab_a, BF16),
@@ -714,9 +743,8 @@
             dma((24,)), dma((24,)),
             dma((7, 4)), dma((6, 4)),
             dma((6, 2)), dma((5, 2)),
-            dma((2, 8)), dma((2, 8)),
             dma((16,)), dma((16,)),
-            dma((2,)), dma((2,)),
+            dma((4,)), dma((4,)),
         ],
         compiler_params=pltpu.CompilerParams(
             collective_id=0, has_side_effects=True, vmem_limit_bytes=VMEM_GRANT

time: 73 us -> 68.9 us (0.944)
  the two profiles are of different devices: /device:TPU:8 before, /device:TPU:1 now
where the time goes in v5:
time: 68.9 us; the launch traced here: 68.7 us
  Pallas kernels  66.8 us (97%)
  between operations  1.93 us (3%)
    pallas_call x1, Pallas kernels, per_device(): pl.pallas_call(kernel, out_shape=results, in_specs=[hbm, hbm, hbm, hbm, s...  64.8 us
    pallas_call x1, Pallas kernels, per_device(): pl.pallas_call(finish, out_shape=results, in_specs=[hbm] * 4, out_specs=(...  1.96 us

profile of v5, /device:TPU:1, one launch (start us, length us, event | category | flops | bytes accessed | tf_op | source)
XLA Modules:
  0.0 68.7 jit_solution(1049313198778559351)
XLA Ops:
  1.9 64.8 %shard_map.93 = (f32[1,128]{1,0:T(1,128)}, bf16[128,1152]{1,0:T(8,128)(2,1)}, bf16[128,1152]{1,0:T(8,128)(2,1)}, f32[72,1152]{1,0:T(8,128)}) custom-call(bf16[128,1152]{1,0:T(8,128)(2,1)} %img_hbm.1, bf16[128,1152]{1,0:T(8,128)(2,1)} %pool_hbm.1, bf16[72,1152]{1,0:T(8,128)(2,1)} %wsh_hbm.1, f32[1152]{0:T(1024)} %hb_hbm.1, f32[1]{0:T(128)S(6)} %copy.10.log_scale, ...), custom_call_target="tpu_custom_call" | custom-call | flops 4000000000 | bytes 6000000 | tf_op jit(solution)/shard_map/pallas_call | solution.py:698
  66.8 2.0 %shard_map.94 = (f32[1,128]{1,0:T(1,128)}, bf16[128,1152]{1,0:T(8,128)(2,1)}, bf16[128,1152]{1,0:T(8,128)(2,1)}, f32[72,1152]{1,0:T(8,128)}) custom-call(f32[1,128]{1,0:T(1,128)} %get-tuple-element.12.refs_0_, bf16[128,1152]{1,0:T(8,128)(2,1)} %get-tuple-element.13.refs_1_, bf16[128,1152]{1,0:T(8,128)(2,1)} %get-tuple-element.14.refs_2_, ...), custom_call_target="tpu_custom_call" | custom-call | tf_op jit(solution)/shard_map/pallas_call | solution.py:754

commit v6 on v5

--- a/solution.py
+++ b/solution.py
@@ -21,6 +21,7 @@
 VMEM_GRANT = 60 * 1024 * 1024
 HALF = 64
 SPLIT = 640
+PLACE = {1: 0, 3: 1, 4: 2, 2: 3}
 ORDER = (2, 1, 3, 0)
 
 
@@ -36,7 +37,7 @@
     wtmp, wf, xbuf, pbuf, xb, zb, ximg, ztxt, u, dzb, psib, ptf, pt, terms,
     st_a, st_b, far_a, far_b, near_a, near_b,
     y_a, y_b, pass_a, pass_b, in_a, in_b,
-    gdx_out, gsum_out, gdx_in, gsum_in,
+    gdx, gdx_out, gsum_out, gdx_in, gsum_in,
     l_s, o_s, w_s, w_r, x_s, x_r, p_s, p_r, g_s, g_r, h_s, h_r,
 ):
     loads = [
@@ -101,13 +102,15 @@
             copy(part(src, h), part(xbuf.at[k - 1], h), x_s.at[k, h], x_r.at[k - 1, h], up).start()
 
     def send_p(k, src, h):
-        @pl.when(jnp.logical_and(k <= j, j <= 1))
-        def _():
-            copy(part(src, h), part(pbuf.at[k + 1], h), p_s.at[k, h], p_r.at[k + 1, h], up).start()
-
-        @pl.when(jnp.logical_and(k > j, j >= 2))
-        def _():
-            copy(part(src, h), part(pbuf.at[k - 1], h), p_s.at[k, h], p_r.at[k - 1, h], dn).start()
+        if k < 4:
+          @pl.when(jnp.logical_and(k <= j, j <= 1))
+          def _():
+            copy(part(src, h), part(pbuf.at[PLACE[k + 1]], h), p_s.at[k, h], p_r.at[k + 1, h], up).start()
+
+        if k > 2:
+          @pl.when(jnp.logical_and(k > j, j >= 2))
+          def _():
+            copy(part(src, h), part(pbuf.at[PLACE[k - 1]], h), p_s.at[k, h], p_r.at[k - 1, h], dn).start()
 
     def wait_x(k, h, whole=False):
         dst = xbuf.at[k] if whole else part(xbuf.at[k], h)
@@ -120,7 +123,7 @@
     hop_up = [copy(quarter(4, q), quarter(3, q), x_s.at[4, q], x_r.at[3, q // 2], up) for q in range(4)]
 
     def wait_p(k, h):
-        dst = part(pbuf.at[k], h)
+        dst = part(pbuf.at[PLACE[k]], h)
         copy(dst, dst, p_s.at[k, h], p_r.at[k, h], up).wait_recv()
 
     def pass_x(k, h):
@@ -130,7 +133,7 @@
     def pass_p(k):
         for h in range(2):
             wait_p(k, h)
-            send_p(k, pbuf.at[k], h)
+            send_p(k, pbuf.at[PLACE[k]], h)
 
     def x_done(k, src):
         @pl.when(jnp.logical_or(jnp.logical_and(k <= 3 - j, j >= 1), jnp.logical_and(k > 3 - j, j <= 2)))
@@ -142,7 +145,7 @@
         @pl.when(jnp.logical_or(jnp.logical_and(k <= j, j <= 1), jnp.logical_and(k > j, j >= 2)))
         def _():
             for h in range(2):
-                copy(part(src, h), part(pbuf.at[1], h), p_s.at[k, h], p_r.at[1, h], up).wait_send()
+                copy(part(src, h), part(pbuf.at[0], h), p_s.at[k, h], p_r.at[1, h], up).wait_send()
 
     middle = lax.rem(lax.div(j + 1, 2), 2)
     outer = middle == 0
@@ -159,7 +162,7 @@
         copy(img.at[pl.ds(HALF // 2 * q, HALF // 2), :], quarter(4, q), x_s.at[5, q], x_r.at[4, q], zm)
         for q in range(4)
     ]
-    p_hop = [copy(part(pool, h), part(pbuf.at[4], h), p_s.at[5, h], p_r.at[4, h], zp) for h in range(2)]
+    p_hop = [copy(part(pool, h), part(pbuf.at[PLACE[4]], h), p_s.at[5, h], p_r.at[4, h], zp) for h in range(2)]
 
     @pl.when(j <= 2)
     def _():
@@ -359,28 +362,35 @@
         theirs_rest()
         pass_x(2, 0)
 
+    @pl.when(j == 2)
+    def _():
+        pass_p(4)
+
+    @pl.when(j == 1)
+    def _():
+        pass_x(2, 1)
+
     near_first(1, 1 - yh)
 
-    @pl.when(inner)
+    @pl.when(j == 2)
     def _():
         pass_x(2, 1)
 
+    @pl.when(j == 1)
+    def _():
+        send_p(0, pool, 1)
+
     near_rest(1, 1 - yh)
 
     @pl.when(j == 1)
     def _():
-        send_p(0, pool, 1)
         pass_p(1)
 
     @pl.when(j == 2)
     def _():
-        pass_p(4)
+        pass_p(3)
 
     far_units(1, 1 - yh)
-
-    @pl.when(j == 2)
-    def _():
-        pass_p(3)
 
     def ready(k):
         xb[k] = normalize(xbuf[k].astype(F32))[0].astype(BF16)
@@ -485,10 +495,13 @@
         copy(ref, ref, g_s.at[ident], g_r.at[ident], xp).wait_recv()
         return ref[...].astype(F32)
 
-    def first_sends(g):
+    def far_sends(g):
         n = 4 * g
         g_go(st_a.at[g, 0], pair_a(n), 6 * g, far_a.at[g], xp)
         g_go(st_b.at[g, 0], pair_b(n), 6 * g + 1, far_b.at[g], xm)
+
+    def near_sends(g):
+        n = 4 * g
         g_go(st_b.at[g, 1], pair_b(n + 1), 6 * g + 2, near_b.at[g, 0], xp)
         g_go(st_a.at[g, 1], pair_a(n + 2), 6 * g + 3, near_a.at[g, 1], xm)
 
@@ -524,38 +537,74 @@
         u[ROWS:2 * ROWS] = jnp.dot(g, zb[0], preferred_element_type=F32)
         loss_out[...] = losses(m)
 
+    def texts_done(first, last):
+        for n in range(first, last):
+            v = u[ROWS * (n - 1):ROWS * n]
+            zb[n] = normalize(v)[0].astype(BF16)
+
+    def meet(image, texts, own):
+        m, g = weights(image, texts, own)
+        return jnp.dot(g, texts, preferred_element_type=F32), losses(m)
+
+    @pl.when(j == 1)
+    def _():
+        for h in range(2):
+            wait_p(3, h)
+            wait_p(4, h)
+        wait_x(5, 0, whole=True)
+        ready(5)
+
+    @pl.when(j == 2)
+    def _():
+        for h in range(2):
+            wait_p(1, h)
+
+    @pl.when(inner)
+    def _():
+        project(pbuf[0:3].reshape(3 * ROWS, WIDTH), u.at[:3 * ROWS])
+
     pair.wait_recv()
     make(0)
+    far_sends(0)
     make(2)
-    first_sends(0)
+    near_sends(0)
     make(4)
     make(6)
 
+    @pl.when(inner)
+    def _():
+        texts_done(1, 4)
+        d, row = meet(xb[9 - 4 * j], zb[pl.ds(4 - 2 * j, 2)].reshape(2 * ROWS, WIDTH), False)
+        gdx[...] = d
+        gsum_out[...] = row
+
     @pl.when(outer)
     def _():
         back()
 
     second_sends(0)
-    first_sends(1)
-
-    @pl.when(j == 1)
-    def _():
-        for h in range(2):
-            wait_p(4, h)
-            wait_p(3, h)
-        wait_x(5, 0, whole=True)
-        ready(5)
-
-    @pl.when(j == 2)
-    def _():
-        for h in range(2):
-            wait_p(1, h)
+    far_sends(1)
+    near_sends(1)
 
     @pl.when(inner)
     def _():
         for h in range(2):
             wait_p(2, h)
-        project(pbuf[1:5].reshape(4 * ROWS, WIDTH), u)
+        project(pbuf[3], u.at[3 * ROWS:])
+        texts_done(4, 5)
+        d, row = meet(xb[9 - 4 * j], zb[4], False)
+        gdx_out[...] = (gdx[...] + d).astype(BF16)
+        gsum_out[...] += row
+
+        @pl.when(j == 1)
+        def _():
+            gdx_dn.start()
+            gsum_dn.start()
+
+        @pl.when(j == 2)
+        def _():
+            gdx_up.start()
+            gsum_up.start()
 
     a, b = sums(0)
     g_go(y_a, a, 12, pass_a, up2)
@@ -579,28 +628,9 @@
 
     @pl.when(inner)
     def _():
-        @pl.loop(1, 5)
-        def _(k):
-            zb[k] = normalize(u[pl.ds(pl.multiple_of((k - 1) * ROWS, ROWS), ROWS), :])[0].astype(BF16)
-
-        hosted = zb[pl.ds(4 - 2 * j, 3)].reshape(3 * ROWS, WIDTH)
-        m, g = weights(xb[9 - 4 * j], hosted, False)
-        gdx_out[...] = jnp.dot(g, hosted, preferred_element_type=F32).astype(BF16)
-        gsum_out[...] = losses(m)
-
-        @pl.when(j == 1)
-        def _():
-            gdx_dn.start()
-            gsum_dn.start()
-
-        @pl.when(j == 2)
-        def _():
-            gdx_up.start()
-            gsum_up.start()
-
-        texts = zb[0:4].reshape(4 * ROWS, WIDTH)
-        m, g = weights(xb[0], texts, True)
-        image_side(jnp.dot(g, texts, preferred_element_type=F32), losses(m))
+        d, row = meet(xb[0], zb[0:3].reshape(3 * ROWS, WIDTH), True)
+        e, more = meet(xb[0], zb[4], False)
+        image_side(d + e, row + more)
         back()
 
     a, b = sums(1)
@@ -658,8 +688,8 @@
     p_done(0, pool)
     for k in range(1, 4):
         x_done(k, xbuf.at[k])
-        p_done(k, pbuf.at[k])
-    p_done(4, pbuf.at[4])
+        p_done(k, pbuf.at[0])
+    p_done(4, pbuf.at[0])
     pool_swap.wait_send()
     pair.wait_send()
     for d in g_sent + onward:
@@ -712,7 +742,7 @@
             pltpu.VMEM(slab, BF16),
             pltpu.VMEM((WIDTH, WIDTH), BF16),
             pltpu.VMEM((6,) + block, BF16),
-            pltpu.VMEM((5,) + block, BF16),
+            pltpu.VMEM((4,) + block, BF16),
             pltpu.VMEM((6,) + block, BF16),
             pltpu.VMEM((5,) + block, BF16),
             pltpu.VMEM(block, F32),
@@ -735,6 +765,7 @@
             pltpu.VMEM(slab_b, BF16),
             pltpu.VMEM(slab_a, BF16),
             pltpu.VMEM(slab_b, BF16),
+            pltpu.VMEM(block, F32),
             pltpu.VMEM(block, BF16),
             pltpu.VMEM((1, ROWS), F32),
             pltpu.VMEM(block, BF16),

time: 68.9 us -> 71.4 us (1.036)
  the two profiles are of different devices: /device:TPU:1 before, /device:TPU:8 now
where the time goes in v6:
time: 71.4 us; the launch traced here: 71.3 us
  Pallas kernels  69.3 us (97%)
  between operations  1.93 us (3%)
    pallas_call x1, Pallas kernels, per_device(): pl.pallas_call(kernel, out_shape=results, in_specs=[hbm, hbm, hbm, hbm, s...  67.4 us
    pallas_call x1, Pallas kernels, per_device(): pl.pallas_call(finish, out_shape=results, in_specs=[hbm] * 4, out_specs=(...  1.96 us

profile of v6, /device:TPU:8, one launch (start us, length us, event | category | flops | bytes accessed | tf_op | source)
XLA Modules:
  0.0 71.3 jit_solution(311785291213700640)
XLA Ops:
  1.9 67.4 %shard_map.93 = (f32[1,128]{1,0:T(1,128)}, bf16[128,1152]{1,0:T(8,128)(2,1)}, bf16[128,1152]{1,0:T(8,128)(2,1)}, f32[72,1152]{1,0:T(8,128)}) custom-call(bf16[128,1152]{1,0:T(8,128)(2,1)} %img_hbm.1, bf16[128,1152]{1,0:T(8,128)(2,1)} %pool_hbm.1, bf16[72,1152]{1,0:T(8,128)(2,1)} %wsh_hbm.1, f32[1152]{0:T(1024)} %hb_hbm.1, f32[1]{0:T(128)S(6)} %copy.10.log_scale, ...), custom_call_target="tpu_custom_call" | custom-call | flops 4000000000 | bytes 6000000 | tf_op jit(solution)/shard_map/pallas_call | solution.py:728
  69.3 2.0 %shard_map.94 = (f32[1,128]{1,0:T(1,128)}, bf16[128,1152]{1,0:T(8,128)(2,1)}, bf16[128,1152]{1,0:T(8,128)(2,1)}, f32[72,1152]{1,0:T(8,128)}) custom-call(f32[1,128]{1,0:T(1,128)} %get-tuple-element.12.refs_0_, bf16[128,1152]{1,0:T(8,128)(2,1)} %get-tuple-element.13.refs_1_, bf16[128,1152]{1,0:T(8,128)(2,1)} %get-tuple-element.14.refs_2_, ...), custom_call_target="tpu_custom_call" | custom-call | tf_op jit(solution)/shard_map/pallas_call | solution.py:785

commit v7 on v6

--- a/solution.py
+++ b/solution.py
@@ -18,9 +18,9 @@
 PART = 64
 AHEAD = 48
 TILE = 384
-VMEM_GRANT = 60 * 1024 * 1024
+VMEM_GRANT = 44 * 1024 * 1024
 HALF = 64
-SPLIT = 640
+PIECES = ((0, 384, 1), (640, 256, -1), (384, 256, 1), (896, 256, -1))
 PLACE = {1: 0, 3: 1, 4: 2, 2: 3}
 ORDER = (2, 1, 3, 0)
 
@@ -32,13 +32,13 @@
 
 def kernel(
     img_hbm, pool_hbm, wsh_hbm, hb_hbm, log_scale, bias,
-    loss_hbm, img_grad_hbm, pool_grad_hbm, head_grad_hbm,
-    img, pool, wsh, hb, loss_out, img_out, pool_out, head_out,
+    loss_out, img_out, pool_out, head_out,
+    img, pool, wsh, hb,
     wtmp, wf, xbuf, pbuf, xb, zb, ximg, ztxt, u, dzb, psib, ptf, pt, terms,
-    st_a, st_b, far_a, far_b, near_a, near_b,
-    y_a, y_b, pass_a, pass_b, in_a, in_b,
+    g_out, g_far, g_near,
+    y_out, y_pass, y_in,
     gdx, gdx_out, gsum_out, gdx_in, gsum_in,
-    l_s, o_s, w_s, w_r, x_s, x_r, p_s, p_r, g_s, g_r, h_s, h_r,
+    l_s, w_s, w_r, x_s, x_r, p_s, p_r, g_s, g_r, h_s, h_r,
 ):
     loads = [
         pltpu.make_async_copy(src, dst, l_s.at[i])
@@ -48,13 +48,6 @@
     ]
     for d in loads:
         d.start()
-    stores = [
-        pltpu.make_async_copy(src, dst, o_s.at[i])
-        for i, (src, dst) in enumerate(
-            ((loss_out, loss_hbm), (img_out, img_grad_hbm), (pool_out, pool_grad_hbm), (head_out, head_grad_hbm))
-        )
-    ]
-
     dp = lax.axis_index("dp")
     f = lax.axis_index("fsdp")
     j = lax.rem(dp, 4)
@@ -435,10 +428,8 @@
 
     def image_side(d, row):
         loss_out[...] = row * (1.0 / ROWS)
-        stores[0].start()
         v = ximg[...]
         img_out[...] = (xr * (d - v * jnp.sum(v * d, axis=-1, keepdims=True))).astype(BF16)
-        stores[1].start()
 
     project(pool[...], ztxt)
     v, zr = normalize(ztxt[...])
@@ -477,11 +468,9 @@
         terms[n] = t[:SHARD]
         terms[n + 1] = t[SHARD:]
 
-    def pair_a(n):
-        return terms[n, :, :SPLIT]
-
-    def pair_b(n):
-        return terms[n, :, SPLIT:]
+    def cols(n, q):
+        start, size, _ = PIECES[q]
+        return terms[n, :, start:start + size]
 
     g_sent = []
 
@@ -495,26 +484,27 @@
         copy(ref, ref, g_s.at[ident], g_r.at[ident], xp).wait_recv()
         return ref[...].astype(F32)
 
+    def slot(refs, q, *index):
+        return refs[q].at[index] if index else refs[q]
+
     def far_sends(g):
-        n = 4 * g
-        g_go(st_a.at[g, 0], pair_a(n), 6 * g, far_a.at[g], xp)
-        g_go(st_b.at[g, 0], pair_b(n), 6 * g + 1, far_b.at[g], xm)
+        for q, (_, _, way) in enumerate(PIECES):
+            g_go(slot(g_out, q, g, 0), cols(4 * g, q), 12 * g + q, slot(g_far, q, g), xp if way > 0 else xm)
 
     def near_sends(g):
-        n = 4 * g
-        g_go(st_b.at[g, 1], pair_b(n + 1), 6 * g + 2, near_b.at[g, 0], xp)
-        g_go(st_a.at[g, 1], pair_a(n + 2), 6 * g + 3, near_a.at[g, 1], xm)
+        for q, (_, _, way) in enumerate(PIECES):
+            n, who = (2, xm) if way > 0 else (1, xp)
+            g_go(slot(g_out, q, g, 1), cols(4 * g + n, q), 12 * g + 4 + q, slot(g_near, q, g, 0), who)
 
     def second_sends(g):
-        n = 4 * g
-        g_go(st_a.at[g, 2], pair_a(n + 1) + g_wait(far_a.at[g], 6 * g), 6 * g + 4, near_a.at[g, 0], xp)
-        g_go(st_b.at[g, 2], pair_b(n + 2) + g_wait(far_b.at[g], 6 * g + 1), 6 * g + 5, near_b.at[g, 1], xm)
-
-    def sums(g):
-        n = 4 * g + 3
-        a = pair_a(n) + g_wait(near_a.at[g, 0], 6 * g + 4) + g_wait(near_a.at[g, 1], 6 * g + 3)
-        b = pair_b(n) + g_wait(near_b.at[g, 0], 6 * g + 2) + g_wait(near_b.at[g, 1], 6 * g + 5)
-        return a, b
+        for q, (_, _, way) in enumerate(PIECES):
+            n, who = (1, xp) if way > 0 else (2, xm)
+            value = cols(4 * g + n, q) + g_wait(slot(g_far, q, g), 12 * g + q)
+            g_go(slot(g_out, q, g, 2), value, 12 * g + 8 + q, slot(g_near, q, g, 1), who)
+
+    def total(g, q):
+        value = cols(4 * g + 3, q) + g_wait(slot(g_near, q, g, 0), 12 * g + 4 + q)
+        return value + g_wait(slot(g_near, q, g, 1), 12 * g + 8 + q)
 
     def back():
         @pl.loop(0, WIDTH // TILE)
@@ -524,8 +514,6 @@
                 dzb[:ROWS], wf[cols, :], NT, preferred_element_type=F32
             ).astype(BF16)
 
-        stores[2].start()
-
     gdx_up = copy(gdx_out, gdx_in, h_s.at[0], h_r.at[0], up)
     gdx_dn = copy(gdx_out, gdx_in, h_s.at[0], h_r.at[0], dn)
     gsum_up = copy(gsum_out, gsum_in, h_s.at[1], h_r.at[1], up)
@@ -551,8 +539,6 @@
         for h in range(2):
             wait_p(3, h)
             wait_p(4, h)
-        wait_x(5, 0, whole=True)
-        ready(5)
 
     @pl.when(j == 2)
     def _():
@@ -571,6 +557,11 @@
     make(4)
     make(6)
 
+    @pl.when(j == 1)
+    def _():
+        wait_x(5, 0, whole=True)
+        ready(5)
+
     @pl.when(inner)
     def _():
         texts_done(1, 4)
@@ -585,6 +576,23 @@
     second_sends(0)
     far_sends(1)
     near_sends(1)
+
+    for q, (_, _, way) in enumerate(PIECES):
+        g_go(slot(y_out, q), total(0, q), 24 + q, slot(y_pass, q), up2 if way > 0 else dn2)
+
+    onward = [
+        copy(slot(y_pass, q), slot(y_in, q), g_s.at[28 + q], g_r.at[28 + q], up2 if way > 0 else dn2)
+        for q, (_, _, way) in enumerate(PIECES)
+    ]
+
+    def relay():
+        for q in range(4):
+            copy(slot(y_pass, q), slot(y_pass, q), g_s.at[24 + q], g_r.at[24 + q], xp).wait_recv()
+            onward[q].start()
+
+    @pl.when(outer)
+    def _():
+        relay()
 
     @pl.when(inner)
     def _():
@@ -606,24 +614,6 @@
             gdx_up.start()
             gsum_up.start()
 
-    a, b = sums(0)
-    g_go(y_a, a, 12, pass_a, up2)
-    g_go(y_b, b, 13, pass_b, dn2)
-
-    onward = [
-        copy(pass_a, in_a, g_s.at[14], g_r.at[14], up2),
-        copy(pass_b, in_b, g_s.at[15], g_r.at[15], dn2),
-    ]
-
-    def relay():
-        for ref, ident, d in ((pass_a, 12, onward[0]), (pass_b, 13, onward[1])):
-            copy(ref, ref, g_s.at[ident], g_r.at[ident], xp).wait_recv()
-            d.start()
-
-    @pl.when(outer)
-    def _():
-        relay()
-
     second_sends(1)
 
     @pl.when(inner)
@@ -631,15 +621,14 @@
         d, row = meet(xb[0], zb[0:3].reshape(3 * ROWS, WIDTH), True)
         e, more = meet(xb[0], zb[4], False)
         image_side(d + e, row + more)
+
+    @pl.when(inner)
+    def _():
+        relay()
         back()
 
-    a, b = sums(1)
-    head_out[:, :SPLIT] = a
-    head_out[:, SPLIT:] = b
-
-    @pl.when(inner)
-    def _():
-        relay()
+    for q, (start, size, _) in enumerate(PIECES):
+        head_out[:, start:start + size] = total(1, q)
 
     @pl.when(outer)
     def _():
@@ -647,9 +636,8 @@
         gdx_up.wait_recv()
         image_side(u[ROWS:2 * ROWS] + gdx_in[...].astype(F32), loss_out[...] + gsum_in[...])
 
-    head_out[:, :SPLIT] += g_wait(in_a, 14)
-    head_out[:, SPLIT:] += g_wait(in_b, 15)
-    stores[3].start()
+    for q, (start, size, _) in enumerate(PIECES):
+        head_out[:, start:start + size] += g_wait(slot(y_in, q), 28 + q)
 
     w_swap.wait_send()
     for d in w_sent:
@@ -694,30 +682,23 @@
     pair.wait_send()
     for d in g_sent + onward:
         d.wait_send()
-    for d in stores:
+
+
+def finish(*refs):
+    moves = [pltpu.make_async_copy(refs[i], refs[4 + i], refs[8].at[i]) for i in range(4)]
+    for d in moves:
+        d.start()
+    for d in moves:
         d.wait()
-
-
-def finish(*refs):
-    into, out = refs[12], refs[13]
-    loads = [pltpu.make_async_copy(refs[i], refs[8 + i], into.at[i]) for i in range(4)]
-    stores = [pltpu.make_async_copy(refs[8 + i], refs[4 + i], out.at[i]) for i in range(4)]
-    for d in loads:
-        d.start()
-    for d, e in zip(loads, stores):
-        d.wait()
-        e.start()
-    for e in stores:
-        e.wait()
 
 
 def per_device(images, pooled, head_weight, head_bias, log_scale, bias):
     smem = pl.BlockSpec(memory_space=pltpu.SMEM)
+    vmem = pl.BlockSpec(memory_space=pltpu.VMEM)
     hbm = pl.BlockSpec(memory_space=pltpu.HBM)
     block = (ROWS, WIDTH)
     slab = (SHARD, WIDTH)
-    slab_a = (SHARD, SPLIT)
-    slab_b = (SHARD, WIDTH - SPLIT)
+    parts = [(SHARD, size) for _, size, _ in PIECES]
     dma = pltpu.SemaphoreType.DMA
     results = (
         jax.ShapeDtypeStruct((1, ROWS), F32),
@@ -729,16 +710,12 @@
         kernel,
         out_shape=results,
         in_specs=[hbm, hbm, hbm, hbm, smem, smem],
-        out_specs=(hbm, hbm, hbm, hbm),
+        out_specs=(vmem,) * 4,
         scratch_shapes=[
             pltpu.VMEM(block, BF16),
             pltpu.VMEM(block, BF16),
             pltpu.VMEM(slab, BF16),
             pltpu.VMEM((1, WIDTH), F32),
-            pltpu.VMEM((1, ROWS), F32),
-            pltpu.VMEM(block, BF16),
-            pltpu.VMEM(block, BF16),
-            pltpu.VMEM(slab, F32),
             pltpu.VMEM(slab, BF16),
             pltpu.VMEM((WIDTH, WIDTH), BF16),
             pltpu.VMEM((6,) + block, BF16),
@@ -753,42 +730,35 @@
             pltpu.VMEM((WIDTH, ROWS), F32),
             pltpu.VMEM((8 * SHARD, 2 * ROWS), BF16),
             pltpu.VMEM((8,) + slab, F32),
-            pltpu.VMEM((2, 3) + slab_a, BF16),
-            pltpu.VMEM((2, 3) + slab_b, BF16),
-            pltpu.VMEM((2,) + slab_a, BF16),
-            pltpu.VMEM((2,) + slab_b, BF16),
-            pltpu.VMEM((2, 2) + slab_a, BF16),
-            pltpu.VMEM((2, 2) + slab_b, BF16),
-            pltpu.VMEM(slab_a, BF16),
-            pltpu.VMEM(slab_b, BF16),
-            pltpu.VMEM(slab_a, BF16),
-            pltpu.VMEM(slab_b, BF16),
-            pltpu.VMEM(slab_a, BF16),
-            pltpu.VMEM(slab_b, BF16),
+            [pltpu.VMEM((2, 3) + p, BF16) for p in parts],
+            [pltpu.VMEM((2,) + p, BF16) for p in parts],
+            [pltpu.VMEM((2, 2) + p, BF16) for p in parts],
+            [pltpu.VMEM(p, BF16) for p in parts],
+            [pltpu.VMEM(p, BF16) for p in parts],
+            [pltpu.VMEM(p, BF16) for p in parts],
             pltpu.VMEM(block, F32),
             pltpu.VMEM(block, BF16),
             pltpu.VMEM((1, ROWS), F32),
             pltpu.VMEM(block, BF16),
             pltpu.VMEM((1, ROWS), F32),
-            dma((4,)), dma((4,)),
+            dma((4,)),
             dma((24,)), dma((24,)),
             dma((7, 4)), dma((6, 4)),
             dma((6, 2)), dma((5, 2)),
-            dma((16,)), dma((16,)),
+            dma((32,)), dma((32,)),
             dma((4,)), dma((4,)),
         ],
         compiler_params=pltpu.CompilerParams(
             collective_id=0, has_side_effects=True, vmem_limit_bytes=VMEM_GRANT
         ),
         cost_estimate=pl.CostEstimate(flops=4_000_000_000, bytes_accessed=6_000_000, transcendentals=300_000),
-    )(images, pooled, head_weight, head_bias, log_scale, bias)
+    )(*[pltpu.with_memory_space_constraint(v, pltpu.HBM) for v in (images, pooled, head_weight, head_bias)], log_scale, bias)
     loss, image_grad, pooled_grad, head_grad = pl.pallas_call(
         finish,
         out_shape=results,
-        in_specs=[hbm] * 4,
+        in_specs=[vmem] * 4,
         out_specs=(hbm,) * 4,
-        scratch_shapes=[pltpu.VMEM(r.shape, r.dtype) for r in results] + [dma((4,)), dma((4,))],
-        compiler_params=pltpu.CompilerParams(vmem_limit_bytes=VMEM_GRANT),
+        scratch_shapes=[dma((4,))],
     )(*made)
     return loss.reshape(ROWS), image_grad, pooled_grad, head_grad
 

time: 71.4 us -> 72.1 us (level)
  the two profiles are of different devices: /device:TPU:8 before, /device:TPU:1 now
where the time goes in v7:
time: 72.1 us; the launch traced here: 71.9 us
  Pallas kernels  67.2 us (93%)
  local copies, waits for them, and re-layouts  2.74 us (4%)
  between operations  1.94 us (3%)
    pallas_call x1, Pallas kernels, per_device(): pl.pallas_call(kernel, out_shape=results, in_specs=[hbm, hbm, hbm, hbm, s...  65.1 us
    unnamed x8, local copies, waits for them, and re-layouts  2.74 us
    pallas_call x1, Pallas kernels, per_device(): pl.pallas_call(finish, out_shape=results, in_specs=[vmem] * 4, out_specs=...  2.11 us

profile of v7, /device:TPU:1, one launch (start us, length us, event | category | flops | bytes accessed | tf_op | source)
XLA Modules:
  0.0 71.9 jit_solution(3637085175169605175)
XLA Ops:
  1.9 65.1 %shard_map.93 = (f32[1,128]{1,0:T(1,128)S(1)}, bf16[128,1152]{1,0:T(8,128)(2,1)S(1)}, bf16[128,1152]{1,0:T(8,128)(2,1)S(1)}, f32[72,1152]{1,0:T(8,128)S(1)}) custom-call(bf16[128,1152]{1,0:T(8,128)(2,1)} %img_hbm.1, bf16[128,1152]{1,0:T(8,128)(2,1)} %pool_hbm.1, bf16[72,1152]{1,0:T(8,128)(2,1)} %wsh_hbm.1, f32[1152]{0:T(1024)} %hb_hbm.1, ...), custom_call_target="tpu_custom_call" | custom-call | flops 4000000000 | bytes 6000000 | tf_op jit(solution)/shard_map/pallas_call | solution.py:709
  67.0 0.0 copy-start
  67.0 0.7 copy-done
  67.8 0.0 copy-start.1
  67.8 0.7 copy-done.1
  68.5 0.0 copy-start.2
  68.5 0.7 %copy-done.2 = bf16[128,1152]{1,0:T(8,128)(2,1)} copy-done((bf16[128,1152]{1,0:T(8,128)(2,1)}, bf16[128,1152]{1,0:T(8,128)(2,1)S(1)}, u32[]{:S(2)}) %copy-start.2) | copy-done | bytes 294936
  69.2 0.0 copy-start.3
  69.2 0.6 copy-done.3
  69.8 2.1 %shard_map.94 = (f32[1,128]{1,0:T(1,128)}, bf16[128,1152]{1,0:T(8,128)(2,1)}, bf16[128,1152]{1,0:T(8,128)(2,1)}, f32[72,1152]{1,0:T(8,128)}) custom-call(f32[1,128]{1,0:T(1,128)} %copy-done.3, bf16[128,1152]{1,0:T(8,128)(2,1)} %copy-done.1, bf16[128,1152]{1,0:T(8,128)(2,1)} %copy-done.2, f32[72,1152]{1,0:T(8,128)} %copy-done), custom_call_target="tpu_custom_call" | custom-call | tf_op jit(solution)/shard_map/pallas_call | solution.py:756
Async XLA Ops:
  67.0 0.7 %copy-start = (f32[72,1152]{1,0:T(8,128)}, f32[72,1152]{1,0:T(8,128)S(1)}, u32[]{:S(2)}) copy-start(f32[72,1152]{1,0:T(8,128)S(1)} %get-tuple-element.15.refs_3_) | copy-start | bytes 995332
  67.8 0.7 copy-start.1
  68.5 0.7 %copy-start.2 = (bf16[128,1152]{1,0:T(8,128)(2,1)}, bf16[128,1152]{1,0:T(8,128)(2,1)S(1)}, u32[]{:S(2)}) copy-start(bf16[128,1152]{1,0:T(8,128)(2,1)S(1)} %get-tuple-element.14.refs_2_) | copy-start | bytes 884740
  69.2 0.6 copy-start.3

commit v8 on v7

--- a/solution.py
+++ b/solution.py
@@ -65,15 +65,27 @@
     up = (dp + 1 - 4 * wrap_up, lax.rem(f + 8 * wrap_up, 16))
     wrap_dn = lax.div(3 - j, 3)
     dn = (dp - 1 + 4 * wrap_dn, lax.rem(f + 8 * wrap_dn, 16))
-    wrap = lax.div(j + 2, 4)
-    up2 = (dp + 2 - 4 * wrap, lax.rem(f + 8 * wrap, 16))
+    odd = lax.rem(j, 2)
+    step = 3 - 2 * odd
+    wrap = lax.div(j + step, 4)
+    y_up = (dp + step - 4 * wrap, lax.rem(f + 8 * wrap, 16))
+    step = 1 + 2 * odd
     wrap = lax.div(3 - j, 2)
-    dn2 = (dp - 2 + 4 * wrap, lax.rem(f + 8 * wrap, 16))
+    y_dn = (dp - step + 4 * wrap, lax.rem(f + 8 * wrap, 16))
 
     barrier = pltpu.get_barrier_semaphore()
-    for who in (sib, xp, xm, zp, zm, up, dn, up2, dn2):
+    for who in (sib, xp, xm, zp, zm, up, dn):
         pl.semaphore_signal(barrier, inc=1, device_id=who, device_id_type=MESH)
-    pl.semaphore_wait(barrier, 9)
+
+    @pl.when(odd == 0)
+    def _():
+        pl.semaphore_signal(barrier, inc=1, device_id=y_up, device_id_type=MESH)
+
+    @pl.when(odd == 1)
+    def _():
+        pl.semaphore_signal(barrier, inc=1, device_id=y_dn, device_id_type=MESH)
+
+    pl.semaphore_wait(barrier, 8)
     for d in loads:
         d.wait()
 
@@ -577,23 +589,6 @@
     far_sends(1)
     near_sends(1)
 
-    for q, (_, _, way) in enumerate(PIECES):
-        g_go(slot(y_out, q), total(0, q), 24 + q, slot(y_pass, q), up2 if way > 0 else dn2)
-
-    onward = [
-        copy(slot(y_pass, q), slot(y_in, q), g_s.at[28 + q], g_r.at[28 + q], up2 if way > 0 else dn2)
-        for q, (_, _, way) in enumerate(PIECES)
-    ]
-
-    def relay():
-        for q in range(4):
-            copy(slot(y_pass, q), slot(y_pass, q), g_s.at[24 + q], g_r.at[24 + q], xp).wait_recv()
-            onward[q].start()
-
-    @pl.when(outer)
-    def _():
-        relay()
-
     @pl.when(inner)
     def _():
         for h in range(2):
@@ -614,6 +609,19 @@
             gdx_up.start()
             gsum_up.start()
 
+    for q, (_, _, way) in enumerate(PIECES):
+        g_go(slot(y_out, q), total(0, q), 24 + q, slot(y_pass, q), y_up if way > 0 else y_dn)
+
+    onward = [
+        copy(slot(y_pass, q), slot(y_in, q), g_s.at[28 + q], g_r.at[28 + q], y_up if way > 0 else y_dn)
+        for q, (_, _, way) in enumerate(PIECES)
+    ]
+
+    def relay():
+        for q in range(4):
+            copy(slot(y_pass, q), slot(y_pass, q), g_s.at[24 + q], g_r.at[24 + q], xp).wait_recv()
+            onward[q].start()
+
     second_sends(1)
 
     @pl.when(inner)
@@ -622,9 +630,10 @@
         e, more = meet(xb[0], zb[4], False)
         image_side(d + e, row + more)
 
-    @pl.when(inner)
-    def _():
-        relay()
+    relay()
+
+    @pl.when(inner)
+    def _():
         back()
 
     for q, (start, size, _) in enumerate(PIECES):
@@ -759,6 +768,7 @@
         in_specs=[vmem] * 4,
         out_specs=(hbm,) * 4,
         scratch_shapes=[dma((4,))],
+        compiler_params=pltpu.CompilerParams(vmem_limit_bytes=4 * 1024 * 1024),
     )(*made)
     return loss.reshape(ROWS), image_grad, pooled_grad, head_grad
 

time: 72.1 us -> 69.7 us (0.967)
  the two profiles are of different devices: /device:TPU:1 before, /device:TPU:8 now
where the time goes in v8:
time: 69.7 us; the launch traced here: 69.5 us
  Pallas kernels  67.6 us (97%)
  between operations  1.93 us (3%)
    pallas_call x1, Pallas kernels, per_device(): pl.pallas_call(kernel, out_shape=results, in_specs=[hbm, hbm, hbm, hbm, s...  66.6 us

profile of v8, /device:TPU:8, one launch (start us, length us, event | category | flops | bytes accessed | tf_op | source)
XLA Modules:
  0.0 69.5 jit_solution(2446207941345746835)
XLA Ops:
  1.9 66.6 %shard_map.93 = (f32[1,128]{1,0:T(1,128)S(1)}, bf16[128,1152]{1,0:T(8,128)(2,1)S(1)}, bf16[128,1152]{1,0:T(8,128)(2,1)S(1)}, f32[72,1152]{1,0:T(8,128)S(1)}) custom-call(bf16[128,1152]{1,0:T(8,128)(2,1)} %img_hbm.1, bf16[128,1152]{1,0:T(8,128)(2,1)} %pool_hbm.1, bf16[72,1152]{1,0:T(8,128)(2,1)} %wsh_hbm.1, f32[1152]{0:T(1024)} %hb_hbm.1, ...), custom_call_target="tpu_custom_call" | custom-call | flops 4000000000 | bytes 6000000 | tf_op jit(solution)/shard_map/pallas_call | solution.py:718
  68.6 1.0 %shard_map.94 = (f32[1,128]{1,0:T(1,128)}, bf16[128,1152]{1,0:T(8,128)(2,1)}, bf16[128,1152]{1,0:T(8,128)(2,1)}, f32[72,1152]{1,0:T(8,128)}) custom-call(f32[1,128]{1,0:T(1,128)S(1)} %get-tuple-element.12.refs_0_, bf16[128,1152]{1,0:T(8,128)(2,1)S(1)} %get-tuple-element.13.refs_1_, bf16[128,1152]{1,0:T(8,128)(2,1)S(1)} %get-tuple-element.14.refs_2_, ...), custom_call_target="tpu_custom_call" | custom-call | tf_op jit(solution)/shard_map/pallas_call | solution.py:765

commit v9 on v8

--- a/solution.py
+++ b/solution.py
@@ -546,28 +546,46 @@
         m, g = weights(image, texts, own)
         return jnp.dot(g, texts, preferred_element_type=F32), losses(m)
 
-    @pl.when(j == 1)
-    def _():
-        for h in range(2):
-            wait_p(3, h)
-            wait_p(4, h)
-
-    @pl.when(j == 2)
-    def _():
-        for h in range(2):
-            wait_p(1, h)
-
-    @pl.when(inner)
-    def _():
-        project(pbuf[0:3].reshape(3 * ROWS, WIDTH), u.at[:3 * ROWS])
+    @pl.when(inner)
+    def _():
+        back()
 
     pair.wait_recv()
     make(0)
     far_sends(0)
     make(2)
     near_sends(0)
-    make(4)
-    make(6)
+
+    @pl.when(j == 1)
+    def _():
+        for h in range(2):
+            wait_p(3, h)
+            wait_p(4, h)
+
+    @pl.when(j == 2)
+    def _():
+        for h in range(2):
+            wait_p(1, h)
+
+    @pl.when(inner)
+    def _():
+        project(pbuf[0:3].reshape(3 * ROWS, WIDTH), u.at[:3 * ROWS])
+
+    @pl.when(outer)
+    def _():
+        make(4)
+        make(6)
+        back()
+
+    second_sends(0)
+
+    @pl.when(inner)
+    def _():
+        make(4)
+        make(6)
+
+    far_sends(1)
+    near_sends(1)
 
     @pl.when(j == 1)
     def _():
@@ -581,13 +599,18 @@
         gdx[...] = d
         gsum_out[...] = row
 
-    @pl.when(outer)
-    def _():
-        back()
-
-    second_sends(0)
-    far_sends(1)
-    near_sends(1)
+    for q, (_, _, way) in enumerate(PIECES):
+        g_go(slot(y_out, q), total(0, q), 24 + q, slot(y_pass, q), y_up if way > 0 else y_dn)
+
+    onward = [
+        copy(slot(y_pass, q), slot(y_in, q), g_s.at[28 + q], g_r.at[28 + q], y_up if way > 0 else y_dn)
+        for q, (_, _, way) in enumerate(PIECES)
+    ]
+
+    def relay():
+        for q in range(4):
+            copy(slot(y_pass, q), slot(y_pass, q), g_s.at[24 + q], g_r.at[24 + q], xp).wait_recv()
+            onward[q].start()
 
     @pl.when(inner)
     def _():
@@ -609,19 +632,6 @@
             gdx_up.start()
             gsum_up.start()
 
-    for q, (_, _, way) in enumerate(PIECES):
-        g_go(slot(y_out, q), total(0, q), 24 + q, slot(y_pass, q), y_up if way > 0 else y_dn)
-
-    onward = [
-        copy(slot(y_pass, q), slot(y_in, q), g_s.at[28 + q], g_r.at[28 + q], y_up if way > 0 else y_dn)
-        for q, (_, _, way) in enumerate(PIECES)
-    ]
-
-    def relay():
-        for q in range(4):
-            copy(slot(y_pass, q), slot(y_pass, q), g_s.at[24 + q], g_r.at[24 + q], xp).wait_recv()
-            onward[q].start()
-
     second_sends(1)
 
     @pl.when(inner)
@@ -631,10 +641,6 @@
         image_side(d + e, row + more)
 
     relay()
-
-    @pl.when(inner)
-    def _():
-        back()
 
     for q, (start, size, _) in enumerate(PIECES):
         head_out[:, start:start + size] = total(1, q)

time: 69.7 us -> 68.1 us (0.977)
  Pallas kernels: 67.6 us -> 66 us
    pallas_call x1, Pallas kernels: 66.6 us -> 65.1 us  [per_device(): pl.pallas_call(kernel, out_shape=results, in_specs=[hbm, hbm, hbm, hbm, s...]
where the time goes in v9:
time: 68.1 us; the launch traced here: 68 us
  Pallas kernels  66 us (97%)
  between operations  1.93 us (3%)
    pallas_call x1, Pallas kernels, per_device(): pl.pallas_call(kernel, out_shape=results, in_specs=[hbm, hbm, hbm, hbm, s...  65.1 us

profile of v9, /device:TPU:8, one launch (start us, length us, event | category | flops | bytes accessed | tf_op | source)
XLA Modules:
  0.0 68.0 jit_solution(1739145359547906891)
XLA Ops:
  1.9 65.1 %shard_map.93 = (f32[1,128]{1,0:T(1,128)S(1)}, bf16[128,1152]{1,0:T(8,128)(2,1)S(1)}, bf16[128,1152]{1,0:T(8,128)(2,1)S(1)}, f32[72,1152]{1,0:T(8,128)S(1)}) custom-call(bf16[128,1152]{1,0:T(8,128)(2,1)} %img_hbm.1, bf16[128,1152]{1,0:T(8,128)(2,1)} %pool_hbm.1, bf16[72,1152]{1,0:T(8,128)(2,1)} %wsh_hbm.1, f32[1152]{0:T(1024)} %hb_hbm.1, ...), custom_call_target="tpu_custom_call" | custom-call | flops 4000000000 | bytes 6000000 | tf_op jit(solution)/shard_map/pallas_call | solution.py:724
  67.0 1.0 %shard_map.94 = (f32[1,128]{1,0:T(1,128)}, bf16[128,1152]{1,0:T(8,128)(2,1)}, bf16[128,1152]{1,0:T(8,128)(2,1)}, f32[72,1152]{1,0:T(8,128)}) custom-call(f32[1,128]{1,0:T(1,128)S(1)} %get-tuple-element.12.refs_0_, bf16[128,1152]{1,0:T(8,128)(2,1)S(1)} %get-tuple-element.13.refs_1_, bf16[128,1152]{1,0:T(8,128)(2,1)S(1)} %get-tuple-element.14.refs_2_, ...), custom_call_target="tpu_custom_call" | custom-call | tf_op jit(solution)/shard_map/pallas_call | solution.py:771

commit v10 on v9

--- a/solution.py
+++ b/solution.py
@@ -14,9 +14,7 @@
 WIDTH = 1152
 SHARD = 72
 CHIP = 144
-UNIT = 80
-PART = 64
-AHEAD = 48
+FIRST = 640
 TILE = 384
 VMEM_GRANT = 44 * 1024 * 1024
 HALF = 64
@@ -33,21 +31,13 @@
 def kernel(
     img_hbm, pool_hbm, wsh_hbm, hb_hbm, log_scale, bias,
     loss_out, img_out, pool_out, head_out,
-    img, pool, wsh, hb,
-    wtmp, wf, xbuf, pbuf, xb, zb, ximg, ztxt, u, dzb, psib, ptf, pt, terms,
+    img, pool, hb,
+    wa, wb, wf, xbuf, pbuf, xb, zb, ximg, ztxt, u, dzb, psib, ptf, pt, terms,
     g_out, g_far, g_near,
     y_out, y_pass, y_in,
     gdx, gdx_out, gsum_out, gdx_in, gsum_in,
     l_s, w_s, w_r, x_s, x_r, p_s, p_r, g_s, g_r, h_s, h_r,
 ):
-    loads = [
-        pltpu.make_async_copy(src, dst, l_s.at[i])
-        for i, (src, dst) in enumerate(
-            ((wsh_hbm, wsh), (img_hbm, img), (pool_hbm, pool), (hb_hbm, hb.at[0]))
-        )
-    ]
-    for d in loads:
-        d.start()
     dp = lax.axis_index("dp")
     f = lax.axis_index("fsdp")
     j = lax.rem(dp, 4)
@@ -73,8 +63,27 @@
     wrap = lax.div(3 - j, 2)
     y_dn = (dp - step + 4 * wrap, lax.rem(f + 8 * wrap, 16))
 
+    across = (dp - j + lax.rem(j + 2, 4), lax.rem(f + 8, 16))
+    mine = yh * 4 + x
+    theirs = 4 - yh * 4 + x
+
+    loads = [
+        pltpu.make_async_copy(src, dst, l_s.at[i])
+        for i, (src, dst) in enumerate(
+            (
+                (wsh_hbm.at[:, :FIRST], wa.at[c, mine]),
+                (wsh_hbm.at[:, FIRST:], wb.at[c, mine]),
+                (img_hbm, img),
+                (pool_hbm, pool),
+                (hb_hbm, hb.at[0]),
+            )
+        )
+    ]
+    for d in loads:
+        d.start()
+
     barrier = pltpu.get_barrier_semaphore()
-    for who in (sib, xp, xm, zp, zm, up, dn):
+    for who in (sib, xp, xm, zp, zm, up, dn, across):
         pl.semaphore_signal(barrier, inc=1, device_id=who, device_id_type=MESH)
 
     @pl.when(odd == 0)
@@ -85,7 +94,7 @@
     def _():
         pl.semaphore_signal(barrier, inc=1, device_id=y_dn, device_id_type=MESH)
 
-    pl.semaphore_wait(barrier, 8)
+    pl.semaphore_wait(barrier, 9)
     for d in loads:
         d.wait()
 
@@ -160,8 +169,6 @@
     xk2 = 6 - xk0 - xk1
     guest = copy(img, xbuf.at[5], x_s.at[6, 0], x_r.at[5, 0], up)
 
-    w_swap = copy(wsh, wtmp, w_s.at[0], w_r.at[0], sib)
-    w_swap.start()
     pool_swap = copy(pool, psib, h_s.at[2], h_r.at[2], sib)
     x_hop = [
         copy(img.at[pl.ds(HALF // 2 * q, HALF // 2), :], quarter(4, q), x_s.at[5, q], x_r.at[4, q], zm)
@@ -177,27 +184,11 @@
     send_x(0, img, 0)
     send_x(0, img, 1)
 
-    @pl.when(j == 1)
-    def _():
-        send_p(0, pool, 0)
-
-    @pl.when(j >= 1)
-    def _():
-        for d in p_hop:
-            d.start()
-
-    v, xr = normalize(img[...].astype(F32))
-    ximg[...] = v
-    xb[0] = v.astype(BF16)
-
     def chip(h, off):
         return h * 4 + lax.rem(x + off, 4)
 
-    def rows_of(m, start, size):
-        return wf.at[pl.ds(pl.multiple_of(m * CHIP + start, 16), size), :]
-
     def piece(m, p):
-        return rows_of(m, 64 * c, AHEAD) if p == 0 else rows_of(m, 64 * c + AHEAD, UNIT - AHEAD)
+        return (wa if p == 0 else wb).at[c, m]
 
     def w_copy(src, dst, ident, who, send=None):
         return copy(src, dst, w_s.at[ident if send is None else send], w_r.at[ident], who)
@@ -209,20 +200,22 @@
         d.start()
         w_sent.append(d)
 
-    mine = chip(yh, 0)
-    theirs = chip(1 - yh, 0)
-    w_swap.wait_recv()
-    own_rows = wsh[...].astype(F32)
-    sib_rows = wtmp[...].astype(F32)
-    first = c == 0
-    wf[pl.ds(pl.multiple_of(mine * CHIP, 16), CHIP), :] = jnp.concatenate(
-        [jnp.where(first, own_rows, sib_rows), jnp.where(first, sib_rows, own_rows)], axis=0
-    ).astype(BF16)
+    def to_sibling(n, m, p):
+        w_go(piece(m, p), 17 + 2 * n + p, sib)
+
+    def assemble(n, m):
+        for p in range(2):
+            src = (wa if p == 0 else wb).at[1 - c, m]
+            w_copy(src, src, 17 + 2 * n + p, sib).wait_recv()
+        rows = pl.ds(pl.multiple_of(m * CHIP, 16), CHIP)
+        for ref, cols in ((wa, slice(0, FIRST)), (wb, slice(FIRST, WIDTH))):
+            wf[rows, cols] = jnp.concatenate(
+                [ref[0, m].astype(F32), ref[1, m].astype(F32)], axis=0
+            ).astype(BF16)
 
     edge_up = [w_copy(piece(mine, p), piece(mine, p), 13 + p, up) for p in range(2)]
     edge_dn = [w_copy(piece(mine, p), piece(mine, p), 13 + p, dn) for p in range(2)]
-    pass_up = [w_copy(piece(theirs, p), piece(theirs, p), 13 + p, up, 15 + p) for p in range(2)]
-    pass_dn = [w_copy(piece(theirs, p), piece(theirs, p), 13 + p, dn, 15 + p) for p in range(2)]
+    edge_far = [w_copy(piece(mine, p), piece(mine, p), 13 + p, across, 15 + p) for p in range(2)]
 
     @pl.when(j == 3)
     def _():
@@ -232,6 +225,11 @@
     @pl.when(j == 0)
     def _():
         for d in edge_dn:
+            d.start()
+
+    @pl.when(outer)
+    def _():
+        for d in edge_far:
             d.start()
 
     def along_x(r, m):
@@ -247,7 +245,22 @@
         mine_x[key].start()
     w_sent.extend(mine_x.values())
     w_sent.extend(theirs_x.values())
+    to_sibling(0, mine, 0)
+    to_sibling(0, mine, 1)
     pool_swap.start()
+
+    @pl.when(j == 1)
+    def _():
+        send_p(0, pool, 0)
+
+    @pl.when(j >= 1)
+    def _():
+        for d in p_hop:
+            d.start()
+
+    v, xr = normalize(img[...].astype(F32))
+    ximg[...] = v
+    xb[0] = v.astype(BF16)
 
     def slab_rows(n):
         m = chip(1 - yh if n < 4 else yh, ORDER[n % 4])
@@ -260,60 +273,41 @@
                 [slab_rows(n), slab_rows(n + 1)], axis=0
             ).astype(BF16)
 
-    def to_sibling(m, ident):
-        w_go(rows_of(m, 80 * c, PART), ident, sib)
-
     def near_first(r, h):
         for d, (off, onward) in enumerate(((3, xp), (1, xm))):
             got = piece(chip(h, off), d)
             w_copy(got, got, 1 + 4 * r + 3 * d, xp).wait_recv()
             w_go(got, 9 + 2 * r + d, onward)
+            to_sibling(1 + 4 * r + d, chip(h, off), d)
 
     def near_rest(r, h):
         for d, off in enumerate((3, 1)):
             m = chip(h, off)
             got = piece(m, 1 - d)
             w_copy(got, got, 2 + 4 * r + d, xp).wait_recv()
-            to_sibling(m, 17 + 4 * r + d)
+            to_sibling(1 + 4 * r + d, m, 1 - d)
 
     def far_units(r, h):
         m = chip(h, 2)
         for p in range(2):
             w_copy(piece(m, p), piece(m, p), 9 + 2 * r + p, xp).wait_recv()
-        to_sibling(m, 19 + 4 * r)
+            to_sibling(3 + 4 * r, m, p)
 
     edge_in = [w_copy(piece(theirs, p), piece(theirs, p), 13 + p, xp) for p in range(2)]
-    theirs_part = rows_of(theirs, 80 * c, PART)
-    theirs_sib = w_copy(theirs_part, theirs_part, 20, sib)
-    w_sent.append(theirs_sib)
 
     def theirs_first():
         edge_in[0].wait_recv()
-
-        @pl.when(j == 0)
-        def _():
-            pass_up[0].start()
-
-        @pl.when(j == 3)
-        def _():
-            pass_dn[0].start()
-
         theirs_x[0, 0].start()
+        theirs_sib[0].start()
 
     def theirs_rest():
         edge_in[1].wait_recv()
-
-        @pl.when(j == 0)
-        def _():
-            pass_up[1].start()
-
-        @pl.when(j == 3)
-        def _():
-            pass_dn[1].start()
-
         for key in ((1, 1), (0, 1), (1, 0)):
             theirs_x[key].start()
-        theirs_sib.start()
+        theirs_sib[1].start()
+
+    theirs_sib = [w_copy(piece(theirs, p), piece(theirs, p), 25 + p, sib) for p in range(2)]
+    w_sent.extend(theirs_sib)
 
     def hop_on(h):
         @pl.when(j <= 2)
@@ -360,6 +354,7 @@
         theirs_first()
 
     far_units(0, yh)
+    assemble(0, mine)
 
     @pl.when(inner)
     def _():
@@ -376,6 +371,8 @@
         pass_x(2, 1)
 
     near_first(1, 1 - yh)
+    for n, off in ((1, 3), (2, 1), (3, 2)):
+        assemble(n, chip(yh, off))
 
     @pl.when(j == 2)
     def _():
@@ -405,12 +402,9 @@
         for k in range(1, 4):
             ready(k)
 
-    for ident, m in (
-        (17, chip(yh, 3)), (18, chip(yh, 1)), (19, chip(yh, 2)), (20, theirs),
-        (21, chip(1 - yh, 3)), (22, chip(1 - yh, 1)), (23, chip(1 - yh, 2)),
-    ):
-        got = rows_of(m, 80 - 80 * c, PART)
-        w_copy(got, got, ident, sib).wait_recv()
+    assemble(4, theirs)
+    for n, off in ((5, 3), (6, 1), (7, 2)):
+        assemble(n, chip(1 - yh, off))
 
     temper = jnp.exp(jnp.full((1, 1), log_scale[0], F32))
     offset = jnp.full((1, 1), bias[0], F32)
@@ -654,18 +648,22 @@
     for q, (start, size, _) in enumerate(PIECES):
         head_out[:, start:start + size] += g_wait(slot(y_in, q), 28 + q)
 
-    w_swap.wait_send()
     for d in w_sent:
         d.wait_send()
 
     @pl.when(j == 3)
     def _():
-        for d in edge_up + pass_dn:
+        for d in edge_up:
             d.wait_send()
 
     @pl.when(j == 0)
     def _():
-        for d in edge_dn + pass_up:
+        for d in edge_dn:
+            d.wait_send()
+
+    @pl.when(outer)
+    def _():
+        for d in edge_far:
             d.wait_send()
 
     @pl.when(j <= 2)
@@ -729,9 +727,9 @@
         scratch_shapes=[
             pltpu.VMEM(block, BF16),
             pltpu.VMEM(block, BF16),
-            pltpu.VMEM(slab, BF16),
             pltpu.VMEM((1, WIDTH), F32),
-            pltpu.VMEM(slab, BF16),
+            pltpu.VMEM((2, 8, SHARD, FIRST), BF16),
+            pltpu.VMEM((2, 8, SHARD, WIDTH - FIRST), BF16),
             pltpu.VMEM((WIDTH, WIDTH), BF16),
             pltpu.VMEM((6,) + block, BF16),
             pltpu.VMEM((4,) + block, BF16),
@@ -756,8 +754,8 @@
             pltpu.VMEM((1, ROWS), F32),
             pltpu.VMEM(block, BF16),
             pltpu.VMEM((1, ROWS), F32),
-            dma((4,)),
-            dma((24,)), dma((24,)),
+            dma((5,)),
+            dma((33,)), dma((33,)),
             dma((7, 4)), dma((6, 4)),
             dma((6, 2)), dma((5, 2)),
             dma((32,)), dma((32,)),

time: 68.1 us -> 67.3 us (0.988)
  Pallas kernels: 66 us -> 65.2 us
    pallas_call x1, Pallas kernels: 65.1 us -> 64.2 us  [per_device(): pl.pallas_call(kernel, out_shape=results, in_specs=[hbm, hbm, hbm, hbm, s...]
where the time goes in v10:
time: 67.3 us; the launch traced here: 67.1 us
  Pallas kernels  65.2 us (97%)
  between operations  1.93 us (3%)
    pallas_call x1, Pallas kernels, per_device(): pl.pallas_call(kernel, out_shape=results, in_specs=[hbm, hbm, hbm, hbm, s...  64.2 us

profile of v10, /device:TPU:8, one launch (start us, length us, event | category | flops | bytes accessed | tf_op | source)
XLA Modules:
  0.0 67.1 jit_solution(15432246131210256479)
XLA Ops:
  1.9 64.2 %shard_map.93 = (f32[1,128]{1,0:T(1,128)S(1)}, bf16[128,1152]{1,0:T(8,128)(2,1)S(1)}, bf16[128,1152]{1,0:T(8,128)(2,1)S(1)}, f32[72,1152]{1,0:T(8,128)S(1)}) custom-call(bf16[128,1152]{1,0:T(8,128)(2,1)} %img_hbm.1, bf16[128,1152]{1,0:T(8,128)(2,1)} %pool_hbm.1, bf16[72,1152]{1,0:T(8,128)(2,1)} %wsh_hbm.1, f32[1152]{0:T(1024)} %hb_hbm.1, ...), custom_call_target="tpu_custom_call" | custom-call | flops 4000000000 | bytes 6000000 | tf_op jit(solution)/shard_map/pallas_call | solution.py:722
  66.2 1.0 %shard_map.94 = (f32[1,128]{1,0:T(1,128)}, bf16[128,1152]{1,0:T(8,128)(2,1)}, bf16[128,1152]{1,0:T(8,128)(2,1)}, f32[72,1152]{1,0:T(8,128)}) custom-call(f32[1,128]{1,0:T(1,128)S(1)} %get-tuple-element.12.refs_0_, bf16[128,1152]{1,0:T(8,128)(2,1)S(1)} %get-tuple-element.13.refs_1_, bf16[128,1152]{1,0:T(8,128)(2,1)S(1)} %get-tuple-element.14.refs_2_, ...), custom_call_target="tpu_custom_call" | custom-call | tf_op jit(solution)/shard_map/pallas_call | solution.py:769

commit v11 on v10

--- a/solution.py
+++ b/solution.py
@@ -18,8 +18,11 @@
 TILE = 384
 VMEM_GRANT = 44 * 1024 * 1024
 HALF = 64
-PIECES = ((0, 384, 1), (640, 256, -1), (384, 256, 1), (896, 256, -1))
-PLACE = {1: 0, 3: 1, 4: 2, 2: 3}
+PIECES = (
+    ((0, 384, 1), (640, 256, -1), (384, 256, 1), (896, 256, -1)),
+    ((0, 640, 1), (640, 512, -1)),
+)
+PLACE = {1: 0, 3: 1, 2: 2, 4: 3}
 ORDER = (2, 1, 3, 0)
 
 
@@ -117,12 +120,12 @@
 
     def send_p(k, src, h):
         if k < 4:
-          @pl.when(jnp.logical_and(k <= j, j <= 1))
+          @pl.when(jnp.logical_and(k <= j, j <= (2 if k == 0 else 1)))
           def _():
             copy(part(src, h), part(pbuf.at[PLACE[k + 1]], h), p_s.at[k, h], p_r.at[k + 1, h], up).start()
 
         if k > 2:
-          @pl.when(jnp.logical_and(k > j, j >= 2))
+          @pl.when(jnp.logical_and(k > j, j >= (1 if k == 4 else 2)))
           def _():
             copy(part(src, h), part(pbuf.at[PLACE[k - 1]], h), p_s.at[k, h], p_r.at[k - 1, h], dn).start()
 
@@ -156,7 +159,12 @@
                 copy(part(src, h), part(xbuf.at[1], h), x_s.at[k, h], x_r.at[1, h], up).wait_send()
 
     def p_done(k, src):
-        @pl.when(jnp.logical_or(jnp.logical_and(k <= j, j <= 1), jnp.logical_and(k > j, j >= 2)))
+        @pl.when(
+            jnp.logical_or(
+                jnp.logical_and(k <= j, j <= (2 if k == 0 else 1)),
+                jnp.logical_and(k > j, j >= (1 if k == 4 else 2)),
+            )
+        )
         def _():
             for h in range(2):
                 copy(part(src, h), part(pbuf.at[0], h), p_s.at[k, h], p_r.at[1, h], up).wait_send()
@@ -387,10 +395,13 @@
     @pl.when(j == 1)
     def _():
         pass_p(1)
+        pass_p(4)
 
     @pl.when(j == 2)
     def _():
         pass_p(3)
+        send_p(0, pool, 0)
+        send_p(0, pool, 1)
 
     far_units(1, 1 - yh)
 
@@ -475,7 +486,7 @@
         terms[n + 1] = t[SHARD:]
 
     def cols(n, q):
-        start, size, _ = PIECES[q]
+        start, size, _ = PIECES[n // 4][q]
         return terms[n, :, start:start + size]
 
     g_sent = []
@@ -490,27 +501,24 @@
         copy(ref, ref, g_s.at[ident], g_r.at[ident], xp).wait_recv()
         return ref[...].astype(F32)
 
-    def slot(refs, q, *index):
-        return refs[q].at[index] if index else refs[q]
-
     def far_sends(g):
-        for q, (_, _, way) in enumerate(PIECES):
-            g_go(slot(g_out, q, g, 0), cols(4 * g, q), 12 * g + q, slot(g_far, q, g), xp if way > 0 else xm)
+        for q, (_, _, way) in enumerate(PIECES[g]):
+            g_go(g_out[g][q].at[0], cols(4 * g, q), 12 * g + q, g_far[g][q], xp if way > 0 else xm)
 
     def near_sends(g):
-        for q, (_, _, way) in enumerate(PIECES):
+        for q, (_, _, way) in enumerate(PIECES[g]):
             n, who = (2, xm) if way > 0 else (1, xp)
-            g_go(slot(g_out, q, g, 1), cols(4 * g + n, q), 12 * g + 4 + q, slot(g_near, q, g, 0), who)
+            g_go(g_out[g][q].at[1], cols(4 * g + n, q), 12 * g + 4 + q, g_near[g][q].at[0], who)
 
     def second_sends(g):
-        for q, (_, _, way) in enumerate(PIECES):
+        for q, (_, _, way) in enumerate(PIECES[g]):
             n, who = (1, xp) if way > 0 else (2, xm)
-            value = cols(4 * g + n, q) + g_wait(slot(g_far, q, g), 12 * g + q)
-            g_go(slot(g_out, q, g, 2), value, 12 * g + 8 + q, slot(g_near, q, g, 1), who)
+            value = cols(4 * g + n, q) + g_wait(g_far[g][q], 12 * g + q)
+            g_go(g_out[g][q].at[2], value, 12 * g + 8 + q, g_near[g][q].at[1], who)
 
     def total(g, q):
-        value = cols(4 * g + 3, q) + g_wait(slot(g_near, q, g, 0), 12 * g + 4 + q)
-        return value + g_wait(slot(g_near, q, g, 1), 12 * g + 8 + q)
+        value = cols(4 * g + 3, q) + g_wait(g_near[g][q].at[0], 12 * g + 4 + q)
+        return value + g_wait(g_near[g][q].at[1], 12 * g + 8 + q)
 
     def back():
         @pl.loop(0, WIDTH // TILE)
@@ -554,7 +562,6 @@
     def _():
         for h in range(2):
             wait_p(3, h)
-            wait_p(4, h)
 
     @pl.when(j == 2)
     def _():
@@ -563,7 +570,7 @@
 
     @pl.when(inner)
     def _():
-        project(pbuf[0:3].reshape(3 * ROWS, WIDTH), u.at[:3 * ROWS])
+        project(pbuf[0:2].reshape(2 * ROWS, WIDTH), u.at[:2 * ROWS])
 
     @pl.when(outer)
     def _():
@@ -588,31 +595,31 @@
 
     @pl.when(inner)
     def _():
-        texts_done(1, 4)
-        d, row = meet(xb[9 - 4 * j], zb[pl.ds(4 - 2 * j, 2)].reshape(2 * ROWS, WIDTH), False)
+        texts_done(1, 3)
+        d, row = meet(xb[9 - 4 * j], zb[3 - j], False)
         gdx[...] = d
         gsum_out[...] = row
 
-    for q, (_, _, way) in enumerate(PIECES):
-        g_go(slot(y_out, q), total(0, q), 24 + q, slot(y_pass, q), y_up if way > 0 else y_dn)
+    for q, (_, _, way) in enumerate(PIECES[0]):
+        g_go(y_out[q], total(0, q), 24 + q, y_pass[q], y_up if way > 0 else y_dn)
 
     onward = [
-        copy(slot(y_pass, q), slot(y_in, q), g_s.at[28 + q], g_r.at[28 + q], y_up if way > 0 else y_dn)
-        for q, (_, _, way) in enumerate(PIECES)
+        copy(y_pass[q], y_in[q], g_s.at[28 + q], g_r.at[28 + q], y_up if way > 0 else y_dn)
+        for q, (_, _, way) in enumerate(PIECES[0])
     ]
 
     def relay():
         for q in range(4):
-            copy(slot(y_pass, q), slot(y_pass, q), g_s.at[24 + q], g_r.at[24 + q], xp).wait_recv()
+            copy(y_pass[q], y_pass[q], g_s.at[24 + q], g_r.at[24 + q], xp).wait_recv()
             onward[q].start()
 
     @pl.when(inner)
     def _():
         for h in range(2):
             wait_p(2, h)
-        project(pbuf[3], u.at[3 * ROWS:])
-        texts_done(4, 5)
-        d, row = meet(xb[9 - 4 * j], zb[4], False)
+        project(pbuf[2], u.at[2 * ROWS:3 * ROWS])
+        texts_done(3, 4)
+        d, row = meet(xb[9 - 4 * j], zb[3], False)
         gdx_out[...] = (gdx[...] + d).astype(BF16)
         gsum_out[...] += row
 
@@ -628,25 +635,31 @@
 
     second_sends(1)
 
+    @pl.when(j == 0)
+    def _():
+        for h in range(2):
+            wait_p(3, h)
+
+    @pl.when(j == 3)
+    def _():
+        for h in range(2):
+            wait_p(1, h)
+
+    @pl.when(outer)
+    def _():
+        project(pbuf[1 - lax.div(j, 3)], u.at[2 * ROWS:3 * ROWS])
+        texts_done(3, 4)
+        d, row = meet(xb[0], zb[3], False)
+        u[ROWS:2 * ROWS] += d
+        loss_out[...] += row
+
     @pl.when(inner)
     def _():
         d, row = meet(xb[0], zb[0:3].reshape(3 * ROWS, WIDTH), True)
-        e, more = meet(xb[0], zb[4], False)
+        e, more = meet(xb[0], zb[3], False)
         image_side(d + e, row + more)
 
     relay()
-
-    for q, (start, size, _) in enumerate(PIECES):
-        head_out[:, start:start + size] = total(1, q)
-
-    @pl.when(outer)
-    def _():
-        gsum_up.wait_recv()
-        gdx_up.wait_recv()
-        image_side(u[ROWS:2 * ROWS] + gdx_in[...].astype(F32), loss_out[...] + gsum_in[...])
-
-    for q, (start, size, _) in enumerate(PIECES):
-        head_out[:, start:start + size] += g_wait(slot(y_in, q), 28 + q)
 
     for d in w_sent:
         d.wait_send()
@@ -679,11 +692,6 @@
     @pl.when(j == 0)
     def _():
         guest.wait_send()
-
-    @pl.when(inner)
-    def _():
-        gdx_up.wait_send()
-        gsum_up.wait_send()
 
     x_done(0, img)
     p_done(0, pool)
@@ -693,7 +701,27 @@
     p_done(4, pbuf.at[0])
     pool_swap.wait_send()
     pair.wait_send()
-    for d in g_sent + onward:
+    for d in g_sent[:24]:
+        d.wait_send()
+
+    for q, (start, size, _) in enumerate(PIECES[1]):
+        head_out[:, start:start + size] = total(1, q)
+
+    @pl.when(outer)
+    def _():
+        gsum_up.wait_recv()
+        gdx_up.wait_recv()
+        image_side(u[ROWS:2 * ROWS] + gdx_in[...].astype(F32), loss_out[...] + gsum_in[...])
+
+    for q, (start, size, _) in enumerate(PIECES[0]):
+        head_out[:, start:start + size] += g_wait(y_in[q], 28 + q)
+
+    @pl.when(inner)
+    def _():
+        gdx_up.wait_send()
+        gsum_up.wait_send()
+
+    for d in g_sent[24:] + onward:
         d.wait_send()
 
 
@@ -711,7 +739,7 @@
     hbm = pl.BlockSpec(memory_space=pltpu.HBM)
     block = (ROWS, WIDTH)
     slab = (SHARD, WIDTH)
-    parts = [(SHARD, size) for _, size, _ in PIECES]
+    parts = [[(SHARD, size) for _, size, _ in pieces] for pieces in PIECES]
     dma = pltpu.SemaphoreType.DMA
     results = (
         jax.ShapeDtypeStruct((1, ROWS), F32),
@@ -734,21 +762,21 @@
             pltpu.VMEM((6,) + block, BF16),
             pltpu.VMEM((4,) + block, BF16),
             pltpu.VMEM((6,) + block, BF16),
-            pltpu.VMEM((5,) + block, BF16),
+            pltpu.VMEM((4,) + block, BF16),
             pltpu.VMEM(block, F32),
             pltpu.VMEM(block, F32),
-            pltpu.VMEM((4 * ROWS, WIDTH), F32),
+            pltpu.VMEM((3 * ROWS, WIDTH), F32),
             pltpu.VMEM((2 * ROWS, WIDTH), BF16),
             pltpu.VMEM(block, BF16),
             pltpu.VMEM((WIDTH, ROWS), F32),
             pltpu.VMEM((8 * SHARD, 2 * ROWS), BF16),
             pltpu.VMEM((8,) + slab, F32),
-            [pltpu.VMEM((2, 3) + p, BF16) for p in parts],
-            [pltpu.VMEM((2,) + p, BF16) for p in parts],
-            [pltpu.VMEM((2, 2) + p, BF16) for p in parts],
-            [pltpu.VMEM(p, BF16) for p in parts],
-            [pltpu.VMEM(p, BF16) for p in parts],
-            [pltpu.VMEM(p, BF16) for p in parts],
+            [[pltpu.VMEM((3,) + p, BF16) for p in ps] for ps in parts],
+            [[pltpu.VMEM(p, BF16) for p in ps] for ps in parts],
+            [[pltpu.VMEM((2,) + p, BF16) for p in ps] for ps in parts],
+            [pltpu.VMEM(p, BF16) for p in parts[0]],
+            [pltpu.VMEM(p, BF16) for p in parts[0]],
+            [pltpu.VMEM(p, BF16) for p in parts[0]],
             pltpu.VMEM(block, F32),
             pltpu.VMEM(block, BF16),
             pltpu.VMEM((1, ROWS), F32),

time: 67.3 us -> 67.8 us (level)
  no operation moved by 1% of the time
where the time goes in v11:
time: 67.8 us; the launch traced here: 67.6 us
  Pallas kernels  65.7 us (97%)
  between operations  1.93 us (3%)
    pallas_call x1, Pallas kernels, per_device(): pl.pallas_call(kernel, out_shape=results, in_specs=[hbm, hbm, hbm, hbm, s...  64.7 us

profile of v11, /device:TPU:8, one launch (start us, length us, event | category | flops | bytes accessed | tf_op | source)
XLA Modules:
  0.0 67.6 jit_solution(10685411420425320488)
XLA Ops:
  1.9 64.7 %shard_map.93 = (f32[1,128]{1,0:T(1,128)S(1)}, bf16[128,1152]{1,0:T(8,128)(2,1)S(1)}, bf16[128,1152]{1,0:T(8,128)(2,1)S(1)}, f32[72,1152]{1,0:T(8,128)S(1)}) custom-call(bf16[128,1152]{1,0:T(8,128)(2,1)} %img_hbm.1, bf16[128,1152]{1,0:T(8,128)(2,1)} %pool_hbm.1, bf16[72,1152]{1,0:T(8,128)(2,1)} %wsh_hbm.1, f32[1152]{0:T(1024)} %hb_hbm.1, ...), custom_call_target="tpu_custom_call" | custom-call | flops 4000000000 | bytes 6000000 | tf_op jit(solution)/shard_map/pallas_call | solution.py:750
  66.7 1.0 %shard_map.94 = (f32[1,128]{1,0:T(1,128)}, bf16[128,1152]{1,0:T(8,128)(2,1)}, bf16[128,1152]{1,0:T(8,128)(2,1)}, f32[72,1152]{1,0:T(8,128)}) custom-call(f32[1,128]{1,0:T(1,128)S(1)} %get-tuple-element.12.refs_0_, bf16[128,1152]{1,0:T(8,128)(2,1)S(1)} %get-tuple-element.13.refs_1_, bf16[128,1152]{1,0:T(8,128)(2,1)S(1)} %get-tuple-element.14.refs_2_, ...), custom_call_target="tpu_custom_call" | custom-call | tf_op jit(solution)/shard_map/pallas_call | solution.py:797

commit v12 on v10

--- a/solution.py
+++ b/solution.py
@@ -606,6 +606,16 @@
             copy(slot(y_pass, q), slot(y_pass, q), g_s.at[24 + q], g_r.at[24 + q], xp).wait_recv()
             onward[q].start()
 
+    second_sends(1)
+
+    @pl.when(inner)
+    def _():
+        d, row = meet(xb[0], zb[0:3].reshape(3 * ROWS, WIDTH), True)
+        u[:ROWS] = d
+        loss_out[...] = row
+
+    relay()
+
     @pl.when(inner)
     def _():
         for h in range(2):
@@ -626,27 +636,10 @@
             gdx_up.start()
             gsum_up.start()
 
-    second_sends(1)
-
-    @pl.when(inner)
-    def _():
-        d, row = meet(xb[0], zb[0:3].reshape(3 * ROWS, WIDTH), True)
-        e, more = meet(xb[0], zb[4], False)
-        image_side(d + e, row + more)
-
-    relay()
-
-    for q, (start, size, _) in enumerate(PIECES):
-        head_out[:, start:start + size] = total(1, q)
-
-    @pl.when(outer)
-    def _():
-        gsum_up.wait_recv()
-        gdx_up.wait_recv()
-        image_side(u[ROWS:2 * ROWS] + gdx_in[...].astype(F32), loss_out[...] + gsum_in[...])
-
-    for q, (start, size, _) in enumerate(PIECES):
-        head_out[:, start:start + size] += g_wait(slot(y_in, q), 28 + q)
+    @pl.when(inner)
+    def _():
+        d, row = meet(xb[0], zb[4], False)
+        image_side(u[:ROWS] + d, loss_out[...] + row)
 
     for d in w_sent:
         d.wait_send()
@@ -679,11 +672,6 @@
     @pl.when(j == 0)
     def _():
         guest.wait_send()
-
-    @pl.when(inner)
-    def _():
-        gdx_up.wait_send()
-        gsum_up.wait_send()
 
     x_done(0, img)
     p_done(0, pool)
@@ -693,7 +681,28 @@
     p_done(4, pbuf.at[0])
     pool_swap.wait_send()
     pair.wait_send()
-    for d in g_sent + onward:
+    for d in g_sent[:24]:
+        d.wait_send()
+
+
+    for q, (start, size, _) in enumerate(PIECES):
+        head_out[:, start:start + size] = total(1, q)
+
+    @pl.when(outer)
+    def _():
+        gsum_up.wait_recv()
+        gdx_up.wait_recv()
+        image_side(u[ROWS:2 * ROWS] + gdx_in[...].astype(F32), loss_out[...] + gsum_in[...])
+
+    for q, (start, size, _) in enumerate(PIECES):
+        head_out[:, start:start + size] += g_wait(slot(y_in, q), 28 + q)
+
+    @pl.when(inner)
+    def _():
+        gdx_up.wait_send()
+        gsum_up.wait_send()
+
+    for d in g_sent[24:] + onward:
         d.wait_send()
 
 

time: 67.3 us -> 66.5 us (0.988)
  the two profiles are of different devices: /device:TPU:8 before, /device:TPU:1 now
where the time goes in v12:
time: 66.5 us; the launch traced here: 66.4 us
  Pallas kernels  64.4 us (97%)
  between operations  1.93 us (3%)
    pallas_call x1, Pallas kernels, per_device(): pl.pallas_call(kernel, out_shape=results, in_specs=[hbm, hbm, hbm, hbm, s...  63.5 us

profile of v12, /device:TPU:1, one launch (start us, length us, event | category | flops | bytes accessed | tf_op | source)
XLA Modules:
  0.0 66.4 jit_solution(17671517148667515776)
XLA Ops:
  1.9 63.5 %shard_map.93 = (f32[1,128]{1,0:T(1,128)S(1)}, bf16[128,1152]{1,0:T(8,128)(2,1)S(1)}, bf16[128,1152]{1,0:T(8,128)(2,1)S(1)}, f32[72,1152]{1,0:T(8,128)S(1)}) custom-call(bf16[128,1152]{1,0:T(8,128)(2,1)} %img_hbm.1, bf16[128,1152]{1,0:T(8,128)(2,1)} %pool_hbm.1, bf16[72,1152]{1,0:T(8,128)(2,1)} %wsh_hbm.1, f32[1152]{0:T(1024)} %hb_hbm.1, ...), custom_call_target="tpu_custom_call" | custom-call | flops 4000000000 | bytes 6000000 | tf_op jit(solution)/shard_map/pallas_call | solution.py:731
  65.4 1.0 %shard_map.94 = (f32[1,128]{1,0:T(1,128)}, bf16[128,1152]{1,0:T(8,128)(2,1)}, bf16[128,1152]{1,0:T(8,128)(2,1)}, f32[72,1152]{1,0:T(8,128)}) custom-call(f32[1,128]{1,0:T(1,128)S(1)} %get-tuple-element.12.refs_0_, bf16[128,1152]{1,0:T(8,128)(2,1)S(1)} %get-tuple-element.13.refs_1_, bf16[128,1152]{1,0:T(8,128)(2,1)S(1)} %get-tuple-element.14.refs_2_, ...), custom_call_target="tpu_custom_call" | custom-call | tf_op jit(solution)/shard_map/pallas_call | solution.py:778

commit v13 on v12

--- a/solution.py
+++ b/solution.py
@@ -610,14 +610,6 @@
 
     @pl.when(inner)
     def _():
-        d, row = meet(xb[0], zb[0:3].reshape(3 * ROWS, WIDTH), True)
-        u[:ROWS] = d
-        loss_out[...] = row
-
-    relay()
-
-    @pl.when(inner)
-    def _():
         for h in range(2):
             wait_p(2, h)
         project(pbuf[3], u.at[3 * ROWS:])
@@ -626,20 +618,23 @@
         gdx_out[...] = (gdx[...] + d).astype(BF16)
         gsum_out[...] += row
 
-        @pl.when(j == 1)
-        def _():
-            gdx_dn.start()
-            gsum_dn.start()
-
-        @pl.when(j == 2)
-        def _():
-            gdx_up.start()
-            gsum_up.start()
-
-    @pl.when(inner)
-    def _():
-        d, row = meet(xb[0], zb[4], False)
-        image_side(u[:ROWS] + d, loss_out[...] + row)
+    relay()
+
+    @pl.when(j == 1)
+    def _():
+        gdx_dn.start()
+        gsum_dn.start()
+
+    @pl.when(j == 2)
+    def _():
+        gdx_up.start()
+        gsum_up.start()
+
+    @pl.when(inner)
+    def _():
+        d, row = meet(xb[0], zb[0:3].reshape(3 * ROWS, WIDTH), True)
+        e, more = meet(xb[0], zb[4], False)
+        image_side(d + e, row + more)
 
     for d in w_sent:
         d.wait_send()

time: 66.5 us -> 66.6 us (level)
  no operation moved by 1% of the time
where the time goes in v13:
time: 66.6 us; the launch traced here: 66.4 us
  Pallas kernels  64.5 us (97%)
  between operations  1.93 us (3%)
    pallas_call x1, Pallas kernels, per_device(): pl.pallas_call(kernel, out_shape=results, in_specs=[hbm, hbm, hbm, hbm, s...  63.6 us

profile of v13, /device:TPU:1, one launch (start us, length us, event | category | flops | bytes accessed | tf_op | source)
XLA Modules:
  0.0 66.4 jit_solution(11751882484421866559)
XLA Ops:
  1.9 63.6 %shard_map.93 = (f32[1,128]{1,0:T(1,128)S(1)}, bf16[128,1152]{1,0:T(8,128)(2,1)S(1)}, bf16[128,1152]{1,0:T(8,128)(2,1)S(1)}, f32[72,1152]{1,0:T(8,128)S(1)}) custom-call(bf16[128,1152]{1,0:T(8,128)(2,1)} %img_hbm.1, bf16[128,1152]{1,0:T(8,128)(2,1)} %pool_hbm.1, bf16[72,1152]{1,0:T(8,128)(2,1)} %wsh_hbm.1, f32[1152]{0:T(1024)} %hb_hbm.1, ...), custom_call_target="tpu_custom_call" | custom-call | flops 4000000000 | bytes 6000000 | tf_op jit(solution)/shard_map/pallas_call | solution.py:726
  65.5 1.0 %shard_map.94 = (f32[1,128]{1,0:T(1,128)}, bf16[128,1152]{1,0:T(8,128)(2,1)}, bf16[128,1152]{1,0:T(8,128)(2,1)}, f32[72,1152]{1,0:T(8,128)}) custom-call(f32[1,128]{1,0:T(1,128)S(1)} %get-tuple-element.12.refs_0_, bf16[128,1152]{1,0:T(8,128)(2,1)S(1)} %get-tuple-element.13.refs_1_, bf16[128,1152]{1,0:T(8,128)(2,1)S(1)} %get-tuple-element.14.refs_2_, ...), custom_call_target="tpu_custom_call" | custom-call | tf_op jit(solution)/shard_map/pallas_call | solution.py:773

commit v14 on v13

--- a/solution.py
+++ b/solution.py
@@ -520,8 +520,8 @@
                 dzb[:ROWS], wf[cols, :], NT, preferred_element_type=F32
             ).astype(BF16)
 
-    gdx_up = copy(gdx_out, gdx_in, h_s.at[0], h_r.at[0], up)
-    gdx_dn = copy(gdx_out, gdx_in, h_s.at[0], h_r.at[0], dn)
+    gdx_up = [copy(part(gdx_out, h), part(gdx_in, h), h_s.at[4 * h], h_r.at[4 * h], up) for h in range(2)]
+    gdx_dn = [copy(part(gdx_out, h), part(gdx_in, h), h_s.at[4 * h], h_r.at[4 * h], dn) for h in range(2)]
     gsum_up = copy(gsum_out, gsum_in, h_s.at[1], h_r.at[1], up)
     gsum_dn = copy(gsum_out, gsum_in, h_s.at[1], h_r.at[1], dn)
 
@@ -618,17 +618,25 @@
         gdx_out[...] = (gdx[...] + d).astype(BF16)
         gsum_out[...] += row
 
+    @pl.when(j == 1)
+    def _():
+        gsum_dn.start()
+        gdx_dn[0].start()
+
+    @pl.when(j == 2)
+    def _():
+        gsum_up.start()
+        gdx_up[0].start()
+
     relay()
 
     @pl.when(j == 1)
     def _():
-        gdx_dn.start()
-        gsum_dn.start()
+        gdx_dn[1].start()
 
     @pl.when(j == 2)
     def _():
-        gdx_up.start()
-        gsum_up.start()
+        gdx_up[1].start()
 
     @pl.when(inner)
     def _():
@@ -686,7 +694,8 @@
     @pl.when(outer)
     def _():
         gsum_up.wait_recv()
-        gdx_up.wait_recv()
+        gdx_up[0].wait_recv()
+        gdx_up[1].wait_recv()
         image_side(u[ROWS:2 * ROWS] + gdx_in[...].astype(F32), loss_out[...] + gsum_in[...])
 
     for q, (start, size, _) in enumerate(PIECES):
@@ -694,7 +703,8 @@
 
     @pl.when(inner)
     def _():
-        gdx_up.wait_send()
+        gdx_up[0].wait_send()
+        gdx_up[1].wait_send()
         gsum_up.wait_send()
 
     for d in g_sent[24:] + onward:
@@ -763,7 +773,7 @@
             dma((7, 4)), dma((6, 4)),
             dma((6, 2)), dma((5, 2)),
             dma((32,)), dma((32,)),
-            dma((4,)), dma((4,)),
+            dma((5,)), dma((5,)),
         ],
         compiler_params=pltpu.CompilerParams(
             collective_id=0, has_side_effects=True, vmem_limit_bytes=VMEM_GRANT

time: 66.6 us -> 65.6 us (0.985)
  the two profiles are of different devices: /device:TPU:1 before, /device:TPU:16 now
where the time goes in v14:
time: 65.6 us; the launch traced here: 65.5 us
  Pallas kernels  63.6 us (97%)
  between operations  1.93 us (3%)
    pallas_call x1, Pallas kernels, per_device(): pl.pallas_call(kernel, out_shape=results, in_specs=[hbm, hbm, hbm, hbm, s...  62.6 us

profile of v14, /device:TPU:16, one launch (start us, length us, event | category | flops | bytes accessed | tf_op | source)
XLA Modules:
  0.0 65.5 jit_solution(1301643134847892604)
XLA Ops:
  1.9 62.6 %shard_map.93 = (f32[1,128]{1,0:T(1,128)S(1)}, bf16[128,1152]{1,0:T(8,128)(2,1)S(1)}, bf16[128,1152]{1,0:T(8,128)(2,1)S(1)}, f32[72,1152]{1,0:T(8,128)S(1)}) custom-call(bf16[128,1152]{1,0:T(8,128)(2,1)} %img_hbm.1, bf16[128,1152]{1,0:T(8,128)(2,1)} %pool_hbm.1, bf16[72,1152]{1,0:T(8,128)(2,1)} %wsh_hbm.1, f32[1152]{0:T(1024)} %hb_hbm.1, ...), custom_call_target="tpu_custom_call" | custom-call | flops 4000000000 | bytes 6000000 | tf_op jit(solution)/shard_map/pallas_call | solution.py:736
  64.5 1.0 %shard_map.94 = (f32[1,128]{1,0:T(1,128)}, bf16[128,1152]{1,0:T(8,128)(2,1)}, bf16[128,1152]{1,0:T(8,128)(2,1)}, f32[72,1152]{1,0:T(8,128)}) custom-call(f32[1,128]{1,0:T(1,128)S(1)} %get-tuple-element.12.refs_0_, bf16[128,1152]{1,0:T(8,128)(2,1)S(1)} %get-tuple-element.13.refs_1_, bf16[128,1152]{1,0:T(8,128)(2,1)S(1)} %get-tuple-element.14.refs_2_, ...), custom_call_target="tpu_custom_call" | custom-call | tf_op jit(solution)/shard_map/pallas_call | solution.py:783

commit v15 on v14

--- a/solution.py
+++ b/solution.py
@@ -309,34 +309,36 @@
     theirs_sib = [w_copy(piece(theirs, p), piece(theirs, p), 25 + p, sib) for p in range(2)]
     w_sent.extend(theirs_sib)
 
-    def hop_on(h):
+    def hop_on(h, quarters):
         @pl.when(j <= 2)
         def _():
-            for q in (2 * h, 2 * h + 1):
+            for q in quarters:
                 hop_in[q].wait_recv()
                 hop_up[q].start()
+
+        if h is None:
+            return
 
         @pl.when(inner)
         def _():
             pass_x(1, h)
 
-    hop_on(0)
+    hop_on(0, (0, 1))
     transpose_into(pool, 0)
 
     @pl.when(outer)
     def _():
         theirs_first()
 
+    hop_on(None, (2,))
     near_first(0, yh)
 
     @pl.when(outer)
     def _():
         theirs_rest()
 
-    hop_on(1)
+    hop_on(1, (3,))
     near_rest(0, yh)
-    pool_swap.wait_recv()
-    transpose_into(psib, ROWS)
 
     @pl.when(j == 0)
     def _():
@@ -392,6 +394,8 @@
     def _():
         pass_p(3)
 
+    pool_swap.wait_recv()
+    transpose_into(psib, ROWS)
     far_units(1, 1 - yh)
 
     def ready(k):

time: 65.6 us -> 66 us (level)
  the two profiles are of different devices: /device:TPU:16 before, /device:TPU:8 now
where the time goes in v15:
time: 66 us; the launch traced here: 65.8 us
  Pallas kernels  63.9 us (97%)
  between operations  1.93 us (3%)
    pallas_call x1, Pallas kernels, per_device(): pl.pallas_call(kernel, out_shape=results, in_specs=[hbm, hbm, hbm, hbm, s...  62.9 us

profile of v15, /device:TPU:8, one launch (start us, length us, event | category | flops | bytes accessed | tf_op | source)
XLA Modules:
  0.0 65.8 jit_solution(3793689237738634386)
XLA Ops:
  1.9 62.9 %shard_map.93 = (f32[1,128]{1,0:T(1,128)S(1)}, bf16[128,1152]{1,0:T(8,128)(2,1)S(1)}, bf16[128,1152]{1,0:T(8,128)(2,1)S(1)}, f32[72,1152]{1,0:T(8,128)S(1)}) custom-call(bf16[128,1152]{1,0:T(8,128)(2,1)} %img_hbm.1, bf16[128,1152]{1,0:T(8,128)(2,1)} %pool_hbm.1, bf16[72,1152]{1,0:T(8,128)(2,1)} %wsh_hbm.1, f32[1152]{0:T(1024)} %hb_hbm.1, ...), custom_call_target="tpu_custom_call" | custom-call | flops 4000000000 | bytes 6000000 | tf_op jit(solution)/shard_map/pallas_call | solution.py:740
  64.9 1.0 %shard_map.94 = (f32[1,128]{1,0:T(1,128)}, bf16[128,1152]{1,0:T(8,128)(2,1)}, bf16[128,1152]{1,0:T(8,128)(2,1)}, f32[72,1152]{1,0:T(8,128)}) custom-call(f32[1,128]{1,0:T(1,128)S(1)} %get-tuple-element.12.refs_0_, bf16[128,1152]{1,0:T(8,128)(2,1)S(1)} %get-tuple-element.13.refs_1_, bf16[128,1152]{1,0:T(8,128)(2,1)S(1)} %get-tuple-element.14.refs_2_, ...), custom_call_target="tpu_custom_call" | custom-call | tf_op jit(solution)/shard_map/pallas_call | solution.py:787

commit v16 on v14

--- a/solution.py
+++ b/solution.py
@@ -606,8 +606,6 @@
             copy(slot(y_pass, q), slot(y_pass, q), g_s.at[24 + q], g_r.at[24 + q], xp).wait_recv()
             onward[q].start()
 
-    second_sends(1)
-
     @pl.when(inner)
     def _():
         for h in range(2):
@@ -628,6 +626,7 @@
         gsum_up.start()
         gdx_up[0].start()
 
+    second_sends(1)
     relay()
 
     @pl.when(j == 1)

time: 65.6 us -> 65.9 us (level)
  the two profiles are of different devices: /device:TPU:16 before, /device:TPU:1 now
where the time goes in v16:
time: 65.9 us; the launch traced here: 65.7 us
  Pallas kernels  63.8 us (97%)
  between operations  1.93 us (3%)
    pallas_call x1, Pallas kernels, per_device(): pl.pallas_call(kernel, out_shape=results, in_specs=[hbm, hbm, hbm, hbm, s...  62.8 us

profile of v16, /device:TPU:1, one launch (start us, length us, event | category | flops | bytes accessed | tf_op | source)
XLA Modules:
  0.0 65.7 jit_solution(4344642522484886045)
XLA Ops:
  1.9 62.8 %shard_map.93 = (f32[1,128]{1,0:T(1,128)S(1)}, bf16[128,1152]{1,0:T(8,128)(2,1)S(1)}, bf16[128,1152]{1,0:T(8,128)(2,1)S(1)}, f32[72,1152]{1,0:T(8,128)S(1)}) custom-call(bf16[128,1152]{1,0:T(8,128)(2,1)} %img_hbm.1, bf16[128,1152]{1,0:T(8,128)(2,1)} %pool_hbm.1, bf16[72,1152]{1,0:T(8,128)(2,1)} %wsh_hbm.1, f32[1152]{0:T(1024)} %hb_hbm.1, ...), custom_call_target="tpu_custom_call" | custom-call | flops 4000000000 | bytes 6000000 | tf_op jit(solution)/shard_map/pallas_call | solution.py:735
  64.8 1.0 %shard_map.94 = (f32[1,128]{1,0:T(1,128)}, bf16[128,1152]{1,0:T(8,128)(2,1)}, bf16[128,1152]{1,0:T(8,128)(2,1)}, f32[72,1152]{1,0:T(8,128)}) custom-call(f32[1,128]{1,0:T(1,128)S(1)} %get-tuple-element.12.refs_0_, bf16[128,1152]{1,0:T(8,128)(2,1)S(1)} %get-tuple-element.13.refs_1_, bf16[128,1152]{1,0:T(8,128)(2,1)S(1)} %get-tuple-element.14.refs_2_, ...), custom_call_target="tpu_custom_call" | custom-call | tf_op jit(solution)/shard_map/pallas_call | solution.py:782
